TPU v7x, 128 devices: a whole 4x4x4 slice. The times are simulated.
128 devices in a mesh: region: 32 (over y, z, core), tracer: 4 (over x).
Axes of the slice: x: 4, y: 4, z: 4, core: 2. Of those that a mesh axis runs over, the one named last changes fastest.
Arguments:
- tracers: float32 [256, 131072], P('tracer', 'region'), may hold values from -6 to 6
- transport: bfloat16 [1024, 16, 128, 128], P('region'), may hold values from -0.09375 to 0.09375
- col_slot: int32 [1024, 16], P('region'), may hold values from 0 to 47, as said below
- export_rows: int32 [32, 8], P('region'), may hold values from 0 to 31
- send_pos: int32 [32, 4, 4], replicated, may hold values from 0 to 7
- live_blocks: int32 [32], replicated, may hold values from 1 to 32, 768 in all
- inverse: bfloat16 [1024, 128, 128], P('region'), may hold values from -0.4 to 1
- vmax: float32 [256], P('tracer'), may hold values from 1 to 4
- half_sat: float32 [256], P('tracer'), may hold values from 0.1 to 3
Outputs:
- final_tracers: float32 [256, 131072], P('tracer', 'region')
Inputs may be any that keep to these rules, and one draw needn't show every extreme that they name: col_slot[g, 0] is the block row's own local block; other values are local blocks (below 32) or read slots.
All inputs are finite; a program needn't handle non-finite values.
Results may differ from a plain program's by a relative error of at most 0.01.
Values may be sent and summed in bfloat16 or wider, within the bound.
No kernel may reach another device: no remote copies, remote signals or barrier semaphores. Data moves between devices by JAX's collectives and lax.ppermute only.
A program may use at most 128 MiB of HBM per device.

v0:
```python
import functools

import jax
import jax.numpy as jnp
from jax import lax
from jax.experimental import pallas as pl
from jax.experimental.pallas import tpu as pltpu
from jax.sharding import PartitionSpec as P

NTR = 256
LEVPAD = 64
LEVELS = 50
CYCLES = 2
OFFSETS = (-2, -1, 1, 2)

EXPORTS, SENDS, LINKS, REST, LIVE, SPARE, TABLE = 0, 16, 48, 64, 100, 120, 136

VMEM = pltpu.VMEM
SMEM = pltpu.SMEM
F32 = jnp.float32
BF16 = jnp.bfloat16


def from_behind(value, axis, distance):
    n = lax.axis_size(axis)
    route = [((i - distance) % n, i) for i in range(n)]
    return lax.ppermute(value, axis, route)


def link_neighbour(link, region):
    chip, core = region // 2 % 2, region % 2
    return (3 * chip, 1 + core, 3 - 3 * chip, 2 - core)[link]


def offset_of(which):
    return which - 2 + which // 2


def exchange(parts):
    n = lax.axis_size("region")
    arrived = []
    for link, part in enumerate(parts):
        route = [(r, (r + offset_of(link_neighbour(link, r))) % n) for r in range(n)]
        arrived.append(lax.ppermute(part, "region", route))
    return arrived


def in_vmem(value):
    return pltpu.with_memory_space_constraint(value, VMEM)


def spec(space):
    return pl.BlockSpec(memory_space=space)


def in_hbm(value):
    return pltpu.with_memory_space_constraint(value, pltpu.HBM)


def call(kernel, name, args, outs, scratch=(), flops=0, moved=1 << 20):
    return pl.pallas_call(
        kernel,
        in_specs=[spec(s) for _, s in args],
        out_specs=[spec(s) for _, s in outs],
        out_shape=[o for o, _ in outs],
        scratch_shapes=list(scratch),
        compiler_params=pltpu.CompilerParams(vmem_limit_bytes=24 << 20),
        cost_estimate=pl.CostEstimate(flops=flops, bytes_accessed=moved, transcendentals=0),
        name=name,
    )(*[v for v, _ in args])


def kept(shape, dtype):
    return (VMEM(shape, dtype), VMEM)


def sent(shape, dtype):
    return (jax.ShapeDtypeStruct(shape, dtype), VMEM)


def whole(values, space=VMEM):
    return [(v, space) for v in values]


def row_mask(block, live, shape):
    level = lax.rem(lax.broadcasted_iota(jnp.int32, shape, 1), LEVPAD)
    limit = jnp.where(block < live, LEVELS, 0)
    return jnp.where(level < limit, 1.0, 0.0).astype(F32)


def fetch(pairs, sems):
    copies = [pltpu.make_async_copy(a, b, sems.at[i]) for i, (a, b) in enumerate(pairs)]
    for copy in copies:
        copy.start()
    return copies


def read_position(positions, link, k):
    regions = positions.shape[2]
    mine = lax.axis_index("region")
    which = link_neighbour(link, mine)
    partner = lax.rem(mine + offset_of(which) + regions, regions)
    return positions[3 - which, k, partner]


def first_kernel(block, export_rows, send_pos, tracers, *refs):
    near, reach = send_pos.shape[:2]
    sends, (exports, positions, landed, sems, block_sems) = refs[:near], refs[near:]
    small = fetch([(export_rows, exports), (send_pos, positions)], sems)
    small[0].wait()
    copies = []
    for e in range(exports.shape[1]):
        start = pl.multiple_of(exports[0, e] * block, block)
        copies.append((tracers.at[:, pl.ds(start, block)], landed.at[e]))
    copies = fetch(copies, block_sems)
    for copy in small[1:] + copies:
        copy.wait()
    for link in range(near):
        for k in range(reach):
            sends[link][k] = landed[read_position(positions, link, k)].astype(BF16)


def write_table(table, exports, positions, lives, blocks):
    offered = exports.shape[1]
    near, reach = positions.shape[:2]
    exported = [exports[0, e] for e in range(offered)]
    free = jnp.int32(0)
    places = SPARE - offered
    for e, row in enumerate(exported):
        table[EXPORTS + e] = row
        seen = jnp.bool_(False)
        place = jnp.int32(e)
        for f in reversed(range(e)):
            same = exported[f] == row
            seen = jnp.logical_or(seen, same)
            place = jnp.where(same, f, place)
        table[SPARE + e] = place
        table[places + free] = jnp.int32(e)
        free = free + jnp.where(seen, 1, 0)
    for link in range(near):
        table[LINKS + link] = link_neighbour(link, lax.axis_index("region"))
        for k in range(reach):
            table[SENDS + link * reach + k] = table[SPARE + read_position(positions, link, k)]
    table[LIVE] = lives[lax.axis_index("region")]
    n = jnp.int32(0)
    for b in range(blocks):
        hit = exported[0] == b
        for row in exported[1:]:
            hit = jnp.logical_or(hit, row == b)
        fills = EXPORTS + table[places + jnp.minimum(n, offered - 1)]
        place = jnp.where(n < free, fills, REST + n - free)
        table[jnp.where(hit, TABLE - 1, place)] = jnp.int32(b)
        n = n + jnp.where(hit, 0, 1)


def prepare_kernel(
    export_rows,
    send_pos,
    live,
    col_slot,
    tracers,
    transport,
    state,
    low,
    early,
    table,
    cols,
    exports,
    positions,
    lives,
    landed,
    landed_rows,
    sems,
    block_sems,
):
    blocks, slots, block, _ = transport.shape
    offered = exports.shape[1]
    small = fetch(
        [
            (export_rows, exports),
            (send_pos, positions),
            (live, lives),
            (col_slot, cols),
            (tracers, landed),
        ],
        sems,
    )
    small[0].wait()
    exported = [exports[0, e] for e in range(offered)]
    again = []
    for e in range(offered):
        seen = jnp.bool_(False)
        for f in range(e):
            seen = jnp.logical_or(seen, exported[f] == exported[e])
        again.append(seen)

    def rows_copy(e, b):
        return pltpu.make_async_copy(transport.at[b], landed_rows.at[e], block_sems.at[e])

    for e in range(offered):

        @pl.when(jnp.logical_not(again[e]))
        def _():
            rows_copy(e, exported[e]).start()

    for copy in small[1:3]:
        copy.wait()
    write_table(table, exports, positions, lives, blocks)
    for e in range(offered):

        @pl.when(again[e])
        def _():
            rows_copy(e, table[EXPORTS + e]).start()

    for copy in small[3:]:
        copy.wait()
    for b in range(blocks):
        value = landed[:, b * block : (b + 1) * block]
        state[b] = value
        low[b] = value.astype(BF16)
    for e in range(offered):
        rows_copy(e, table[EXPORTS + e]).wait()
        for s in range(slots):
            early[e, s] = landed_rows[e, s].T


def fill(ext, low, halo, table):
    blocks = low.shape[0]
    reach = halo[0].shape[0]
    ext[:blocks] = low[...]
    for link, part in enumerate(halo):
        ext[pl.ds(blocks + table[LINKS + link] * reach, reach)] = part[...]


def flux_of(b, cols, weights, ext):
    picked = jnp.concatenate([ext[cols[s, b]] for s in range(cols.shape[0])], axis=1)
    return jnp.dot(picked, weights, preferred_element_type=F32)


def stacked(rows):
    slots, block, _ = rows.shape
    return rows[...].reshape(slots * block, block)


def in_groups(count, group, one):
    def several(i, carry):
        for u in range(group):
            one(i * group + u)
        return carry

    lax.fori_loop(0, count // group, several, 0)


def tracer_weights(width):
    first = lax.axis_index("tracer") * width
    ids = (first + lax.broadcasted_iota(jnp.int32, (width, 1), 0)).astype(F32)
    return 1.0 + 8.0 * ids / (NTR - 1)


def shade_part(state, weights):
    return jnp.sum(weights * state * state, axis=0, keepdims=True)


def export_kernel(cols, table, early, low, state, *refs):
    near = len(OFFSETS)
    halo, exported, sends, ext = refs[:near], refs[near], refs[near + 1 : -1], refs[-1]
    fill(ext, low, halo, table)
    for e in range(exported.shape[0]):
        b = table[EXPORTS + e]
        value = state[b] + flux_of(b, cols, stacked(early.at[e]), ext)
        exported[e] = row_mask(b, table[LIVE], value.shape) * value
    reach = sends[0].shape[0]
    for link in range(near):
        for k in range(reach):
            sends[link][k] = exported[table[SENDS + link * reach + k]].astype(BF16)


def rest_kernel(first, cols, table, weights, low, state, *refs):
    near = len(OFFSETS)
    halo, exported, refs = refs[:near], refs[near], refs[near + 1 :]
    offered = exported.shape[0]
    rest = state.shape[0] - offered
    if first:
        early, new_state, new_low, turned, ext, landed, sems = refs

        def chunk(i):
            return pltpu.make_async_copy(weights.at[table[REST + i]], landed.at[i], sems.at[i])

        for i in range(rest):
            chunk(i).start()
    else:
        new_state, new_low, ext = refs
    fill(ext, low, halo, table)

    def put(b, value):
        new_state[b] = value
        new_low[b] = value.astype(BF16)

    for e in range(offered):
        put(table[EXPORTS + e], exported[e])
        if first:
            turned[table[EXPORTS + e]] = early[e]

    def one(i):
        b = table[REST + i]
        rows = stacked((turned if first else weights).at[b])
        value = state[b] + flux_of(b, cols, rows, ext)
        put(b, row_mask(b, table[LIVE], value.shape) * value)

    if not first:
        in_groups(rest, 8, one)
        return

    group = 2

    def turn(start):
        for i in range(group):
            b = table[REST + start + i]
            for s in range(landed.shape[1]):
                turned[b, s] = landed[start + i, s].T

    def wait(start):
        for i in range(group):
            chunk(start + i).wait()

    def several(g, carry):
        start = g * group
        wait(start + group)
        for i in range(group):
            one(start + i)
        turn(start + group)
        return carry

    wait(0)
    turn(0)
    lax.fori_loop(0, rest // group - 1, several, 0)
    for i in range(group):
        one(rest - group + i)


def whole_kernel(cols, table, turned, low, state, *refs):
    near = len(OFFSETS)
    halo, (new_state, part, ext) = refs[:near], refs[near:]
    fill(ext, low, halo, table)
    weights = tracer_weights(state.shape[1])

    def one(b):
        value = state[b] + flux_of(b, cols, stacked(turned.at[b]), ext)
        value = row_mask(b, table[LIVE], value.shape) * value
        new_state[b] = value
        part[pl.ds(b, 1), :] = shade_part(value, weights)

    in_groups(state.shape[0], 8, one)


def column_of(row):
    n = row.shape[1]
    there = lax.broadcasted_iota(jnp.int32, (n, n), 0) == lax.broadcasted_iota(jnp.int32, (n, n), 1)
    return jnp.sum(jnp.where(there, row, 0.0), axis=1, keepdims=True)


def mixed_block(value, shade, vmax, half_sat, inverse):
    level = lax.rem(lax.broadcasted_iota(jnp.int32, shade.shape, 1), LEVPAD)
    light = jnp.exp(-level.astype(F32) / LEVELS)
    uptake = vmax * (light / (1.0 + shade)) * value / (half_sat + jnp.abs(value))
    pre = (value - uptake).astype(BF16)
    return lax.dot_general(pre, inverse, (((1,), (1,)), ((), ())), preferred_element_type=F32)


def implicit_kernel(kind, peers, table, state, inverse, vmax_row, half_row, *refs):
    parts, outs = refs[:peers], refs[peers:]
    total = parts[0][...]
    for p in parts[1:]:
        total = total + p[...]
    total = total / (16.0 * NTR)
    vmax = column_of(vmax_row[...])
    half_sat = column_of(half_row[...])
    if kind == "export":
        *sends, mixes, shade = outs
        shade[...] = total
        for e in range(mixes.shape[0]):
            b = table[EXPORTS + e]
            mixed = mixed_block(state[b], shade[pl.ds(b, 1), :], vmax, half_sat, inverse[b])
            mixes[e] = (row_mask(b, table[LIVE], mixed.shape) * mixed).astype(BF16)
        reach = sends[0].shape[0]
        for link, part in enumerate(sends):
            for k in range(reach):
                part[k] = mixes[table[SENDS + link * reach + k]]
        return
    blocks, _, block = state.shape
    copies = []
    for b in range(blocks):
        mixed = mixed_block(state[b], total[b : b + 1], vmax, half_sat, inverse[b])
        mixed = row_mask(b, table[LIVE], mixed.shape) * mixed
        if kind == "rest":
            outs[0][b] = mixed
            outs[1][b] = mixed.astype(BF16)
        else:
            out, made, sems = outs
            made[:, b * block : (b + 1) * block] = mixed
            each = blocks // sems.shape[0]
            if (b + 1) % each == 0:
                part = pl.ds((b + 1 - each) * block, each * block)
                copy = pltpu.make_async_copy(made.at[:, part], out.at[:, part], sems.at[b // each])
                copy.start()
                copies.append(copy)
    for copy in copies:
        copy.wait()


def on_device(
    tracers, transport, col_slot, export_rows, send_pos, live_blocks, inverse, vmax, half_sat
):
    width, rows = tracers.shape
    blocks, slots = col_slot.shape
    block = rows // blocks
    near, reach = send_pos.shape[1:]
    offered = export_rows.shape[1]
    peers = lax.axis_size("tracer")
    row_flops = 2 * width * slots * block * block

    sends = [sent((reach, width, block), BF16)] * near
    ext = VMEM((blocks + near * reach, width, block), BF16)
    state_type = kept((blocks, width, block), F32)
    low_type = kept((blocks, width, block), BF16)

    def across(part):
        return [part] + [from_behind(part, "tracer", d) for d in range(1, peers)]

    tracers, transport = in_hbm(tracers), in_hbm(transport)
    indices = [in_hbm(export_rows), in_hbm(send_pos.transpose(1, 2, 0))]
    regions = send_pos.shape[0]
    index_scratch = [
        SMEM((1, offered), jnp.int32),
        SMEM((near, reach, regions), jnp.int32),
    ]
    halo = exchange(
        call(
            functools.partial(first_kernel, block),
            "offer_first",
            whole([*indices, tracers], pl.ANY),
            sends,
            scratch=index_scratch
            + [
                VMEM((offered, width, block), F32),
                pltpu.SemaphoreType.DMA((2,)),
                pltpu.SemaphoreType.DMA((offered,)),
            ],
        )
    )
    state, low, early, table, cols = call(
        prepare_kernel,
        "prepare",
        whole([*indices, in_hbm(live_blocks), in_hbm(col_slot.T), tracers, transport], pl.ANY),
        [
            state_type,
            low_type,
            kept((offered, slots, block, block), BF16),
            (jax.ShapeDtypeStruct((TABLE,), jnp.int32), SMEM),
            (jax.ShapeDtypeStruct((slots, blocks), jnp.int32), SMEM),
        ],
        scratch=index_scratch
        + [
            SMEM((regions,), jnp.int32),
            VMEM((width, rows), F32),
            VMEM((offered, slots, block, block), BF16),
            pltpu.SemaphoreType.DMA((5,)),
            pltpu.SemaphoreType.DMA((offered,)),
        ],
        flops=row_flops * blocks,
        moved=8 << 20,
    )
    turned = None
    landing = [
        VMEM((blocks - offered, slots, block, block), BF16),
        pltpu.SemaphoreType.DMA((blocks - offered,)),
    ]
    scalars = whole([cols, table], SMEM)
    tracer_rows = [in_vmem(inverse), vmax.reshape(1, -1), half_sat.reshape(1, -1)]
    for cycle in range(CYCLES):
        for step in range(2):
            exported, *parts = call(
                export_kernel,
                "export_step",
                scalars + whole([early, low, state, *halo]),
                [kept((offered, width, block), F32)] + sends,
                scratch=[ext],
                flops=row_flops * offered,
            )
            arriving = exchange(parts)
            first = turned is None
            state, low, *more = call(
                functools.partial(rest_kernel, first),
                "rest_step",
                scalars
                + [(transport, pl.ANY) if first else (turned, VMEM)]
                + whole([low, state, *halo, exported] + ([early] if first else [])),
                [state_type, low_type] + ([kept(transport.shape, BF16)] if first else []),
                scratch=[ext] + (landing if first else []),
                flops=row_flops * blocks,
            )
            if first:
                (turned,) = more
            halo = arriving
        state, part = call(
            whole_kernel,
            "whole_step",
            scalars + whole([turned, low, state, *halo]),
            [state_type, sent((blocks, block), F32)],
            scratch=[ext],
            flops=row_flops * blocks,
        )
        operands = [(table, SMEM)] + whole([state, *tracer_rows, *across(part)])
        if cycle == CYCLES - 1:
            (out,) = call(
                functools.partial(implicit_kernel, "last", peers),
                "last_mix",
                operands,
                [(jax.ShapeDtypeStruct((width, rows), F32), pl.ANY)],
                scratch=[VMEM((width, rows), F32), pltpu.SemaphoreType.DMA((4,))],
                flops=row_flops * blocks // slots,
            )
            return out
        halo = exchange(
            call(
                functools.partial(implicit_kernel, "export", peers),
                "export_mix",
                operands,
                sends,
                scratch=[VMEM((offered, width, block), BF16), VMEM((blocks, block), F32)],
                flops=row_flops * offered // slots,
            )
        )
        state, low = call(
            functools.partial(implicit_kernel, "rest", peers),
            "rest_mix",
            operands,
            [state_type, low_type],
            flops=row_flops * blocks // slots,
        )


def solution(mesh):
    in_specs = (
        P("tracer", "region"),
        P("region", None, None, None),
        P("region", None),
        P("region", None),
        P(),
        P(),
        P("region", None, None),
        P("tracer"),
        P("tracer"),
    )
    out_specs = P("tracer", "region")
    return jax.shard_map(
        on_device, mesh=mesh, in_specs=in_specs, out_specs=out_specs, check_vma=False
    )
```

profile of v0, /device:TPU:0, one launch (start us, length us, event | category | flops | bytes accessed | tf_op | source)
XLA Modules:
  0.0 100.8 jit_solution(8275353589845994803)
XLA Ops:
  0.0 1.7 %offer_first.1 = (bf16[4,64,128]{2,1,0:T(8,128)(2,1)S(1)}, bf16[4,64,128]{2,1,0:T(8,128)(2,1)S(1)}, bf16[4,64,128]{2,1,0:T(8,128)(2,1)S(1)}, bf16[4,64,128]{2,1,0:T(8,128)(2,1)S(1)}) custom-call(s32[1,8]{1,0:T(1,128)} %export_rows.3, s32[4,4,32]{2,1,0:T(4,128)} %bitcast.10, f32[64,4096]{1,0:T(8,128)} %tracers.3), custom_call_target="tpu_custom_call" | custom-call | bytes 1048576 | tf_op jit(solution)/shard_map/offer_first/pallas_call | solution.py:61
  1.8 6.6 %collective-permute-start = (bf16[4,64,128]{2,1,0:T(8,128)(2,1)S(1)}, bf16[4,64,128]{2,1,0:T(8,128)(2,1)S(1)}, u32[]{:S(2)}, u32[]{:S(2)}) collective-permute-start(bf16[4,64,128]{2,1,0:T(8,128)(2,1)S(1)} %get-tuple-element.57), channel_id=1, source_target_pairs={{0,120},{4,124},{8,16},{12,20},{16,8},{20,12},{24,32},{28,36},{32,... | collective-permute-start | bytes 196616 | tf_op jit(solution)/shard_map/ppermute | solution.py:44
  8.3 0.0 collective-permute-start.1
  8.3 1.2 %collective-permute-start.2 = (bf16[4,64,128]{2,1,0:T(8,128)(2,1)S(1)}, bf16[4,64,128]{2,1,0:T(8,128)(2,1)S(1)}, u32[]{:S(2)}, u32[]{:S(2)}) collective-permute-start(bf16[4,64,128]{2,1,0:T(8,128)(2,1)S(1)} %get-tuple-element.59), channel_id=1, source_target_pairs={{0,8},{4,12},{8,0},{12,4},{16,24},{20,28},{24,16},{28,20},{32,40},... | collective-permute-start | bytes 196616 | tf_op jit(solution)/shard_map/ppermute | solution.py:44
  9.5 4.2 %prepare.1 = (f32[32,64,128]{2,1,0:T(8,128)S(1)}, bf16[32,64,128]{2,1,0:T(8,128)(2,1)S(1)}, bf16[8,16,128,128]{3,2,1,0:T(8,128)(2,1)S(1)}, s32[136]{0:T(256)S(1)}, s32[16,32]{1,0:T(8,128)S(1)}) custom-call(s32[1,8]{1,0:T(1,128)} %export_rows.3, s32[4,4,32]{2,1,0:T(4,128)} %bitcast.11, s32[32]{0:T(128)} %live.1, s32[16,32]{1,0:T(8,128)} %bitcast.12, ...), custom_call_target="tpu_custom_call" | custom-call | flops 1073741824 | bytes 8388608 | tf_op jit(solution)/shard_map/prepare/pallas_call | solution.py:61
  13.7 1.6 %collective-permute-done.1.refs_1_ = bf16[4,64,128]{2,1,0:T(8,128)(2,1)S(1)} collective-permute-done((bf16[4,64,128]{2,1,0:T(8,128)(2,1)S(1)}, bf16[4,64,128]{2,1,0:T(8,128)(2,1)S(1)}, u32[]{:S(2)}, u32[]{:S(2)}) %collective-permute-start.1) | collective-permute-done | bytes 65568 | tf_op jit(solution)/shard_map/ppermute | solution.py:44
  15.3 0.0 collective-permute-done.2.refs_2_
  15.3 1.7 %export_step.4 = (f32[8,64,128]{2,1,0:T(8,128)S(1)}, bf16[4,64,128]{2,1,0:T(8,128)(2,1)S(1)}, bf16[4,64,128]{2,1,0:T(8,128)(2,1)S(1)}, bf16[4,64,128]{2,1,0:T(8,128)(2,1)S(1)}, bf16[4,64,128]{2,1,0:T(8,128)(2,1)S(1)}) custom-call(s32[16,32]{1,0:T(8,128)S(1)} %get-tuple-element.54.cols, s32[136]{0:T(256)S(1)} %get-tuple-element.53.table, ...), custom_call_target="tpu_custom_call" | custom-call | flops 268435456 | bytes 1048576 | tf_op jit(solution)/shard_map/export_step/pallas_call | solution.py:61
  17.1 2.6 %collective-permute-start.4 = (bf16[4,64,128]{2,1,0:T(8,128)(2,1)S(1)}, bf16[4,64,128]{2,1,0:T(8,128)(2,1)S(1)}, u32[]{:S(2)}, u32[]{:S(2)}) collective-permute-start(bf16[4,64,128]{2,1,0:T(8,128)(2,1)S(1)} %get-tuple-element.66), channel_id=1, source_target_pairs={{0,120},{4,124},{8,16},{12,20},{16,8},{20,12},{24,32},{28,36},{32,... | collective-permute-start | bytes 196616 | tf_op jit(solution)/shard_map/ppermute | solution.py:44
  19.6 1.7 %collective-permute-start.5 = (bf16[4,64,128]{2,1,0:T(8,128)(2,1)S(1)}, bf16[4,64,128]{2,1,0:T(8,128)(2,1)S(1)}, u32[]{:S(2)}, u32[]{:S(2)}) collective-permute-start(bf16[4,64,128]{2,1,0:T(8,128)(2,1)S(1)} %get-tuple-element.67), channel_id=1, source_target_pairs={{0,124},{4,8},{8,4},{12,16},{16,12},{20,24},{24,20},{28,32},{32,28... | collective-permute-start | bytes 196616 | tf_op jit(solution)/shard_map/ppermute | solution.py:44
  21.3 8.0 %rest_step.4 = (f32[32,64,128]{2,1,0:T(8,128)S(1)}, bf16[32,64,128]{2,1,0:T(8,128)(2,1)S(1)}, bf16[32,16,128,128]{3,2,1,0:T(8,128)(2,1)S(1)}) custom-call(s32[16,32]{1,0:T(8,128)S(1)} %get-tuple-element.54.cols, s32[136]{0:T(256)S(1)} %get-tuple-element.53.table, bf16[32,16,128,128]{3,2,1,0:T(8,128)(2,1)} %weights.1, ...), custom_call_target="tpu_custom_call" | custom-call | flops 1073741824 | bytes 1048576 | tf_op jit(solution)/shard_map/rest_step/pallas_call | solution.py:61
  29.4 0.0 collective-permute-done.4.refs_0_
  29.4 0.0 collective-permute-done.6.refs_2_
  29.4 0.0 collective-permute-done.7.refs_3_
  29.4 1.7 %export_step.5 = (f32[8,64,128]{2,1,0:T(8,128)S(1)}, bf16[4,64,128]{2,1,0:T(8,128)(2,1)S(1)}, bf16[4,64,128]{2,1,0:T(8,128)(2,1)S(1)}, bf16[4,64,128]{2,1,0:T(8,128)(2,1)S(1)}, bf16[4,64,128]{2,1,0:T(8,128)(2,1)S(1)}) custom-call(s32[16,32]{1,0:T(8,128)S(1)} %get-tuple-element.54.cols, s32[136]{0:T(256)S(1)} %get-tuple-element.53.table, ...), custom_call_target="tpu_custom_call" | custom-call | flops 268435456 | bytes 1048576 | tf_op jit(solution)/shard_map/export_step/pallas_call | solution.py:61
  31.1 3.8 %collective-permute-start.8 = (bf16[4,64,128]{2,1,0:T(8,128)(2,1)S(1)}, bf16[4,64,128]{2,1,0:T(8,128)(2,1)S(1)}, u32[]{:S(2)}, u32[]{:S(2)}) collective-permute-start(bf16[4,64,128]{2,1,0:T(8,128)(2,1)S(1)} %get-tuple-element.73), channel_id=1, source_target_pairs={{0,120},{4,124},{8,16},{12,20},{16,8},{20,12},{24,32},{28,36},{32,... | collective-permute-start | bytes 196616 | tf_op jit(solution)/shard_map/ppermute | solution.py:44
  34.9 1.4 %collective-permute-start.9 = (bf16[4,64,128]{2,1,0:T(8,128)(2,1)S(1)}, bf16[4,64,128]{2,1,0:T(8,128)(2,1)S(1)}, u32[]{:S(2)}, u32[]{:S(2)}) collective-permute-start(bf16[4,64,128]{2,1,0:T(8,128)(2,1)S(1)} %get-tuple-element.74), channel_id=1, source_target_pairs={{0,124},{4,8},{8,4},{12,16},{16,12},{20,24},{24,20},{28,32},{32,28... | collective-permute-start | bytes 196616 | tf_op jit(solution)/shard_map/ppermute | solution.py:44
  36.4 0.0 collective-permute-start.10
  36.4 0.0 collective-permute-start.11
  36.4 0.0 copy-start.1
  36.4 0.0 copy-start.2
  36.4 3.7 %rest_step.5 = (f32[32,64,128]{2,1,0:T(8,128)S(1)}, bf16[32,64,128]{2,1,0:T(8,128)(2,1)S(1)}) custom-call(s32[16,32]{1,0:T(8,128)S(1)} %get-tuple-element.54.cols, s32[136]{0:T(256)S(1)} %get-tuple-element.53.table, bf16[32,16,128,128]{3,2,1,0:T(8,128)(2,1)S(1)} %get-tuple-element.63.weights.turned, bf16[32,64,128]{2,1,0:T(8,128)(2,1)S(1)} %get-tuple-element.64.low, ...), custom_call_target="tpu_custom_call" | custom-call | flops 1073741824 | bytes 1048576 | tf_op jit(solution)/shard_map/rest_step/pallas_call | solution.py:61
  40.1 0.0 collective-permute-done.8.refs_0_
  40.1 1.9 %collective-permute-done.9.refs_1_ = bf16[4,64,128]{2,1,0:T(8,128)(2,1)S(1)} collective-permute-done((bf16[4,64,128]{2,1,0:T(8,128)(2,1)S(1)}, bf16[4,64,128]{2,1,0:T(8,128)(2,1)S(1)}, u32[]{:S(2)}, u32[]{:S(2)}) %collective-permute-start.9) | collective-permute-done | bytes 65568 | tf_op jit(solution)/shard_map/ppermute | solution.py:44
  42.0 0.0 collective-permute-done.10.refs_2_
  42.0 0.0 collective-permute-done.11.refs_3_
  42.0 4.6 %whole_step.2 = (f32[32,64,128]{2,1,0:T(8,128)S(1)}, f32[32,128]{1,0:T(8,128)S(1)}) custom-call(s32[16,32]{1,0:T(8,128)S(1)} %get-tuple-element.54.cols, s32[136]{0:T(256)S(1)} %get-tuple-element.53.table, bf16[32,16,128,128]{3,2,1,0:T(8,128)(2,1)S(1)} %get-tuple-element.63.weights.turned, bf16[32,64,128]{2,1,0:T(8,128)(2,1)S(1)} %get-tuple-element.71.low, ...), custom_call_target="tpu_custom_call" | custom-call | flops 1073741824 | bytes 1048576 | tf_op jit(solution)/shard_map/whole_step/pallas_call | solution.py:61
  46.6 2.8 %collective-permute-start.14 = (f32[32,128]{1,0:T(8,128)S(1)}, f32[32,128]{1,0:T(8,128)S(1)}, u32[]{:S(2)}, u32[]{:S(2)}) collective-permute-start(f32[32,128]{1,0:T(8,128)S(1)} %get-tuple-element.78.refs_0_), channel_id=1, source_target_pairs={{1,0},{2,1},{3,2},{0,3},{5,4},{6,5},{7,6},{4,7},{9,8},{10,9},{11,1... | collective-permute-start | bytes 49160 | tf_op jit(solution)/shard_map/ppermute | solution.py:27
  49.4 0.8 collective-permute-start.13
  50.2 0.9 collective-permute-start.12
  51.1 3.5 %collective-permute-done.13.refs_2_ = f32[32,128]{1,0:T(8,128)S(1)} collective-permute-done((f32[32,128]{1,0:T(8,128)S(1)}, f32[32,128]{1,0:T(8,128)S(1)}, u32[]{:S(2)}, u32[]{:S(2)}) %collective-permute-start.13) | collective-permute-done | bytes 16416 | tf_op jit(solution)/shard_map/ppermute | solution.py:27
  54.7 0.5 collective-permute-done.12.refs_1_
  55.2 0.9 export_mix.1
  56.1 2.4 %collective-permute-start.15 = (bf16[4,64,128]{2,1,0:T(8,128)(2,1)S(1)}, bf16[4,64,128]{2,1,0:T(8,128)(2,1)S(1)}, u32[]{:S(2)}, u32[]{:S(2)}) collective-permute-start(bf16[4,64,128]{2,1,0:T(8,128)(2,1)S(1)} %get-tuple-element.81), channel_id=1, source_target_pairs={{0,120},{4,124},{8,16},{12,20},{16,8},{20,12},{24,32},{28,36},{32,... | collective-permute-start | bytes 196616 | tf_op jit(solution)/shard_map/ppermute | solution.py:44
  58.5 0.0 collective-permute-start.16
  58.5 0.0 collective-permute-start.17
  58.5 0.0 collective-permute-start.18
  58.5 1.4 %rest_mix.1 = (f32[32,64,128]{2,1,0:T(8,128)S(1)}, bf16[32,64,128]{2,1,0:T(8,128)(2,1)S(1)}) custom-call(s32[136]{0:T(256)S(1)} %get-tuple-element.53.table, f32[32,64,128]{2,1,0:T(8,128)S(1)} %get-tuple-element.77.state, bf16[32,128,128]{2,1,0:T(8,128)(2,1)S(1)} %copy-done, f32[1,64]{1,0:T(1,128)S(1)} %bitcast.5, f32[1,64]{1,0:T(1,128)S(1)} %bitcast.8, ...), custom_call_target="tpu_custom_call" | custom-call | flops 67108864 | bytes 1048576 | tf_op jit(solution)/shard_map/rest_mix/pallas_call | solution.py:61
  60.0 4.0 %collective-permute-done.15.refs_0_ = bf16[4,64,128]{2,1,0:T(8,128)(2,1)S(1)} collective-permute-done((bf16[4,64,128]{2,1,0:T(8,128)(2,1)S(1)}, bf16[4,64,128]{2,1,0:T(8,128)(2,1)S(1)}, u32[]{:S(2)}, u32[]{:S(2)}) %collective-permute-start.15) | collective-permute-done | bytes 65568 | tf_op jit(solution)/shard_map/ppermute | solution.py:44
  63.9 1.6 %collective-permute-done.16.refs_1_ = bf16[4,64,128]{2,1,0:T(8,128)(2,1)S(1)} collective-permute-done((bf16[4,64,128]{2,1,0:T(8,128)(2,1)S(1)}, bf16[4,64,128]{2,1,0:T(8,128)(2,1)S(1)}, u32[]{:S(2)}, u32[]{:S(2)}) %collective-permute-start.16) | collective-permute-done | bytes 65568 | tf_op jit(solution)/shard_map/ppermute | solution.py:44
  65.5 0.0 collective-permute-done.17.refs_2_
  65.5 0.0 collective-permute-done.18.refs_3_
  65.5 1.7 %export_step.6 = (f32[8,64,128]{2,1,0:T(8,128)S(1)}, bf16[4,64,128]{2,1,0:T(8,128)(2,1)S(1)}, bf16[4,64,128]{2,1,0:T(8,128)(2,1)S(1)}, bf16[4,64,128]{2,1,0:T(8,128)(2,1)S(1)}, bf16[4,64,128]{2,1,0:T(8,128)(2,1)S(1)}) custom-call(s32[16,32]{1,0:T(8,128)S(1)} %get-tuple-element.54.cols, s32[136]{0:T(256)S(1)} %get-tuple-element.53.table, ...), custom_call_target="tpu_custom_call" | custom-call | flops 268435456 | bytes 1048576 | tf_op jit(solution)/shard_map/export_step/pallas_call | solution.py:61
  67.2 0.7 collective-permute-start.19
  67.9 0.7 collective-permute-start.20
  68.6 1.7 %collective-permute-start.21 = (bf16[4,64,128]{2,1,0:T(8,128)(2,1)S(1)}, bf16[4,64,128]{2,1,0:T(8,128)(2,1)S(1)}, u32[]{:S(2)}, u32[]{:S(2)}) collective-permute-start(bf16[4,64,128]{2,1,0:T(8,128)(2,1)S(1)} %get-tuple-element.90), channel_id=1, source_target_pairs={{0,8},{4,12},{8,0},{12,4},{16,24},{20,28},{24,16},{28,20},{32,40},... | collective-permute-start | bytes 196616 | tf_op jit(solution)/shard_map/ppermute | solution.py:44
  70.2 0.0 collective-permute-start.22
  70.2 3.7 %rest_step.6 = (f32[32,64,128]{2,1,0:T(8,128)S(1)}, bf16[32,64,128]{2,1,0:T(8,128)(2,1)S(1)}) custom-call(s32[16,32]{1,0:T(8,128)S(1)} %get-tuple-element.54.cols, s32[136]{0:T(256)S(1)} %get-tuple-element.53.table, bf16[32,16,128,128]{3,2,1,0:T(8,128)(2,1)S(1)} %get-tuple-element.63.weights.turned, bf16[32,64,128]{2,1,0:T(8,128)(2,1)S(1)} %get-tuple-element.79.low, ...), custom_call_target="tpu_custom_call" | custom-call | flops 1073741824 | bytes 1048576 | tf_op jit(solution)/shard_map/rest_step/pallas_call | solution.py:61
  73.9 1.7 %collective-permute-done.19.refs_0_ = bf16[4,64,128]{2,1,0:T(8,128)(2,1)S(1)} collective-permute-done((bf16[4,64,128]{2,1,0:T(8,128)(2,1)S(1)}, bf16[4,64,128]{2,1,0:T(8,128)(2,1)S(1)}, u32[]{:S(2)}, u32[]{:S(2)}) %collective-permute-start.19) | collective-permute-done | bytes 65568 | tf_op jit(solution)/shard_map/ppermute | solution.py:44
  75.6 0.0 collective-permute-done.20.refs_1_
  75.6 1.7 %export_step.7 = (f32[8,64,128]{2,1,0:T(8,128)S(1)}, bf16[4,64,128]{2,1,0:T(8,128)(2,1)S(1)}, bf16[4,64,128]{2,1,0:T(8,128)(2,1)S(1)}, bf16[4,64,128]{2,1,0:T(8,128)(2,1)S(1)}, bf16[4,64,128]{2,1,0:T(8,128)(2,1)S(1)}) custom-call(s32[16,32]{1,0:T(8,128)S(1)} %get-tuple-element.54.cols, s32[136]{0:T(256)S(1)} %get-tuple-element.53.table, ...), custom_call_target="tpu_custom_call" | custom-call | flops 268435456 | bytes 1048576 | tf_op jit(solution)/shard_map/export_step/pallas_call | solution.py:61
  77.3 2.7 %collective-permute-start.23 = (bf16[4,64,128]{2,1,0:T(8,128)(2,1)S(1)}, bf16[4,64,128]{2,1,0:T(8,128)(2,1)S(1)}, u32[]{:S(2)}, u32[]{:S(2)}) collective-permute-start(bf16[4,64,128]{2,1,0:T(8,128)(2,1)S(1)} %get-tuple-element.95), channel_id=1, source_target_pairs={{0,120},{4,124},{8,16},{12,20},{16,8},{20,12},{24,32},{28,36},{32,... | collective-permute-start | bytes 196616 | tf_op jit(solution)/shard_map/ppermute | solution.py:44
  80.0 0.9 collective-permute-start.24
  80.9 0.5 collective-permute-start.25
  81.4 3.6 %rest_step.7 = (f32[32,64,128]{2,1,0:T(8,128)S(1)}, bf16[32,64,128]{2,1,0:T(8,128)(2,1)S(1)}) custom-call(s32[16,32]{1,0:T(8,128)S(1)} %get-tuple-element.54.cols, s32[136]{0:T(256)S(1)} %get-tuple-element.53.table, bf16[32,16,128,128]{3,2,1,0:T(8,128)(2,1)S(1)} %get-tuple-element.63.weights.turned, bf16[32,64,128]{2,1,0:T(8,128)(2,1)S(1)} %get-tuple-element.86.low, ...), custom_call_target="tpu_custom_call" | custom-call | flops 1073741824 | bytes 1048576 | tf_op jit(solution)/shard_map/rest_step/pallas_call | solution.py:61
  85.0 2.0 %collective-permute-done.24.refs_1_ = bf16[4,64,128]{2,1,0:T(8,128)(2,1)S(1)} collective-permute-done((bf16[4,64,128]{2,1,0:T(8,128)(2,1)S(1)}, bf16[4,64,128]{2,1,0:T(8,128)(2,1)S(1)}, u32[]{:S(2)}, u32[]{:S(2)}) %collective-permute-start.24) | collective-permute-done | bytes 65568 | tf_op jit(solution)/shard_map/ppermute | solution.py:44
  87.0 4.6 %whole_step.3 = (f32[32,64,128]{2,1,0:T(8,128)S(1)}, f32[32,128]{1,0:T(8,128)S(1)}) custom-call(s32[16,32]{1,0:T(8,128)S(1)} %get-tuple-element.54.cols, s32[136]{0:T(256)S(1)} %get-tuple-element.53.table, bf16[32,16,128,128]{3,2,1,0:T(8,128)(2,1)S(1)} %get-tuple-element.63.weights.turned, bf16[32,64,128]{2,1,0:T(8,128)(2,1)S(1)} %get-tuple-element.93.low, ...), custom_call_target="tpu_custom_call" | custom-call | flops 1073741824 | bytes 1048576 | tf_op jit(solution)/shard_map/whole_step/pallas_call | solution.py:61
  91.7 0.4 collective-permute-start.29
  92.1 1.4 %collective-permute-start.28 = (f32[32,128]{1,0:T(8,128)S(1)}, f32[32,128]{1,0:T(8,128)S(1)}, u32[]{:S(2)}, u32[]{:S(2)}) collective-permute-start(f32[32,128]{1,0:T(8,128)S(1)} %get-tuple-element.100.refs_0_), channel_id=1, source_target_pairs={{2,0},{3,1},{0,2},{1,3},{6,4},{7,5},{4,6},{5,7},{10,8},{11,9},{8,1... | collective-permute-start | bytes 49160 | tf_op jit(solution)/shard_map/ppermute | solution.py:27
  93.5 1.2 %collective-permute-start.27 = (f32[32,128]{1,0:T(8,128)S(1)}, f32[32,128]{1,0:T(8,128)S(1)}, u32[]{:S(2)}, u32[]{:S(2)}) collective-permute-start(f32[32,128]{1,0:T(8,128)S(1)} %get-tuple-element.100.refs_0_), channel_id=1, source_target_pairs={{3,0},{0,1},{1,2},{2,3},{7,4},{4,5},{5,6},{6,7},{11,8},{8,9},{9,10... | collective-permute-start | bytes 49160 | tf_op jit(solution)/shard_map/ppermute | solution.py:27
  94.7 0.8 collective-permute-done.29.refs_3_
  95.5 1.8 %collective-permute-done.28.refs_2_ = f32[32,128]{1,0:T(8,128)S(1)} collective-permute-done((f32[32,128]{1,0:T(8,128)S(1)}, f32[32,128]{1,0:T(8,128)S(1)}, u32[]{:S(2)}, u32[]{:S(2)}) %collective-permute-start.28) | collective-permute-done | bytes 16416 | tf_op jit(solution)/shard_map/ppermute | solution.py:27
  97.3 1.1 %collective-permute-done.27.refs_1_ = f32[32,128]{1,0:T(8,128)S(1)} collective-permute-done((f32[32,128]{1,0:T(8,128)S(1)}, f32[32,128]{1,0:T(8,128)S(1)}, u32[]{:S(2)}, u32[]{:S(2)}) %collective-permute-start.27) | collective-permute-done | bytes 16416 | tf_op jit(solution)/shard_map/ppermute | solution.py:27
  98.4 2.2 %last_mix.1 = f32[64,4096]{1,0:T(8,128)} custom-call(s32[136]{0:T(256)S(1)} %get-tuple-element.53.table, f32[32,64,128]{2,1,0:T(8,128)S(1)} %get-tuple-element.99.state, bf16[32,128,128]{2,1,0:T(8,128)(2,1)S(1)} %copy-done, f32[1,64]{1,0:T(1,128)S(1)} %bitcast.6, f32[1,64]{1,0:T(1,128)S(1)} %bitcast.9, f32[32,128]{1,0:T(8,128)S(1)} %get-tuple-element.100.refs_0_, ...), custom_call_target="tpu_custom_call" | custom-call | flops 67108864 | bytes 1048576 | tf_op jit(solution)/shard_map/last_mix/pallas_call | solution.py:61
  (17 shorter events, 0.0 us)
Async XLA Ops:
  1.8 12.0 %collective-permute-start = (bf16[4,64,128]{2,1,0:T(8,128)(2,1)S(1)}, bf16[4,64,128]{2,1,0:T(8,128)(2,1)S(1)}, u32[]{:S(2)}, u32[]{:S(2)}) collective-permute-start(bf16[4,64,128]{2,1,0:T(8,128)(2,1)S(1)} %get-tuple-element.57), channel_id=1, source_target_pairs={{0,120},{4,124},{8,16},{12,20},{16,8},{20,12},{24,32},{28,36},{32,... | collective-permute-start | bytes 196616 | tf_op jit(solution)/shard_map/ppermute | solution.py:44
  8.3 7.0 %collective-permute-start.1 = (bf16[4,64,128]{2,1,0:T(8,128)(2,1)S(1)}, bf16[4,64,128]{2,1,0:T(8,128)(2,1)S(1)}, u32[]{:S(2)}, u32[]{:S(2)}) collective-permute-start(bf16[4,64,128]{2,1,0:T(8,128)(2,1)S(1)} %get-tuple-element.58), channel_id=1, source_target_pairs={{0,124},{4,8},{8,4},{12,16},{16,12},{20,24},{24,20},{28,32},{32,28... | collective-permute-start | bytes 196616 | tf_op jit(solution)/shard_map/ppermute | solution.py:44
  8.3 7.0 %collective-permute-start.2 = (bf16[4,64,128]{2,1,0:T(8,128)(2,1)S(1)}, bf16[4,64,128]{2,1,0:T(8,128)(2,1)S(1)}, u32[]{:S(2)}, u32[]{:S(2)}) collective-permute-start(bf16[4,64,128]{2,1,0:T(8,128)(2,1)S(1)} %get-tuple-element.59), channel_id=1, source_target_pairs={{0,8},{4,12},{8,0},{12,4},{16,24},{20,28},{24,16},{28,20},{32,40},... | collective-permute-start | bytes 196616 | tf_op jit(solution)/shard_map/ppermute | solution.py:44
  9.5 5.8 %collective-permute-start.3 = (bf16[4,64,128]{2,1,0:T(8,128)(2,1)S(1)}, bf16[4,64,128]{2,1,0:T(8,128)(2,1)S(1)}, u32[]{:S(2)}, u32[]{:S(2)}) collective-permute-start(bf16[4,64,128]{2,1,0:T(8,128)(2,1)S(1)} %get-tuple-element.60), channel_id=1, source_target_pairs={{0,4},{4,0},{8,12},{12,8},{16,20},{20,16},{24,28},{28,24},{32,36},... | collective-permute-start | bytes 196616 | tf_op jit(solution)/shard_map/ppermute | solution.py:44
  17.1 12.3 %collective-permute-start.4 = (bf16[4,64,128]{2,1,0:T(8,128)(2,1)S(1)}, bf16[4,64,128]{2,1,0:T(8,128)(2,1)S(1)}, u32[]{:S(2)}, u32[]{:S(2)}) collective-permute-start(bf16[4,64,128]{2,1,0:T(8,128)(2,1)S(1)} %get-tuple-element.66), channel_id=1, source_target_pairs={{0,120},{4,124},{8,16},{12,20},{16,8},{20,12},{24,32},{28,36},{32,... | collective-permute-start | bytes 196616 | tf_op jit(solution)/shard_map/ppermute | solution.py:44
  19.6 9.8 %collective-permute-start.5 = (bf16[4,64,128]{2,1,0:T(8,128)(2,1)S(1)}, bf16[4,64,128]{2,1,0:T(8,128)(2,1)S(1)}, u32[]{:S(2)}, u32[]{:S(2)}) collective-permute-start(bf16[4,64,128]{2,1,0:T(8,128)(2,1)S(1)} %get-tuple-element.67), channel_id=1, source_target_pairs={{0,124},{4,8},{8,4},{12,16},{16,12},{20,24},{24,20},{28,32},{32,28... | collective-permute-start | bytes 196616 | tf_op jit(solution)/shard_map/ppermute | solution.py:44
  21.3 8.1 %collective-permute-start.6 = (bf16[4,64,128]{2,1,0:T(8,128)(2,1)S(1)}, bf16[4,64,128]{2,1,0:T(8,128)(2,1)S(1)}, u32[]{:S(2)}, u32[]{:S(2)}) collective-permute-start(bf16[4,64,128]{2,1,0:T(8,128)(2,1)S(1)} %get-tuple-element.68), channel_id=1, source_target_pairs={{0,8},{4,12},{8,0},{12,4},{16,24},{20,28},{24,16},{28,20},{32,40},... | collective-permute-start | bytes 196616 | tf_op jit(solution)/shard_map/ppermute | solution.py:44
  21.3 8.1 %collective-permute-start.7 = (bf16[4,64,128]{2,1,0:T(8,128)(2,1)S(1)}, bf16[4,64,128]{2,1,0:T(8,128)(2,1)S(1)}, u32[]{:S(2)}, u32[]{:S(2)}) collective-permute-start(bf16[4,64,128]{2,1,0:T(8,128)(2,1)S(1)} %get-tuple-element.69), channel_id=1, source_target_pairs={{0,4},{4,0},{8,12},{12,8},{16,20},{20,16},{24,28},{28,24},{32,36},... | collective-permute-start | bytes 196616 | tf_op jit(solution)/shard_map/ppermute | solution.py:44
  31.1 8.9 %collective-permute-start.8 = (bf16[4,64,128]{2,1,0:T(8,128)(2,1)S(1)}, bf16[4,64,128]{2,1,0:T(8,128)(2,1)S(1)}, u32[]{:S(2)}, u32[]{:S(2)}) collective-permute-start(bf16[4,64,128]{2,1,0:T(8,128)(2,1)S(1)} %get-tuple-element.73), channel_id=1, source_target_pairs={{0,120},{4,124},{8,16},{12,20},{16,8},{20,12},{24,32},{28,36},{32,... | collective-permute-start | bytes 196616 | tf_op jit(solution)/shard_map/ppermute | solution.py:44
  34.9 7.0 %collective-permute-start.9 = (bf16[4,64,128]{2,1,0:T(8,128)(2,1)S(1)}, bf16[4,64,128]{2,1,0:T(8,128)(2,1)S(1)}, u32[]{:S(2)}, u32[]{:S(2)}) collective-permute-start(bf16[4,64,128]{2,1,0:T(8,128)(2,1)S(1)} %get-tuple-element.74), channel_id=1, source_target_pairs={{0,124},{4,8},{8,4},{12,16},{16,12},{20,24},{24,20},{28,32},{32,28... | collective-permute-start | bytes 196616 | tf_op jit(solution)/shard_map/ppermute | solution.py:44
  36.4 5.6 %collective-permute-start.10 = (bf16[4,64,128]{2,1,0:T(8,128)(2,1)S(1)}, bf16[4,64,128]{2,1,0:T(8,128)(2,1)S(1)}, u32[]{:S(2)}, u32[]{:S(2)}) collective-permute-start(bf16[4,64,128]{2,1,0:T(8,128)(2,1)S(1)} %get-tuple-element.75), channel_id=1, source_target_pairs={{0,8},{4,12},{8,0},{12,4},{16,24},{20,28},{24,16},{28,20},{32,40},... | collective-permute-start | bytes 196616 | tf_op jit(solution)/shard_map/ppermute | solution.py:44
  36.4 5.6 %collective-permute-start.11 = (bf16[4,64,128]{2,1,0:T(8,128)(2,1)S(1)}, bf16[4,64,128]{2,1,0:T(8,128)(2,1)S(1)}, u32[]{:S(2)}, u32[]{:S(2)}) collective-permute-start(bf16[4,64,128]{2,1,0:T(8,128)(2,1)S(1)} %get-tuple-element.76), channel_id=1, source_target_pairs={{0,4},{4,0},{8,12},{12,8},{16,20},{20,16},{24,28},{28,24},{32,36},... | collective-permute-start | bytes 196616 | tf_op jit(solution)/shard_map/ppermute | solution.py:44
  36.4 18.8 %copy-start = (bf16[32,128,128]{2,1,0:T(8,128)(2,1)S(1)}, bf16[32,128,128]{2,1,0:T(8,128)(2,1)}, u32[]{:S(2)}) copy-start(bf16[32,128,128]{2,1,0:T(8,128)(2,1)} %inverse.5) | copy-start | bytes 3145732
  36.4 18.8 %copy-start.1 = (f32[64]{0:T(128)S(1)}, f32[64]{0:T(128)}, u32[]{:S(2)}) copy-start(f32[64]{0:T(128)} %param.16) | copy-start | bytes 772
  36.4 18.8 %copy-start.2 = (f32[64]{0:T(128)S(1)}, f32[64]{0:T(128)}, u32[]{:S(2)}) copy-start(f32[64]{0:T(128)} %param.17) | copy-start | bytes 772
  46.6 4.5 %collective-permute-start.14 = (f32[32,128]{1,0:T(8,128)S(1)}, f32[32,128]{1,0:T(8,128)S(1)}, u32[]{:S(2)}, u32[]{:S(2)}) collective-permute-start(f32[32,128]{1,0:T(8,128)S(1)} %get-tuple-element.78.refs_0_), channel_id=1, source_target_pairs={{1,0},{2,1},{3,2},{0,3},{5,4},{6,5},{7,6},{4,7},{9,8},{10,9},{11,1... | collective-permute-start | bytes 49160 | tf_op jit(solution)/shard_map/ppermute | solution.py:27
  49.4 5.2 %collective-permute-start.13 = (f32[32,128]{1,0:T(8,128)S(1)}, f32[32,128]{1,0:T(8,128)S(1)}, u32[]{:S(2)}, u32[]{:S(2)}) collective-permute-start(f32[32,128]{1,0:T(8,128)S(1)} %get-tuple-element.78.refs_0_), channel_id=1, source_target_pairs={{2,0},{3,1},{0,2},{1,3},{6,4},{7,5},{4,6},{5,7},{10,8},{11,9},{8,1... | collective-permute-start | bytes 49160 | tf_op jit(solution)/shard_map/ppermute | solution.py:27
  50.2 4.9 %collective-permute-start.12 = (f32[32,128]{1,0:T(8,128)S(1)}, f32[32,128]{1,0:T(8,128)S(1)}, u32[]{:S(2)}, u32[]{:S(2)}) collective-permute-start(f32[32,128]{1,0:T(8,128)S(1)} %get-tuple-element.78.refs_0_), channel_id=1, source_target_pairs={{3,0},{0,1},{1,2},{2,3},{7,4},{4,5},{5,6},{6,7},{11,8},{8,9},{9,10... | collective-permute-start | bytes 49160 | tf_op jit(solution)/shard_map/ppermute | solution.py:27
  56.1 7.8 %collective-permute-start.15 = (bf16[4,64,128]{2,1,0:T(8,128)(2,1)S(1)}, bf16[4,64,128]{2,1,0:T(8,128)(2,1)S(1)}, u32[]{:S(2)}, u32[]{:S(2)}) collective-permute-start(bf16[4,64,128]{2,1,0:T(8,128)(2,1)S(1)} %get-tuple-element.81), channel_id=1, source_target_pairs={{0,120},{4,124},{8,16},{12,20},{16,8},{20,12},{24,32},{28,36},{32,... | collective-permute-start | bytes 196616 | tf_op jit(solution)/shard_map/ppermute | solution.py:44
  58.5 7.0 %collective-permute-start.16 = (bf16[4,64,128]{2,1,0:T(8,128)(2,1)S(1)}, bf16[4,64,128]{2,1,0:T(8,128)(2,1)S(1)}, u32[]{:S(2)}, u32[]{:S(2)}) collective-permute-start(bf16[4,64,128]{2,1,0:T(8,128)(2,1)S(1)} %get-tuple-element.82), channel_id=1, source_target_pairs={{0,124},{4,8},{8,4},{12,16},{16,12},{20,24},{24,20},{28,32},{32,28... | collective-permute-start | bytes 196616 | tf_op jit(solution)/shard_map/ppermute | solution.py:44
  58.5 7.0 %collective-permute-start.17 = (bf16[4,64,128]{2,1,0:T(8,128)(2,1)S(1)}, bf16[4,64,128]{2,1,0:T(8,128)(2,1)S(1)}, u32[]{:S(2)}, u32[]{:S(2)}) collective-permute-start(bf16[4,64,128]{2,1,0:T(8,128)(2,1)S(1)} %get-tuple-element.83), channel_id=1, source_target_pairs={{0,8},{4,12},{8,0},{12,4},{16,24},{20,28},{24,16},{28,20},{32,40},... | collective-permute-start | bytes 196616 | tf_op jit(solution)/shard_map/ppermute | solution.py:44
  58.5 7.0 %collective-permute-start.18 = (bf16[4,64,128]{2,1,0:T(8,128)(2,1)S(1)}, bf16[4,64,128]{2,1,0:T(8,128)(2,1)S(1)}, u32[]{:S(2)}, u32[]{:S(2)}) collective-permute-start(bf16[4,64,128]{2,1,0:T(8,128)(2,1)S(1)} %get-tuple-element.84), channel_id=1, source_target_pairs={{0,4},{4,0},{8,12},{12,8},{16,20},{20,16},{24,28},{28,24},{32,36},... | collective-permute-start | bytes 196616 | tf_op jit(solution)/shard_map/ppermute | solution.py:44
  67.2 8.4 %collective-permute-start.19 = (bf16[4,64,128]{2,1,0:T(8,128)(2,1)S(1)}, bf16[4,64,128]{2,1,0:T(8,128)(2,1)S(1)}, u32[]{:S(2)}, u32[]{:S(2)}) collective-permute-start(bf16[4,64,128]{2,1,0:T(8,128)(2,1)S(1)} %get-tuple-element.88), channel_id=1, source_target_pairs={{0,120},{4,124},{8,16},{12,20},{16,8},{20,12},{24,32},{28,36},{32,... | collective-permute-start | bytes 196616 | tf_op jit(solution)/shard_map/ppermute | solution.py:44
  67.9 7.7 %collective-permute-start.20 = (bf16[4,64,128]{2,1,0:T(8,128)(2,1)S(1)}, bf16[4,64,128]{2,1,0:T(8,128)(2,1)S(1)}, u32[]{:S(2)}, u32[]{:S(2)}) collective-permute-start(bf16[4,64,128]{2,1,0:T(8,128)(2,1)S(1)} %get-tuple-element.89), channel_id=1, source_target_pairs={{0,124},{4,8},{8,4},{12,16},{16,12},{20,24},{24,20},{28,32},{32,28... | collective-permute-start | bytes 196616 | tf_op jit(solution)/shard_map/ppermute | solution.py:44
  68.6 7.0 %collective-permute-start.21 = (bf16[4,64,128]{2,1,0:T(8,128)(2,1)S(1)}, bf16[4,64,128]{2,1,0:T(8,128)(2,1)S(1)}, u32[]{:S(2)}, u32[]{:S(2)}) collective-permute-start(bf16[4,64,128]{2,1,0:T(8,128)(2,1)S(1)} %get-tuple-element.90), channel_id=1, source_target_pairs={{0,8},{4,12},{8,0},{12,4},{16,24},{20,28},{24,16},{28,20},{32,40},... | collective-permute-start | bytes 196616 | tf_op jit(solution)/shard_map/ppermute | solution.py:44
  70.2 5.4 %collective-permute-start.22 = (bf16[4,64,128]{2,1,0:T(8,128)(2,1)S(1)}, bf16[4,64,128]{2,1,0:T(8,128)(2,1)S(1)}, u32[]{:S(2)}, u32[]{:S(2)}) collective-permute-start(bf16[4,64,128]{2,1,0:T(8,128)(2,1)S(1)} %get-tuple-element.91), channel_id=1, source_target_pairs={{0,4},{4,0},{8,12},{12,8},{16,20},{20,16},{24,28},{28,24},{32,36},... | collective-permute-start | bytes 196616 | tf_op jit(solution)/shard_map/ppermute | solution.py:44
  77.3 7.7 %collective-permute-start.23 = (bf16[4,64,128]{2,1,0:T(8,128)(2,1)S(1)}, bf16[4,64,128]{2,1,0:T(8,128)(2,1)S(1)}, u32[]{:S(2)}, u32[]{:S(2)}) collective-permute-start(bf16[4,64,128]{2,1,0:T(8,128)(2,1)S(1)} %get-tuple-element.95), channel_id=1, source_target_pairs={{0,120},{4,124},{8,16},{12,20},{16,8},{20,12},{24,32},{28,36},{32,... | collective-permute-start | bytes 196616 | tf_op jit(solution)/shard_map/ppermute | solution.py:44
  80.0 7.0 %collective-permute-start.24 = (bf16[4,64,128]{2,1,0:T(8,128)(2,1)S(1)}, bf16[4,64,128]{2,1,0:T(8,128)(2,1)S(1)}, u32[]{:S(2)}, u32[]{:S(2)}) collective-permute-start(bf16[4,64,128]{2,1,0:T(8,128)(2,1)S(1)} %get-tuple-element.96), channel_id=1, source_target_pairs={{0,124},{4,8},{8,4},{12,16},{16,12},{20,24},{24,20},{28,32},{32,28... | collective-permute-start | bytes 196616 | tf_op jit(solution)/shard_map/ppermute | solution.py:44
  80.9 6.1 %collective-permute-start.25 = (bf16[4,64,128]{2,1,0:T(8,128)(2,1)S(1)}, bf16[4,64,128]{2,1,0:T(8,128)(2,1)S(1)}, u32[]{:S(2)}, u32[]{:S(2)}) collective-permute-start(bf16[4,64,128]{2,1,0:T(8,128)(2,1)S(1)} %get-tuple-element.97), channel_id=1, source_target_pairs={{0,8},{4,12},{8,0},{12,4},{16,24},{20,28},{24,16},{28,20},{32,40},... | collective-permute-start | bytes 196616 | tf_op jit(solution)/shard_map/ppermute | solution.py:44
  81.4 5.7 %collective-permute-start.26 = (bf16[4,64,128]{2,1,0:T(8,128)(2,1)S(1)}, bf16[4,64,128]{2,1,0:T(8,128)(2,1)S(1)}, u32[]{:S(2)}, u32[]{:S(2)}) collective-permute-start(bf16[4,64,128]{2,1,0:T(8,128)(2,1)S(1)} %get-tuple-element.98), channel_id=1, source_target_pairs={{0,4},{4,0},{8,12},{12,8},{16,20},{20,16},{24,28},{28,24},{32,36},... | collective-permute-start | bytes 196616 | tf_op jit(solution)/shard_map/ppermute | solution.py:44
  91.7 3.8 %collective-permute-start.29 = (f32[32,128]{1,0:T(8,128)S(1)}, f32[32,128]{1,0:T(8,128)S(1)}, u32[]{:S(2)}, u32[]{:S(2)}) collective-permute-start(f32[32,128]{1,0:T(8,128)S(1)} %get-tuple-element.100.refs_0_), channel_id=1, source_target_pairs={{1,0},{2,1},{3,2},{0,3},{5,4},{6,5},{7,6},{4,7},{9,8},{10,9},{11,1... | collective-permute-start | bytes 49160 | tf_op jit(solution)/shard_map/ppermute | solution.py:27
  92.1 5.2 %collective-permute-start.28 = (f32[32,128]{1,0:T(8,128)S(1)}, f32[32,128]{1,0:T(8,128)S(1)}, u32[]{:S(2)}, u32[]{:S(2)}) collective-permute-start(f32[32,128]{1,0:T(8,128)S(1)} %get-tuple-element.100.refs_0_), channel_id=1, source_target_pairs={{2,0},{3,1},{0,2},{1,3},{6,4},{7,5},{4,6},{5,7},{10,8},{11,9},{8,1... | collective-permute-start | bytes 49160 | tf_op jit(solution)/shard_map/ppermute | solution.py:27
  93.5 4.9 %collective-permute-start.27 = (f32[32,128]{1,0:T(8,128)S(1)}, f32[32,128]{1,0:T(8,128)S(1)}, u32[]{:S(2)}, u32[]{:S(2)}) collective-permute-start(f32[32,128]{1,0:T(8,128)S(1)} %get-tuple-element.100.refs_0_), channel_id=1, source_target_pairs={{3,0},{0,1},{1,2},{2,3},{7,4},{4,5},{5,6},{6,7},{11,8},{8,9},{9,10... | collective-permute-start | bytes 49160 | tf_op jit(solution)/shard_map/ppermute | solution.py:27
where the time goes:
time: 101 us
  Pallas kernels  45.5 us (45%)
  starting transfers between devices  34.3 us (34%)
  waiting for transfers between devices  20.6 us (20%)
    pallas_call x15, Pallas kernels, call(): pl.pallas_call(kernel, in_specs=[spec(s) for _, s in args], out_specs=[sp...  45.5 us
    ppermute x24, starting transfers between devices, exchange(): arrived.append(lax.ppermute(part, 'region', route))  26.7 us
    ppermute x24, waiting for transfers between devices, exchange(): arrived.append(lax.ppermute(part, 'region', route))  12.8 us
    ppermute x6, waiting for transfers between devices, from_behind(): return lax.ppermute(value, axis, route)  7.81 us
    ppermute x6, starting transfers between devices, from_behind(): return lax.ppermute(value, axis, route)  7.52 us
  transfers between devices with their start and end apart: 30, of which 11 were waited for; matrix products, arithmetic and copies ran while one was open for 0% of the time, Pallas kernels for 24%

commit v1 on v0

--- a/solution.py
+++ b/solution.py
@@ -281,7 +281,7 @@
     offered = exported.shape[0]
     rest = state.shape[0] - offered
     if first:
-        early, new_state, new_low, turned, ext, landed, sems = refs
+        early, new_state, new_low, turned, ext, landed, sems, *fresh = refs
 
         def chunk(i):
             return pltpu.make_async_copy(weights.at[table[REST + i]], landed.at[i], sems.at[i])
@@ -301,41 +301,50 @@
         if first:
             turned[table[EXPORTS + e]] = early[e]
 
-    def one(i):
+    def one(i, rows):
         b = table[REST + i]
-        rows = stacked((turned if first else weights).at[b])
         value = state[b] + flux_of(b, cols, rows, ext)
         put(b, row_mask(b, table[LIVE], value.shape) * value)
 
     if not first:
-        in_groups(rest, 8, one)
+        in_groups(rest, 8, lambda i: one(i, stacked(weights.at[table[REST + i]])))
         return
 
-    group = 2
-
-    def turn(start):
+    group = fresh[0].shape[0]
+
+    def turn(start, there):
         for i in range(group):
             b = table[REST + start + i]
             for s in range(landed.shape[1]):
-                turned[b, s] = landed[start + i, s].T
+                tile = landed[start + i, s].T
+                turned[b, s] = tile
+                there[i, s] = tile
 
     def wait(start):
         for i in range(group):
             chunk(start + i).wait()
 
+    def compute(start, there):
+        for i in range(group):
+            one(start + i, stacked(there.at[i]))
+
     def several(g, carry):
-        start = g * group
+        start = 2 * g * group
         wait(start + group)
-        for i in range(group):
-            one(start + i)
-        turn(start + group)
+        compute(start, fresh[0])
+        turn(start + group, fresh[1])
+        wait(start + 2 * group)
+        compute(start + group, fresh[1])
+        turn(start + 2 * group, fresh[0])
         return carry
 
     wait(0)
-    turn(0)
-    lax.fori_loop(0, rest // group - 1, several, 0)
-    for i in range(group):
-        one(rest - group + i)
+    turn(0, fresh[0])
+    lax.fori_loop(0, rest // group // 2 - 1, several, 0)
+    wait(rest - group)
+    compute(rest - 2 * group, fresh[0])
+    turn(rest - group, fresh[1])
+    compute(rest - group, fresh[1])
 
 
 def whole_kernel(cols, table, turned, low, state, *refs):
@@ -456,8 +465,8 @@
             state_type,
             low_type,
             kept((offered, slots, block, block), BF16),
-            (jax.ShapeDtypeStruct((TABLE,), jnp.int32), SMEM),
-            (jax.ShapeDtypeStruct((slots, blocks), jnp.int32), SMEM),
+            (SMEM((TABLE,), jnp.int32), SMEM),
+            (SMEM((slots, blocks), jnp.int32), SMEM),
         ],
         scratch=index_scratch
         + [
@@ -474,6 +483,7 @@
     landing = [
         VMEM((blocks - offered, slots, block, block), BF16),
         pltpu.SemaphoreType.DMA((blocks - offered,)),
+        *[VMEM((2, slots, block, block), BF16)] * 2,
     ]
     scalars = whole([cols, table], SMEM)
     tracer_rows = [in_vmem(inverse), vmax.reshape(1, -1), half_sat.reshape(1, -1)]

time: 101 us -> 92.8 us (0.919)
  Pallas kernels: 45.5 us -> 35.8 us
  waiting for transfers between devices: 20.6 us -> 24 us
  starting transfers between devices: 34.3 us -> 32.6 us
    pallas_call x15, Pallas kernels: 45.5 us -> 35.8 us  [call(): pl.pallas_call(kernel, in_specs=[spec(s) for _, s in args], out_specs=[sp...]
    ppermute x24, waiting for transfers between devices: 12.8 us -> 16.2 us  [exchange(): arrived.append(lax.ppermute(part, 'region', route))]
    ppermute x24, starting transfers between devices: 26.7 us -> 25 us  [exchange(): arrived.append(lax.ppermute(part, 'region', route))]
  transfers between devices with their start and end apart: 30 -> 30, of which waited for: 11 -> 13; matrix products, arithmetic and copies ran while one was open for 0% -> 0% of each run, Pallas kernels for 24% -> 22%
where the time goes in v1:
time: 92.8 us; the launch traced here: 92.7 us
  Pallas kernels  35.8 us (39%)
  starting transfers between devices  32.6 us (35%)
  waiting for transfers between devices  24 us (26%)
    pallas_call x15, Pallas kernels, call(): pl.pallas_call(kernel, in_specs=[spec(s) for _, s in args], out_specs=[sp...  35.8 us
    ppermute x24, starting transfers between devices, exchange(): arrived.append(lax.ppermute(part, 'region', route))  25 us
    ppermute x24, waiting for transfers between devices, exchange(): arrived.append(lax.ppermute(part, 'region', route))  16.2 us
    ppermute x6, waiting for transfers between devices, from_behind(): return lax.ppermute(value, axis, route)  7.8 us
    ppermute x6, starting transfers between devices, from_behind(): return lax.ppermute(value, axis, route)  7.54 us
  transfers between devices with their start and end apart: 30, of which 13 were waited for; matrix products, arithmetic and copies ran while one was open for 0% of the time, Pallas kernels for 22%

profile of v1, /device:TPU:0, one launch (start us, length us, event | category | flops | bytes accessed | tf_op | source)
XLA Modules:
  0.0 92.7 jit_solution(5365299605721050594)
XLA Ops:
  0.0 1.7 %offer_first.1 = (bf16[4,64,128]{2,1,0:T(8,128)(2,1)S(1)}, bf16[4,64,128]{2,1,0:T(8,128)(2,1)S(1)}, bf16[4,64,128]{2,1,0:T(8,128)(2,1)S(1)}, bf16[4,64,128]{2,1,0:T(8,128)(2,1)S(1)}) custom-call(s32[1,8]{1,0:T(1,128)} %export_rows.3, s32[4,4,32]{2,1,0:T(4,128)} %bitcast.10, f32[64,4096]{1,0:T(8,128)} %tracers.3), custom_call_target="tpu_custom_call" | custom-call | bytes 1048576 | tf_op jit(solution)/shard_map/offer_first/pallas_call | solution.py:61
  1.7 6.6 %collective-permute-start = (bf16[4,64,128]{2,1,0:T(8,128)(2,1)S(1)}, bf16[4,64,128]{2,1,0:T(8,128)(2,1)S(1)}, u32[]{:S(2)}, u32[]{:S(2)}) collective-permute-start(bf16[4,64,128]{2,1,0:T(8,128)(2,1)S(1)} %get-tuple-element.57), channel_id=1, source_target_pairs={{0,120},{4,124},{8,16},{12,20},{16,8},{20,12},{24,32},{28,36},{32,... | collective-permute-start | bytes 196616 | tf_op jit(solution)/shard_map/ppermute | solution.py:44
  8.3 0.0 collective-permute-start.1
  8.3 1.2 %collective-permute-start.2 = (bf16[4,64,128]{2,1,0:T(8,128)(2,1)S(1)}, bf16[4,64,128]{2,1,0:T(8,128)(2,1)S(1)}, u32[]{:S(2)}, u32[]{:S(2)}) collective-permute-start(bf16[4,64,128]{2,1,0:T(8,128)(2,1)S(1)} %get-tuple-element.59), channel_id=1, source_target_pairs={{0,8},{4,12},{8,0},{12,4},{16,24},{20,28},{24,16},{28,20},{32,40},... | collective-permute-start | bytes 196616 | tf_op jit(solution)/shard_map/ppermute | solution.py:44
  9.5 0.0 collective-permute-start.3
  9.5 3.4 %prepare.1 = (f32[32,64,128]{2,1,0:T(8,128)S(1)}, bf16[32,64,128]{2,1,0:T(8,128)(2,1)S(1)}, bf16[8,16,128,128]{3,2,1,0:T(8,128)(2,1)S(1)}, s32[136]{0:T(256)S(4)}, s32[16,32]{1,0:T(8,128)S(4)}) custom-call(s32[1,8]{1,0:T(1,128)} %export_rows.3, s32[4,4,32]{2,1,0:T(4,128)} %bitcast.11, s32[32]{0:T(128)} %live.1, s32[16,32]{1,0:T(8,128)} %bitcast.12, ...), custom_call_target="tpu_custom_call" | custom-call | flops 1073741824 | bytes 8388608 | tf_op jit(solution)/shard_map/prepare/pallas_call | solution.py:61
  12.9 0.0 collective-permute-done.refs_0_
  13.0 2.4 %collective-permute-done.1.refs_1_ = bf16[4,64,128]{2,1,0:T(8,128)(2,1)S(1)} collective-permute-done((bf16[4,64,128]{2,1,0:T(8,128)(2,1)S(1)}, bf16[4,64,128]{2,1,0:T(8,128)(2,1)S(1)}, u32[]{:S(2)}, u32[]{:S(2)}) %collective-permute-start.1) | collective-permute-done | bytes 65568 | tf_op jit(solution)/shard_map/ppermute | solution.py:44
  15.4 0.0 collective-permute-done.2.refs_2_
  15.4 0.0 collective-permute-done.3.refs_3_
  15.4 1.0 %export_step.4 = (f32[8,64,128]{2,1,0:T(8,128)S(1)}, bf16[4,64,128]{2,1,0:T(8,128)(2,1)S(1)}, bf16[4,64,128]{2,1,0:T(8,128)(2,1)S(1)}, bf16[4,64,128]{2,1,0:T(8,128)(2,1)S(1)}, bf16[4,64,128]{2,1,0:T(8,128)(2,1)S(1)}) custom-call(s32[16,32]{1,0:T(8,128)S(4)} %get-tuple-element.54.cols, s32[136]{0:T(256)S(4)} %get-tuple-element.53.table, ...), custom_call_target="tpu_custom_call" | custom-call | flops 268435456 | bytes 1048576 | tf_op jit(solution)/shard_map/export_step/pallas_call | solution.py:61
  16.4 2.4 %collective-permute-start.4 = (bf16[4,64,128]{2,1,0:T(8,128)(2,1)S(1)}, bf16[4,64,128]{2,1,0:T(8,128)(2,1)S(1)}, u32[]{:S(2)}, u32[]{:S(2)}) collective-permute-start(bf16[4,64,128]{2,1,0:T(8,128)(2,1)S(1)} %get-tuple-element.66), channel_id=1, source_target_pairs={{0,120},{4,124},{8,16},{12,20},{16,8},{20,12},{24,32},{28,36},{32,... | collective-permute-start | bytes 196616 | tf_op jit(solution)/shard_map/ppermute | solution.py:44
  18.8 0.9 collective-permute-start.5
  19.7 0.0 collective-permute-start.6
  19.7 0.0 collective-permute-start.7
  19.7 7.0 %rest_step.4 = (f32[32,64,128]{2,1,0:T(8,128)S(1)}, bf16[32,64,128]{2,1,0:T(8,128)(2,1)S(1)}, bf16[32,16,128,128]{3,2,1,0:T(8,128)(2,1)S(1)}) custom-call(s32[16,32]{1,0:T(8,128)S(4)} %get-tuple-element.54.cols, s32[136]{0:T(256)S(4)} %get-tuple-element.53.table, bf16[32,16,128,128]{3,2,1,0:T(8,128)(2,1)} %weights.1, ...), custom_call_target="tpu_custom_call" | custom-call | flops 1073741824 | bytes 1048576 | tf_op jit(solution)/shard_map/rest_step/pallas_call | solution.py:61
  26.7 0.0 collective-permute-done.4.refs_0_
  26.7 0.0 collective-permute-done.5.refs_1_
  26.7 0.0 collective-permute-done.6.refs_2_
  26.7 0.0 collective-permute-done.7.refs_3_
  26.7 1.0 %export_step.5 = (f32[8,64,128]{2,1,0:T(8,128)S(1)}, bf16[4,64,128]{2,1,0:T(8,128)(2,1)S(1)}, bf16[4,64,128]{2,1,0:T(8,128)(2,1)S(1)}, bf16[4,64,128]{2,1,0:T(8,128)(2,1)S(1)}, bf16[4,64,128]{2,1,0:T(8,128)(2,1)S(1)}) custom-call(s32[16,32]{1,0:T(8,128)S(4)} %get-tuple-element.54.cols, s32[136]{0:T(256)S(4)} %get-tuple-element.53.table, ...), custom_call_target="tpu_custom_call" | custom-call | flops 268435456 | bytes 1048576 | tf_op jit(solution)/shard_map/export_step/pallas_call | solution.py:61
  27.8 4.6 %collective-permute-start.8 = (bf16[4,64,128]{2,1,0:T(8,128)(2,1)S(1)}, bf16[4,64,128]{2,1,0:T(8,128)(2,1)S(1)}, u32[]{:S(2)}, u32[]{:S(2)}) collective-permute-start(bf16[4,64,128]{2,1,0:T(8,128)(2,1)S(1)} %get-tuple-element.73), channel_id=1, source_target_pairs={{0,120},{4,124},{8,16},{12,20},{16,8},{20,12},{24,32},{28,36},{32,... | collective-permute-start | bytes 196616 | tf_op jit(solution)/shard_map/ppermute | solution.py:44
  32.4 0.7 collective-permute-start.9
  33.0 0.7 collective-permute-start.10
  33.7 0.0 collective-permute-start.11
  33.7 3.0 %rest_step.5 = (f32[32,64,128]{2,1,0:T(8,128)S(1)}, bf16[32,64,128]{2,1,0:T(8,128)(2,1)S(1)}) custom-call(s32[16,32]{1,0:T(8,128)S(4)} %get-tuple-element.54.cols, s32[136]{0:T(256)S(4)} %get-tuple-element.53.table, bf16[32,16,128,128]{3,2,1,0:T(8,128)(2,1)S(1)} %get-tuple-element.63.weights.turned, bf16[32,64,128]{2,1,0:T(8,128)(2,1)S(1)} %get-tuple-element.64.low, ...), custom_call_target="tpu_custom_call" | custom-call | flops 1073741824 | bytes 1048576 | tf_op jit(solution)/shard_map/rest_step/pallas_call | solution.py:61
  36.7 0.0 collective-permute-done.8.refs_0_
  36.7 2.6 %collective-permute-done.9.refs_1_ = bf16[4,64,128]{2,1,0:T(8,128)(2,1)S(1)} collective-permute-done((bf16[4,64,128]{2,1,0:T(8,128)(2,1)S(1)}, bf16[4,64,128]{2,1,0:T(8,128)(2,1)S(1)}, u32[]{:S(2)}, u32[]{:S(2)}) %collective-permute-start.9) | collective-permute-done | bytes 65568 | tf_op jit(solution)/shard_map/ppermute | solution.py:44
  39.4 0.0 collective-permute-done.11.refs_3_
  39.4 3.9 %whole_step.2 = (f32[32,64,128]{2,1,0:T(8,128)S(1)}, f32[32,128]{1,0:T(8,128)S(1)}) custom-call(s32[16,32]{1,0:T(8,128)S(4)} %get-tuple-element.54.cols, s32[136]{0:T(256)S(4)} %get-tuple-element.53.table, bf16[32,16,128,128]{3,2,1,0:T(8,128)(2,1)S(1)} %get-tuple-element.63.weights.turned, bf16[32,64,128]{2,1,0:T(8,128)(2,1)S(1)} %get-tuple-element.71.low, ...), custom_call_target="tpu_custom_call" | custom-call | flops 1073741824 | bytes 1048576 | tf_op jit(solution)/shard_map/whole_step/pallas_call | solution.py:61
  43.3 2.8 %collective-permute-start.14 = (f32[32,128]{1,0:T(8,128)S(1)}, f32[32,128]{1,0:T(8,128)S(1)}, u32[]{:S(2)}, u32[]{:S(2)}) collective-permute-start(f32[32,128]{1,0:T(8,128)S(1)} %get-tuple-element.78.refs_0_), channel_id=1, source_target_pairs={{1,0},{2,1},{3,2},{0,3},{5,4},{6,5},{7,6},{4,7},{9,8},{10,9},{11,1... | collective-permute-start | bytes 49160 | tf_op jit(solution)/shard_map/ppermute | solution.py:27
  46.1 0.8 collective-permute-start.13
  46.9 0.9 collective-permute-start.12
  47.8 0.0 collective-permute-done.14.refs_3_
  47.8 3.6 %collective-permute-done.13.refs_2_ = f32[32,128]{1,0:T(8,128)S(1)} collective-permute-done((f32[32,128]{1,0:T(8,128)S(1)}, f32[32,128]{1,0:T(8,128)S(1)}, u32[]{:S(2)}, u32[]{:S(2)}) %collective-permute-start.13) | collective-permute-done | bytes 16416 | tf_op jit(solution)/shard_map/ppermute | solution.py:27
  51.3 0.5 collective-permute-done.12.refs_1_
  51.9 0.4 export_mix.1
  52.2 1.6 %collective-permute-start.15 = (bf16[4,64,128]{2,1,0:T(8,128)(2,1)S(1)}, bf16[4,64,128]{2,1,0:T(8,128)(2,1)S(1)}, u32[]{:S(2)}, u32[]{:S(2)}) collective-permute-start(bf16[4,64,128]{2,1,0:T(8,128)(2,1)S(1)} %get-tuple-element.81), channel_id=1, source_target_pairs={{0,120},{4,124},{8,16},{12,20},{16,8},{20,12},{24,32},{28,36},{32,... | collective-permute-start | bytes 196616 | tf_op jit(solution)/shard_map/ppermute | solution.py:44
  53.8 0.0 collective-permute-start.18
  53.8 0.9 rest_mix.1
  54.7 5.2 %collective-permute-done.15.refs_0_ = bf16[4,64,128]{2,1,0:T(8,128)(2,1)S(1)} collective-permute-done((bf16[4,64,128]{2,1,0:T(8,128)(2,1)S(1)}, bf16[4,64,128]{2,1,0:T(8,128)(2,1)S(1)}, u32[]{:S(2)}, u32[]{:S(2)}) %collective-permute-start.15) | collective-permute-done | bytes 65568 | tf_op jit(solution)/shard_map/ppermute | solution.py:44
  59.9 0.9 %collective-permute-done.16.refs_1_ = bf16[4,64,128]{2,1,0:T(8,128)(2,1)S(1)} collective-permute-done((bf16[4,64,128]{2,1,0:T(8,128)(2,1)S(1)}, bf16[4,64,128]{2,1,0:T(8,128)(2,1)S(1)}, u32[]{:S(2)}, u32[]{:S(2)}) %collective-permute-start.16) | collective-permute-done | bytes 65568 | tf_op jit(solution)/shard_map/ppermute | solution.py:44
  60.8 1.0 %export_step.6 = (f32[8,64,128]{2,1,0:T(8,128)S(1)}, bf16[4,64,128]{2,1,0:T(8,128)(2,1)S(1)}, bf16[4,64,128]{2,1,0:T(8,128)(2,1)S(1)}, bf16[4,64,128]{2,1,0:T(8,128)(2,1)S(1)}, bf16[4,64,128]{2,1,0:T(8,128)(2,1)S(1)}) custom-call(s32[16,32]{1,0:T(8,128)S(4)} %get-tuple-element.54.cols, s32[136]{0:T(256)S(4)} %get-tuple-element.53.table, ...), custom_call_target="tpu_custom_call" | custom-call | flops 268435456 | bytes 1048576 | tf_op jit(solution)/shard_map/export_step/pallas_call | solution.py:61
  61.9 1.5 %collective-permute-start.19 = (bf16[4,64,128]{2,1,0:T(8,128)(2,1)S(1)}, bf16[4,64,128]{2,1,0:T(8,128)(2,1)S(1)}, u32[]{:S(2)}, u32[]{:S(2)}) collective-permute-start(bf16[4,64,128]{2,1,0:T(8,128)(2,1)S(1)} %get-tuple-element.88), channel_id=1, source_target_pairs={{0,120},{4,124},{8,16},{12,20},{16,8},{20,12},{24,32},{28,36},{32,... | collective-permute-start | bytes 196616 | tf_op jit(solution)/shard_map/ppermute | solution.py:44
  63.4 1.6 %collective-permute-start.21 = (bf16[4,64,128]{2,1,0:T(8,128)(2,1)S(1)}, bf16[4,64,128]{2,1,0:T(8,128)(2,1)S(1)}, u32[]{:S(2)}, u32[]{:S(2)}) collective-permute-start(bf16[4,64,128]{2,1,0:T(8,128)(2,1)S(1)} %get-tuple-element.90), channel_id=1, source_target_pairs={{0,8},{4,12},{8,0},{12,4},{16,24},{20,28},{24,16},{28,20},{32,40},... | collective-permute-start | bytes 196616 | tf_op jit(solution)/shard_map/ppermute | solution.py:44
  65.0 3.0 %rest_step.6 = (f32[32,64,128]{2,1,0:T(8,128)S(1)}, bf16[32,64,128]{2,1,0:T(8,128)(2,1)S(1)}) custom-call(s32[16,32]{1,0:T(8,128)S(4)} %get-tuple-element.54.cols, s32[136]{0:T(256)S(4)} %get-tuple-element.53.table, bf16[32,16,128,128]{3,2,1,0:T(8,128)(2,1)S(1)} %get-tuple-element.63.weights.turned, bf16[32,64,128]{2,1,0:T(8,128)(2,1)S(1)} %get-tuple-element.79.low, ...), custom_call_target="tpu_custom_call" | custom-call | flops 1073741824 | bytes 1048576 | tf_op jit(solution)/shard_map/rest_step/pallas_call | solution.py:61
  68.0 1.5 %collective-permute-done.19.refs_0_ = bf16[4,64,128]{2,1,0:T(8,128)(2,1)S(1)} collective-permute-done((bf16[4,64,128]{2,1,0:T(8,128)(2,1)S(1)}, bf16[4,64,128]{2,1,0:T(8,128)(2,1)S(1)}, u32[]{:S(2)}, u32[]{:S(2)}) %collective-permute-start.19) | collective-permute-done | bytes 65568 | tf_op jit(solution)/shard_map/ppermute | solution.py:44
  69.5 0.9 collective-permute-done.20.refs_1_
  70.4 1.0 %export_step.7 = (f32[8,64,128]{2,1,0:T(8,128)S(1)}, bf16[4,64,128]{2,1,0:T(8,128)(2,1)S(1)}, bf16[4,64,128]{2,1,0:T(8,128)(2,1)S(1)}, bf16[4,64,128]{2,1,0:T(8,128)(2,1)S(1)}, bf16[4,64,128]{2,1,0:T(8,128)(2,1)S(1)}) custom-call(s32[16,32]{1,0:T(8,128)S(4)} %get-tuple-element.54.cols, s32[136]{0:T(256)S(4)} %get-tuple-element.53.table, ...), custom_call_target="tpu_custom_call" | custom-call | flops 268435456 | bytes 1048576 | tf_op jit(solution)/shard_map/export_step/pallas_call | solution.py:61
  71.4 1.9 %collective-permute-start.23 = (bf16[4,64,128]{2,1,0:T(8,128)(2,1)S(1)}, bf16[4,64,128]{2,1,0:T(8,128)(2,1)S(1)}, u32[]{:S(2)}, u32[]{:S(2)}) collective-permute-start(bf16[4,64,128]{2,1,0:T(8,128)(2,1)S(1)} %get-tuple-element.95), channel_id=1, source_target_pairs={{0,120},{4,124},{8,16},{12,20},{16,8},{20,12},{24,32},{28,36},{32,... | collective-permute-start | bytes 196616 | tf_op jit(solution)/shard_map/ppermute | solution.py:44
  73.3 1.0 %collective-permute-start.24 = (bf16[4,64,128]{2,1,0:T(8,128)(2,1)S(1)}, bf16[4,64,128]{2,1,0:T(8,128)(2,1)S(1)}, u32[]{:S(2)}, u32[]{:S(2)}) collective-permute-start(bf16[4,64,128]{2,1,0:T(8,128)(2,1)S(1)} %get-tuple-element.96), channel_id=1, source_target_pairs={{0,124},{4,8},{8,4},{12,16},{16,12},{20,24},{24,20},{28,32},{32,28... | collective-permute-start | bytes 196616 | tf_op jit(solution)/shard_map/ppermute | solution.py:44
  74.3 0.3 collective-permute-start.25
  74.6 0.0 collective-permute-start.26
  74.6 3.0 %rest_step.7 = (f32[32,64,128]{2,1,0:T(8,128)S(1)}, bf16[32,64,128]{2,1,0:T(8,128)(2,1)S(1)}) custom-call(s32[16,32]{1,0:T(8,128)S(4)} %get-tuple-element.54.cols, s32[136]{0:T(256)S(4)} %get-tuple-element.53.table, bf16[32,16,128,128]{3,2,1,0:T(8,128)(2,1)S(1)} %get-tuple-element.63.weights.turned, bf16[32,64,128]{2,1,0:T(8,128)(2,1)S(1)} %get-tuple-element.86.low, ...), custom_call_target="tpu_custom_call" | custom-call | flops 1073741824 | bytes 1048576 | tf_op jit(solution)/shard_map/rest_step/pallas_call | solution.py:61
  77.6 1.5 %collective-permute-done.23.refs_0_ = bf16[4,64,128]{2,1,0:T(8,128)(2,1)S(1)} collective-permute-done((bf16[4,64,128]{2,1,0:T(8,128)(2,1)S(1)}, bf16[4,64,128]{2,1,0:T(8,128)(2,1)S(1)}, u32[]{:S(2)}, u32[]{:S(2)}) %collective-permute-start.23) | collective-permute-done | bytes 65568 | tf_op jit(solution)/shard_map/ppermute | solution.py:44
  79.1 1.2 %collective-permute-done.24.refs_1_ = bf16[4,64,128]{2,1,0:T(8,128)(2,1)S(1)} collective-permute-done((bf16[4,64,128]{2,1,0:T(8,128)(2,1)S(1)}, bf16[4,64,128]{2,1,0:T(8,128)(2,1)S(1)}, u32[]{:S(2)}, u32[]{:S(2)}) %collective-permute-start.24) | collective-permute-done | bytes 65568 | tf_op jit(solution)/shard_map/ppermute | solution.py:44
  80.3 3.9 %whole_step.3 = (f32[32,64,128]{2,1,0:T(8,128)S(1)}, f32[32,128]{1,0:T(8,128)S(1)}) custom-call(s32[16,32]{1,0:T(8,128)S(4)} %get-tuple-element.54.cols, s32[136]{0:T(256)S(4)} %get-tuple-element.53.table, bf16[32,16,128,128]{3,2,1,0:T(8,128)(2,1)S(1)} %get-tuple-element.63.weights.turned, bf16[32,64,128]{2,1,0:T(8,128)(2,1)S(1)} %get-tuple-element.93.low, ...), custom_call_target="tpu_custom_call" | custom-call | flops 1073741824 | bytes 1048576 | tf_op jit(solution)/shard_map/whole_step/pallas_call | solution.py:61
  84.2 0.4 collective-permute-start.29
  84.6 1.4 %collective-permute-start.28 = (f32[32,128]{1,0:T(8,128)S(1)}, f32[32,128]{1,0:T(8,128)S(1)}, u32[]{:S(2)}, u32[]{:S(2)}) collective-permute-start(f32[32,128]{1,0:T(8,128)S(1)} %get-tuple-element.100.refs_0_), channel_id=1, source_target_pairs={{2,0},{3,1},{0,2},{1,3},{6,4},{7,5},{4,6},{5,7},{10,8},{11,9},{8,1... | collective-permute-start | bytes 49160 | tf_op jit(solution)/shard_map/ppermute | solution.py:27
  86.0 1.2 %collective-permute-start.27 = (f32[32,128]{1,0:T(8,128)S(1)}, f32[32,128]{1,0:T(8,128)S(1)}, u32[]{:S(2)}, u32[]{:S(2)}) collective-permute-start(f32[32,128]{1,0:T(8,128)S(1)} %get-tuple-element.100.refs_0_), channel_id=1, source_target_pairs={{3,0},{0,1},{1,2},{2,3},{7,4},{4,5},{5,6},{6,7},{11,8},{8,9},{9,10... | collective-permute-start | bytes 49160 | tf_op jit(solution)/shard_map/ppermute | solution.py:27
  87.2 0.8 collective-permute-done.29.refs_3_
  88.0 1.8 %collective-permute-done.28.refs_2_ = f32[32,128]{1,0:T(8,128)S(1)} collective-permute-done((f32[32,128]{1,0:T(8,128)S(1)}, f32[32,128]{1,0:T(8,128)S(1)}, u32[]{:S(2)}, u32[]{:S(2)}) %collective-permute-start.28) | collective-permute-done | bytes 16416 | tf_op jit(solution)/shard_map/ppermute | solution.py:27
  89.8 1.1 %collective-permute-done.27.refs_1_ = f32[32,128]{1,0:T(8,128)S(1)} collective-permute-done((f32[32,128]{1,0:T(8,128)S(1)}, f32[32,128]{1,0:T(8,128)S(1)}, u32[]{:S(2)}, u32[]{:S(2)}) %collective-permute-start.27) | collective-permute-done | bytes 16416 | tf_op jit(solution)/shard_map/ppermute | solution.py:27
  91.0 1.6 %last_mix.1 = f32[64,4096]{1,0:T(8,128)} custom-call(s32[136]{0:T(256)S(4)} %get-tuple-element.53.table, f32[32,64,128]{2,1,0:T(8,128)S(1)} %get-tuple-element.99.state, bf16[32,128,128]{2,1,0:T(8,128)(2,1)S(1)} %copy-done, f32[1,64]{1,0:T(1,128)S(1)} %bitcast.6, f32[1,64]{1,0:T(1,128)S(1)} %bitcast.9, f32[32,128]{1,0:T(8,128)S(1)} %get-tuple-element.100.refs_0_, ...), custom_call_target="tpu_custom_call" | custom-call | flops 67108864 | bytes 1048576 | tf_op jit(solution)/shard_map/last_mix/pallas_call | solution.py:61
  (17 shorter events, 0.0 us)
Async XLA Ops:
  1.7 11.2 %collective-permute-start = (bf16[4,64,128]{2,1,0:T(8,128)(2,1)S(1)}, bf16[4,64,128]{2,1,0:T(8,128)(2,1)S(1)}, u32[]{:S(2)}, u32[]{:S(2)}) collective-permute-start(bf16[4,64,128]{2,1,0:T(8,128)(2,1)S(1)} %get-tuple-element.57), channel_id=1, source_target_pairs={{0,120},{4,124},{8,16},{12,20},{16,8},{20,12},{24,32},{28,36},{32,... | collective-permute-start | bytes 196616 | tf_op jit(solution)/shard_map/ppermute | solution.py:44
  8.3 7.0 %collective-permute-start.1 = (bf16[4,64,128]{2,1,0:T(8,128)(2,1)S(1)}, bf16[4,64,128]{2,1,0:T(8,128)(2,1)S(1)}, u32[]{:S(2)}, u32[]{:S(2)}) collective-permute-start(bf16[4,64,128]{2,1,0:T(8,128)(2,1)S(1)} %get-tuple-element.58), channel_id=1, source_target_pairs={{0,124},{4,8},{8,4},{12,16},{16,12},{20,24},{24,20},{28,32},{32,28... | collective-permute-start | bytes 196616 | tf_op jit(solution)/shard_map/ppermute | solution.py:44
  8.3 7.0 %collective-permute-start.2 = (bf16[4,64,128]{2,1,0:T(8,128)(2,1)S(1)}, bf16[4,64,128]{2,1,0:T(8,128)(2,1)S(1)}, u32[]{:S(2)}, u32[]{:S(2)}) collective-permute-start(bf16[4,64,128]{2,1,0:T(8,128)(2,1)S(1)} %get-tuple-element.59), channel_id=1, source_target_pairs={{0,8},{4,12},{8,0},{12,4},{16,24},{20,28},{24,16},{28,20},{32,40},... | collective-permute-start | bytes 196616 | tf_op jit(solution)/shard_map/ppermute | solution.py:44
  9.5 5.8 %collective-permute-start.3 = (bf16[4,64,128]{2,1,0:T(8,128)(2,1)S(1)}, bf16[4,64,128]{2,1,0:T(8,128)(2,1)S(1)}, u32[]{:S(2)}, u32[]{:S(2)}) collective-permute-start(bf16[4,64,128]{2,1,0:T(8,128)(2,1)S(1)} %get-tuple-element.60), channel_id=1, source_target_pairs={{0,4},{4,0},{8,12},{12,8},{16,20},{20,16},{24,28},{28,24},{32,36},... | collective-permute-start | bytes 196616 | tf_op jit(solution)/shard_map/ppermute | solution.py:44
  16.4 10.3 %collective-permute-start.4 = (bf16[4,64,128]{2,1,0:T(8,128)(2,1)S(1)}, bf16[4,64,128]{2,1,0:T(8,128)(2,1)S(1)}, u32[]{:S(2)}, u32[]{:S(2)}) collective-permute-start(bf16[4,64,128]{2,1,0:T(8,128)(2,1)S(1)} %get-tuple-element.66), channel_id=1, source_target_pairs={{0,120},{4,124},{8,16},{12,20},{16,8},{20,12},{24,32},{28,36},{32,... | collective-permute-start | bytes 196616 | tf_op jit(solution)/shard_map/ppermute | solution.py:44
  18.8 7.9 %collective-permute-start.5 = (bf16[4,64,128]{2,1,0:T(8,128)(2,1)S(1)}, bf16[4,64,128]{2,1,0:T(8,128)(2,1)S(1)}, u32[]{:S(2)}, u32[]{:S(2)}) collective-permute-start(bf16[4,64,128]{2,1,0:T(8,128)(2,1)S(1)} %get-tuple-element.67), channel_id=1, source_target_pairs={{0,124},{4,8},{8,4},{12,16},{16,12},{20,24},{24,20},{28,32},{32,28... | collective-permute-start | bytes 196616 | tf_op jit(solution)/shard_map/ppermute | solution.py:44
  19.7 7.0 %collective-permute-start.6 = (bf16[4,64,128]{2,1,0:T(8,128)(2,1)S(1)}, bf16[4,64,128]{2,1,0:T(8,128)(2,1)S(1)}, u32[]{:S(2)}, u32[]{:S(2)}) collective-permute-start(bf16[4,64,128]{2,1,0:T(8,128)(2,1)S(1)} %get-tuple-element.68), channel_id=1, source_target_pairs={{0,8},{4,12},{8,0},{12,4},{16,24},{20,28},{24,16},{28,20},{32,40},... | collective-permute-start | bytes 196616 | tf_op jit(solution)/shard_map/ppermute | solution.py:44
  19.7 7.0 %collective-permute-start.7 = (bf16[4,64,128]{2,1,0:T(8,128)(2,1)S(1)}, bf16[4,64,128]{2,1,0:T(8,128)(2,1)S(1)}, u32[]{:S(2)}, u32[]{:S(2)}) collective-permute-start(bf16[4,64,128]{2,1,0:T(8,128)(2,1)S(1)} %get-tuple-element.69), channel_id=1, source_target_pairs={{0,4},{4,0},{8,12},{12,8},{16,20},{20,16},{24,28},{28,24},{32,36},... | collective-permute-start | bytes 196616 | tf_op jit(solution)/shard_map/ppermute | solution.py:44
  27.8 9.0 %collective-permute-start.8 = (bf16[4,64,128]{2,1,0:T(8,128)(2,1)S(1)}, bf16[4,64,128]{2,1,0:T(8,128)(2,1)S(1)}, u32[]{:S(2)}, u32[]{:S(2)}) collective-permute-start(bf16[4,64,128]{2,1,0:T(8,128)(2,1)S(1)} %get-tuple-element.73), channel_id=1, source_target_pairs={{0,120},{4,124},{8,16},{12,20},{16,8},{20,12},{24,32},{28,36},{32,... | collective-permute-start | bytes 196616 | tf_op jit(solution)/shard_map/ppermute | solution.py:44
  32.4 7.0 %collective-permute-start.9 = (bf16[4,64,128]{2,1,0:T(8,128)(2,1)S(1)}, bf16[4,64,128]{2,1,0:T(8,128)(2,1)S(1)}, u32[]{:S(2)}, u32[]{:S(2)}) collective-permute-start(bf16[4,64,128]{2,1,0:T(8,128)(2,1)S(1)} %get-tuple-element.74), channel_id=1, source_target_pairs={{0,124},{4,8},{8,4},{12,16},{16,12},{20,24},{24,20},{28,32},{32,28... | collective-permute-start | bytes 196616 | tf_op jit(solution)/shard_map/ppermute | solution.py:44
  33.0 6.4 %collective-permute-start.10 = (bf16[4,64,128]{2,1,0:T(8,128)(2,1)S(1)}, bf16[4,64,128]{2,1,0:T(8,128)(2,1)S(1)}, u32[]{:S(2)}, u32[]{:S(2)}) collective-permute-start(bf16[4,64,128]{2,1,0:T(8,128)(2,1)S(1)} %get-tuple-element.75), channel_id=1, source_target_pairs={{0,8},{4,12},{8,0},{12,4},{16,24},{20,28},{24,16},{28,20},{32,40},... | collective-permute-start | bytes 196616 | tf_op jit(solution)/shard_map/ppermute | solution.py:44
  33.7 5.7 %collective-permute-start.11 = (bf16[4,64,128]{2,1,0:T(8,128)(2,1)S(1)}, bf16[4,64,128]{2,1,0:T(8,128)(2,1)S(1)}, u32[]{:S(2)}, u32[]{:S(2)}) collective-permute-start(bf16[4,64,128]{2,1,0:T(8,128)(2,1)S(1)} %get-tuple-element.76), channel_id=1, source_target_pairs={{0,4},{4,0},{8,12},{12,8},{16,20},{20,16},{24,28},{28,24},{32,36},... | collective-permute-start | bytes 196616 | tf_op jit(solution)/shard_map/ppermute | solution.py:44
  33.7 18.1 %copy-start = (bf16[32,128,128]{2,1,0:T(8,128)(2,1)S(1)}, bf16[32,128,128]{2,1,0:T(8,128)(2,1)}, u32[]{:S(2)}) copy-start(bf16[32,128,128]{2,1,0:T(8,128)(2,1)} %inverse.5) | copy-start | bytes 3145732
  33.7 18.1 %copy-start.1 = (f32[64]{0:T(128)S(1)}, f32[64]{0:T(128)}, u32[]{:S(2)}) copy-start(f32[64]{0:T(128)} %param.16) | copy-start | bytes 772
  33.7 18.1 %copy-start.2 = (f32[64]{0:T(128)S(1)}, f32[64]{0:T(128)}, u32[]{:S(2)}) copy-start(f32[64]{0:T(128)} %param.17) | copy-start | bytes 772
  43.3 4.5 %collective-permute-start.14 = (f32[32,128]{1,0:T(8,128)S(1)}, f32[32,128]{1,0:T(8,128)S(1)}, u32[]{:S(2)}, u32[]{:S(2)}) collective-permute-start(f32[32,128]{1,0:T(8,128)S(1)} %get-tuple-element.78.refs_0_), channel_id=1, source_target_pairs={{1,0},{2,1},{3,2},{0,3},{5,4},{6,5},{7,6},{4,7},{9,8},{10,9},{11,1... | collective-permute-start | bytes 49160 | tf_op jit(solution)/shard_map/ppermute | solution.py:27
  46.1 5.2 %collective-permute-start.13 = (f32[32,128]{1,0:T(8,128)S(1)}, f32[32,128]{1,0:T(8,128)S(1)}, u32[]{:S(2)}, u32[]{:S(2)}) collective-permute-start(f32[32,128]{1,0:T(8,128)S(1)} %get-tuple-element.78.refs_0_), channel_id=1, source_target_pairs={{2,0},{3,1},{0,2},{1,3},{6,4},{7,5},{4,6},{5,7},{10,8},{11,9},{8,1... | collective-permute-start | bytes 49160 | tf_op jit(solution)/shard_map/ppermute | solution.py:27
  46.9 5.0 %collective-permute-start.12 = (f32[32,128]{1,0:T(8,128)S(1)}, f32[32,128]{1,0:T(8,128)S(1)}, u32[]{:S(2)}, u32[]{:S(2)}) collective-permute-start(f32[32,128]{1,0:T(8,128)S(1)} %get-tuple-element.78.refs_0_), channel_id=1, source_target_pairs={{3,0},{0,1},{1,2},{2,3},{7,4},{4,5},{5,6},{6,7},{11,8},{8,9},{9,10... | collective-permute-start | bytes 49160 | tf_op jit(solution)/shard_map/ppermute | solution.py:27
  52.2 7.7 %collective-permute-start.15 = (bf16[4,64,128]{2,1,0:T(8,128)(2,1)S(1)}, bf16[4,64,128]{2,1,0:T(8,128)(2,1)S(1)}, u32[]{:S(2)}, u32[]{:S(2)}) collective-permute-start(bf16[4,64,128]{2,1,0:T(8,128)(2,1)S(1)} %get-tuple-element.81), channel_id=1, source_target_pairs={{0,120},{4,124},{8,16},{12,20},{16,8},{20,12},{24,32},{28,36},{32,... | collective-permute-start | bytes 196616 | tf_op jit(solution)/shard_map/ppermute | solution.py:44
  53.8 7.0 %collective-permute-start.16 = (bf16[4,64,128]{2,1,0:T(8,128)(2,1)S(1)}, bf16[4,64,128]{2,1,0:T(8,128)(2,1)S(1)}, u32[]{:S(2)}, u32[]{:S(2)}) collective-permute-start(bf16[4,64,128]{2,1,0:T(8,128)(2,1)S(1)} %get-tuple-element.82), channel_id=1, source_target_pairs={{0,124},{4,8},{8,4},{12,16},{16,12},{20,24},{24,20},{28,32},{32,28... | collective-permute-start | bytes 196616 | tf_op jit(solution)/shard_map/ppermute | solution.py:44
  53.8 7.0 %collective-permute-start.17 = (bf16[4,64,128]{2,1,0:T(8,128)(2,1)S(1)}, bf16[4,64,128]{2,1,0:T(8,128)(2,1)S(1)}, u32[]{:S(2)}, u32[]{:S(2)}) collective-permute-start(bf16[4,64,128]{2,1,0:T(8,128)(2,1)S(1)} %get-tuple-element.83), channel_id=1, source_target_pairs={{0,8},{4,12},{8,0},{12,4},{16,24},{20,28},{24,16},{28,20},{32,40},... | collective-permute-start | bytes 196616 | tf_op jit(solution)/shard_map/ppermute | solution.py:44
  53.8 7.0 %collective-permute-start.18 = (bf16[4,64,128]{2,1,0:T(8,128)(2,1)S(1)}, bf16[4,64,128]{2,1,0:T(8,128)(2,1)S(1)}, u32[]{:S(2)}, u32[]{:S(2)}) collective-permute-start(bf16[4,64,128]{2,1,0:T(8,128)(2,1)S(1)} %get-tuple-element.84), channel_id=1, source_target_pairs={{0,4},{4,0},{8,12},{12,8},{16,20},{20,16},{24,28},{28,24},{32,36},... | collective-permute-start | bytes 196616 | tf_op jit(solution)/shard_map/ppermute | solution.py:44
  61.9 7.7 %collective-permute-start.19 = (bf16[4,64,128]{2,1,0:T(8,128)(2,1)S(1)}, bf16[4,64,128]{2,1,0:T(8,128)(2,1)S(1)}, u32[]{:S(2)}, u32[]{:S(2)}) collective-permute-start(bf16[4,64,128]{2,1,0:T(8,128)(2,1)S(1)} %get-tuple-element.88), channel_id=1, source_target_pairs={{0,120},{4,124},{8,16},{12,20},{16,8},{20,12},{24,32},{28,36},{32,... | collective-permute-start | bytes 196616 | tf_op jit(solution)/shard_map/ppermute | solution.py:44
  63.4 7.0 %collective-permute-start.20 = (bf16[4,64,128]{2,1,0:T(8,128)(2,1)S(1)}, bf16[4,64,128]{2,1,0:T(8,128)(2,1)S(1)}, u32[]{:S(2)}, u32[]{:S(2)}) collective-permute-start(bf16[4,64,128]{2,1,0:T(8,128)(2,1)S(1)} %get-tuple-element.89), channel_id=1, source_target_pairs={{0,124},{4,8},{8,4},{12,16},{16,12},{20,24},{24,20},{28,32},{32,28... | collective-permute-start | bytes 196616 | tf_op jit(solution)/shard_map/ppermute | solution.py:44
  63.4 7.0 %collective-permute-start.21 = (bf16[4,64,128]{2,1,0:T(8,128)(2,1)S(1)}, bf16[4,64,128]{2,1,0:T(8,128)(2,1)S(1)}, u32[]{:S(2)}, u32[]{:S(2)}) collective-permute-start(bf16[4,64,128]{2,1,0:T(8,128)(2,1)S(1)} %get-tuple-element.90), channel_id=1, source_target_pairs={{0,8},{4,12},{8,0},{12,4},{16,24},{20,28},{24,16},{28,20},{32,40},... | collective-permute-start | bytes 196616 | tf_op jit(solution)/shard_map/ppermute | solution.py:44
  65.0 5.4 %collective-permute-start.22 = (bf16[4,64,128]{2,1,0:T(8,128)(2,1)S(1)}, bf16[4,64,128]{2,1,0:T(8,128)(2,1)S(1)}, u32[]{:S(2)}, u32[]{:S(2)}) collective-permute-start(bf16[4,64,128]{2,1,0:T(8,128)(2,1)S(1)} %get-tuple-element.91), channel_id=1, source_target_pairs={{0,4},{4,0},{8,12},{12,8},{16,20},{20,16},{24,28},{28,24},{32,36},... | collective-permute-start | bytes 196616 | tf_op jit(solution)/shard_map/ppermute | solution.py:44
  71.4 7.7 %collective-permute-start.23 = (bf16[4,64,128]{2,1,0:T(8,128)(2,1)S(1)}, bf16[4,64,128]{2,1,0:T(8,128)(2,1)S(1)}, u32[]{:S(2)}, u32[]{:S(2)}) collective-permute-start(bf16[4,64,128]{2,1,0:T(8,128)(2,1)S(1)} %get-tuple-element.95), channel_id=1, source_target_pairs={{0,120},{4,124},{8,16},{12,20},{16,8},{20,12},{24,32},{28,36},{32,... | collective-permute-start | bytes 196616 | tf_op jit(solution)/shard_map/ppermute | solution.py:44
  73.3 7.0 %collective-permute-start.24 = (bf16[4,64,128]{2,1,0:T(8,128)(2,1)S(1)}, bf16[4,64,128]{2,1,0:T(8,128)(2,1)S(1)}, u32[]{:S(2)}, u32[]{:S(2)}) collective-permute-start(bf16[4,64,128]{2,1,0:T(8,128)(2,1)S(1)} %get-tuple-element.96), channel_id=1, source_target_pairs={{0,124},{4,8},{8,4},{12,16},{16,12},{20,24},{24,20},{28,32},{32,28... | collective-permute-start | bytes 196616 | tf_op jit(solution)/shard_map/ppermute | solution.py:44
  74.3 6.0 %collective-permute-start.25 = (bf16[4,64,128]{2,1,0:T(8,128)(2,1)S(1)}, bf16[4,64,128]{2,1,0:T(8,128)(2,1)S(1)}, u32[]{:S(2)}, u32[]{:S(2)}) collective-permute-start(bf16[4,64,128]{2,1,0:T(8,128)(2,1)S(1)} %get-tuple-element.97), channel_id=1, source_target_pairs={{0,8},{4,12},{8,0},{12,4},{16,24},{20,28},{24,16},{28,20},{32,40},... | collective-permute-start | bytes 196616 | tf_op jit(solution)/shard_map/ppermute | solution.py:44
  74.6 5.7 %collective-permute-start.26 = (bf16[4,64,128]{2,1,0:T(8,128)(2,1)S(1)}, bf16[4,64,128]{2,1,0:T(8,128)(2,1)S(1)}, u32[]{:S(2)}, u32[]{:S(2)}) collective-permute-start(bf16[4,64,128]{2,1,0:T(8,128)(2,1)S(1)} %get-tuple-element.98), channel_id=1, source_target_pairs={{0,4},{4,0},{8,12},{12,8},{16,20},{20,16},{24,28},{28,24},{32,36},... | collective-permute-start | bytes 196616 | tf_op jit(solution)/shard_map/ppermute | solution.py:44
  84.2 3.8 %collective-permute-start.29 = (f32[32,128]{1,0:T(8,128)S(1)}, f32[32,128]{1,0:T(8,128)S(1)}, u32[]{:S(2)}, u32[]{:S(2)}) collective-permute-start(f32[32,128]{1,0:T(8,128)S(1)} %get-tuple-element.100.refs_0_), channel_id=1, source_target_pairs={{1,0},{2,1},{3,2},{0,3},{5,4},{6,5},{7,6},{4,7},{9,8},{10,9},{11,1... | collective-permute-start | bytes 49160 | tf_op jit(solution)/shard_map/ppermute | solution.py:27
  84.6 5.2 %collective-permute-start.28 = (f32[32,128]{1,0:T(8,128)S(1)}, f32[32,128]{1,0:T(8,128)S(1)}, u32[]{:S(2)}, u32[]{:S(2)}) collective-permute-start(f32[32,128]{1,0:T(8,128)S(1)} %get-tuple-element.100.refs_0_), channel_id=1, source_target_pairs={{2,0},{3,1},{0,2},{1,3},{6,4},{7,5},{4,6},{5,7},{10,8},{11,9},{8,1... | collective-permute-start | bytes 49160 | tf_op jit(solution)/shard_map/ppermute | solution.py:27
  86.0 4.9 %collective-permute-start.27 = (f32[32,128]{1,0:T(8,128)S(1)}, f32[32,128]{1,0:T(8,128)S(1)}, u32[]{:S(2)}, u32[]{:S(2)}) collective-permute-start(f32[32,128]{1,0:T(8,128)S(1)} %get-tuple-element.100.refs_0_), channel_id=1, source_target_pairs={{3,0},{0,1},{1,2},{2,3},{7,4},{4,5},{5,6},{6,7},{11,8},{8,9},{9,10... | collective-permute-start | bytes 49160 | tf_op jit(solution)/shard_map/ppermute | solution.py:27

commit v2 on v1

--- a/solution.py
+++ b/solution.py
@@ -13,7 +13,7 @@
 CYCLES = 2
 OFFSETS = (-2, -1, 1, 2)
 
-EXPORTS, SENDS, LINKS, REST, LIVE, SPARE, TABLE = 0, 16, 48, 64, 100, 120, 136
+EXPORTS, SENDS, LINKS, REST, LIVE, COUNT, SPARE, TABLE = 0, 16, 48, 64, 100, 101, 120, 136
 
 VMEM = pltpu.VMEM
 SMEM = pltpu.SMEM
@@ -29,7 +29,7 @@
 
 def link_neighbour(link, region):
     chip, core = region // 2 % 2, region % 2
-    return (3 * chip, 1 + core, 3 - 3 * chip, 2 - core)[link]
+    return (3 * chip, 3 - 3 * chip, 1 + core, 2 - core)[link]
 
 
 def offset_of(which):
@@ -105,19 +105,14 @@
 
 def first_kernel(block, export_rows, send_pos, tracers, *refs):
     near, reach = send_pos.shape[:2]
-    sends, (exports, positions, landed, sems, block_sems) = refs[:near], refs[near:]
-    small = fetch([(export_rows, exports), (send_pos, positions)], sems)
-    small[0].wait()
-    copies = []
-    for e in range(exports.shape[1]):
-        start = pl.multiple_of(exports[0, e] * block, block)
-        copies.append((tracers.at[:, pl.ds(start, block)], landed.at[e]))
-    copies = fetch(copies, block_sems)
-    for copy in small[1:] + copies:
+    sends, (exports, positions, landed, sems) = refs[:near], refs[near:]
+    for copy in fetch([(tracers, landed), (export_rows, exports), (send_pos, positions)], sems):
         copy.wait()
     for link in range(near):
         for k in range(reach):
-            sends[link][k] = landed[read_position(positions, link, k)].astype(BF16)
+            row = exports[0, read_position(positions, link, k)]
+            columns = pl.ds(pl.multiple_of(row * block, block), block)
+            sends[link][k] = landed[:, columns].astype(BF16)
 
 
 def write_table(table, exports, positions, lives, blocks):
@@ -141,8 +136,10 @@
         table[LINKS + link] = link_neighbour(link, lax.axis_index("region"))
         for k in range(reach):
             table[SENDS + link * reach + k] = table[SPARE + read_position(positions, link, k)]
-    table[LIVE] = lives[lax.axis_index("region")]
+    wet = lives[lax.axis_index("region")]
+    table[LIVE] = wet
     n = jnp.int32(0)
+    count = jnp.int32(0)
     for b in range(blocks):
         hit = exported[0] == b
         for row in exported[1:]:
@@ -150,12 +147,15 @@
         fills = EXPORTS + table[places + jnp.minimum(n, offered - 1)]
         place = jnp.where(n < free, fills, REST + n - free)
         table[jnp.where(hit, TABLE - 1, place)] = jnp.int32(b)
+        listed = jnp.logical_and(jnp.logical_not(hit), n >= free)
+        count = count + jnp.where(jnp.logical_and(listed, b < wet), 1, 0)
         n = n + jnp.where(hit, 0, 1)
+    table[COUNT] = count
 
 
 def prepare_kernel(
-    export_rows,
-    send_pos,
+    exports,
+    positions,
     live,
     col_slot,
     tracers,
@@ -165,8 +165,6 @@
     early,
     table,
     cols,
-    exports,
-    positions,
     lives,
     landed,
     landed_rows,
@@ -175,17 +173,7 @@
 ):
     blocks, slots, block, _ = transport.shape
     offered = exports.shape[1]
-    small = fetch(
-        [
-            (export_rows, exports),
-            (send_pos, positions),
-            (live, lives),
-            (col_slot, cols),
-            (tracers, landed),
-        ],
-        sems,
-    )
-    small[0].wait()
+    small = fetch([(live, lives), (col_slot, cols), (tracers, landed)], sems)
     exported = [exports[0, e] for e in range(offered)]
     again = []
     for e in range(offered):
@@ -203,8 +191,7 @@
         def _():
             rows_copy(e, exported[e]).start()
 
-    for copy in small[1:3]:
-        copy.wait()
+    small[0].wait()
     write_table(table, exports, positions, lives, blocks)
     for e in range(offered):
 
@@ -212,7 +199,7 @@
         def _():
             rows_copy(e, table[EXPORTS + e]).start()
 
-    for copy in small[3:]:
+    for copy in small[1:]:
         copy.wait()
     for b in range(blocks):
         value = landed[:, b * block : (b + 1) * block]
@@ -242,13 +229,27 @@
     return rows[...].reshape(slots * block, block)
 
 
-def in_groups(count, group, one):
-    def several(i, carry):
-        for u in range(group):
-            one(i * group + u)
+def for_rest(table, rest, one, dry):
+    def group_of(size, start):
+        def several(i, carry):
+            for u in range(size):
+                one(start + i * size + u)
+            return carry
+
+        return several
+
+    count = table[COUNT]
+    left = lax.rem(count, 8)
+    eights = lax.div(count, 8) + jnp.where(left > 4, 1, 0)
+    fours = jnp.where(jnp.logical_and(left > 0, left <= 4), 1, 0)
+    lax.fori_loop(0, eights, group_of(8, 0), 0)
+    lax.fori_loop(0, fours, group_of(4, 8 * eights), 0)
+
+    def dry_one(i, carry):
+        dry(i)
         return carry
 
-    lax.fori_loop(0, count // group, several, 0)
+    lax.fori_loop(8 * eights + 4 * fours, rest, dry_one, 0)
 
 
 def tracer_weights(width):
@@ -281,13 +282,18 @@
     offered = exported.shape[0]
     rest = state.shape[0] - offered
     if first:
-        early, new_state, new_low, turned, ext, landed, sems, *fresh = refs
+        new_state, new_low, turned, ext, landed, sems, *fresh = refs
 
         def chunk(i):
             return pltpu.make_async_copy(weights.at[table[REST + i]], landed.at[i], sems.at[i])
 
-        for i in range(rest):
+        quads = jnp.maximum(lax.div(table[COUNT] + 3, 4), 1)
+
+        def begin(i, carry):
             chunk(i).start()
+            return carry
+
+        lax.fori_loop(0, 4 * quads, begin, 0)
     else:
         new_state, new_low, ext = refs
     fill(ext, low, halo, table)
@@ -298,26 +304,26 @@
 
     for e in range(offered):
         put(table[EXPORTS + e], exported[e])
-        if first:
-            turned[table[EXPORTS + e]] = early[e]
 
     def one(i, rows):
         b = table[REST + i]
         value = state[b] + flux_of(b, cols, rows, ext)
         put(b, row_mask(b, table[LIVE], value.shape) * value)
 
+    def dry(i):
+        put(table[REST + i], jnp.zeros(state.shape[1:], F32))
+
     if not first:
-        in_groups(rest, 8, lambda i: one(i, stacked(weights.at[table[REST + i]])))
+        for_rest(table, rest, lambda i: one(i, stacked(weights.at[i])), dry)
         return
 
     group = fresh[0].shape[0]
 
     def turn(start, there):
         for i in range(group):
-            b = table[REST + start + i]
             for s in range(landed.shape[1]):
                 tile = landed[start + i, s].T
-                turned[b, s] = tile
+                turned[start + i, s] = tile
                 there[i, s] = tile
 
     def wait(start):
@@ -331,35 +337,50 @@
     def several(g, carry):
         start = 2 * g * group
         wait(start + group)
+        wait(start + 2 * group)
         compute(start, fresh[0])
         turn(start + group, fresh[1])
-        wait(start + 2 * group)
         compute(start + group, fresh[1])
         turn(start + 2 * group, fresh[0])
         return carry
 
     wait(0)
     turn(0, fresh[0])
-    lax.fori_loop(0, rest // group // 2 - 1, several, 0)
-    wait(rest - group)
-    compute(rest - 2 * group, fresh[0])
-    turn(rest - group, fresh[1])
-    compute(rest - group, fresh[1])
-
-
-def whole_kernel(cols, table, turned, low, state, *refs):
+    lax.fori_loop(0, quads - 1, several, 0)
+    last = 2 * group * (quads - 1)
+    wait(last + group)
+    compute(last, fresh[0])
+    turn(last + group, fresh[1])
+    compute(last + group, fresh[1])
+
+    def dry_one(i, carry):
+        dry(i)
+        return carry
+
+    lax.fori_loop(2 * group * quads, rest, dry_one, 0)
+
+
+def whole_kernel(cols, table, early, turned, low, state, *refs):
     near = len(OFFSETS)
     halo, (new_state, part, ext) = refs[:near], refs[near:]
     fill(ext, low, halo, table)
     weights = tracer_weights(state.shape[1])
 
-    def one(b):
-        value = state[b] + flux_of(b, cols, stacked(turned.at[b]), ext)
+    def one(b, rows):
+        value = state[b] + flux_of(b, cols, rows, ext)
         value = row_mask(b, table[LIVE], value.shape) * value
         new_state[b] = value
         part[pl.ds(b, 1), :] = shade_part(value, weights)
 
-    in_groups(state.shape[0], 8, one)
+    for e in range(early.shape[0]):
+        one(table[EXPORTS + e], stacked(early.at[e]))
+
+    def dry(i):
+        b = table[REST + i]
+        new_state[b] = jnp.zeros(state.shape[1:], F32)
+        part[pl.ds(b, 1), :] = jnp.zeros((1, part.shape[1]), F32)
+
+    for_rest(table, turned.shape[0], lambda i: one(table[REST + i], stacked(turned.at[i])), dry)
 
 
 def column_of(row):
@@ -437,30 +458,24 @@
         return [part] + [from_behind(part, "tracer", d) for d in range(1, peers)]
 
     tracers, transport = in_hbm(tracers), in_hbm(transport)
-    indices = [in_hbm(export_rows), in_hbm(send_pos.transpose(1, 2, 0))]
     regions = send_pos.shape[0]
-    index_scratch = [
-        SMEM((1, offered), jnp.int32),
-        SMEM((near, reach, regions), jnp.int32),
-    ]
-    halo = exchange(
-        call(
-            functools.partial(first_kernel, block),
-            "offer_first",
-            whole([*indices, tracers], pl.ANY),
-            sends,
-            scratch=index_scratch
-            + [
-                VMEM((offered, width, block), F32),
-                pltpu.SemaphoreType.DMA((2,)),
-                pltpu.SemaphoreType.DMA((offered,)),
-            ],
-        )
+    *parts, exports, positions = call(
+        functools.partial(first_kernel, block),
+        "offer_first",
+        whole([in_hbm(export_rows), in_hbm(send_pos.transpose(1, 2, 0)), tracers], pl.ANY),
+        sends
+        + [
+            (SMEM((1, offered), jnp.int32), SMEM),
+            (SMEM((near, reach, regions), jnp.int32), SMEM),
+        ],
+        scratch=[VMEM((width, rows), F32), pltpu.SemaphoreType.DMA((3,))],
     )
+    halo = exchange(parts)
     state, low, early, table, cols = call(
         prepare_kernel,
         "prepare",
-        whole([*indices, in_hbm(live_blocks), in_hbm(col_slot.T), tracers, transport], pl.ANY),
+        whole([exports, positions], SMEM)
+        + whole([in_hbm(live_blocks), in_hbm(col_slot.T), tracers, transport], pl.ANY),
         [
             state_type,
             low_type,
@@ -468,12 +483,11 @@
             (SMEM((TABLE,), jnp.int32), SMEM),
             (SMEM((slots, blocks), jnp.int32), SMEM),
         ],
-        scratch=index_scratch
-        + [
+        scratch=[
             SMEM((regions,), jnp.int32),
             VMEM((width, rows), F32),
             VMEM((offered, slots, block, block), BF16),
-            pltpu.SemaphoreType.DMA((5,)),
+            pltpu.SemaphoreType.DMA((3,)),
             pltpu.SemaphoreType.DMA((offered,)),
         ],
         flops=row_flops * blocks,
@@ -504,8 +518,9 @@
                 "rest_step",
                 scalars
                 + [(transport, pl.ANY) if first else (turned, VMEM)]
-                + whole([low, state, *halo, exported] + ([early] if first else [])),
-                [state_type, low_type] + ([kept(transport.shape, BF16)] if first else []),
+                + whole([low, state, *halo, exported]),
+                [state_type, low_type]
+                + ([kept((blocks - offered, *transport.shape[1:]), BF16)] if first else []),
                 scratch=[ext] + (landing if first else []),
                 flops=row_flops * blocks,
             )
@@ -515,7 +530,7 @@
         state, part = call(
             whole_kernel,
             "whole_step",
-            scalars + whole([turned, low, state, *halo]),
+            scalars + whole([early, turned, low, state, *halo]),
             [state_type, sent((blocks, block), F32)],
             scratch=[ext],
             flops=row_flops * blocks,

time: 92.8 us -> 92 us (level)
  waiting for transfers between devices: 24 us -> 18.4 us
  starting transfers between devices: 32.6 us -> 37.2 us
    ppermute x24, waiting for transfers between devices: 16.2 us -> 10.6 us  [exchange(): arrived.append(lax.ppermute(part, 'region', route))]
    ppermute x24, starting transfers between devices: 25 us -> 29.7 us  [exchange(): arrived.append(lax.ppermute(part, 'region', route))]
where the time goes in v2:
time: 92 us; the launch traced here: 91.8 us
  starting transfers between devices  37.2 us (40%)
  Pallas kernels  35.7 us (39%)
  waiting for transfers between devices  18.4 us (20%)
    pallas_call x15, Pallas kernels, call(): pl.pallas_call(kernel, in_specs=[spec(s) for _, s in args], out_specs=[sp...  35.7 us
    ppermute x24, starting transfers between devices, exchange(): arrived.append(lax.ppermute(part, 'region', route))  29.7 us
    ppermute x24, waiting for transfers between devices, exchange(): arrived.append(lax.ppermute(part, 'region', route))  10.6 us
    ppermute x6, waiting for transfers between devices, from_behind(): return lax.ppermute(value, axis, route)  7.84 us
    ppermute x6, starting transfers between devices, from_behind(): return lax.ppermute(value, axis, route)  7.5 us
  transfers between devices with their start and end apart: 30, of which 13 were waited for; matrix products, arithmetic and copies ran while one was open for 0% of the time, Pallas kernels for 22%

profile of v2, /device:TPU:0, one launch (start us, length us, event | category | flops | bytes accessed | tf_op | source)
XLA Modules:
  0.0 91.8 jit_solution(12996031335107676474)
XLA Ops:
  0.0 1.4 %offer_first.1 = (bf16[4,64,128]{2,1,0:T(8,128)(2,1)S(1)}, bf16[4,64,128]{2,1,0:T(8,128)(2,1)S(1)}, bf16[4,64,128]{2,1,0:T(8,128)(2,1)S(1)}, bf16[4,64,128]{2,1,...) custom-call(s32[1,8]{1,0:T(1,128)} %export_rows.1, s32[4,4,32]{2,1,0:T(4,128)} %bitcast.10, ...), custom_call_target="tpu_custom_call" | custom-call | bytes 1048576 | tf_op jit(solution)/shard_map/offer_first/pallas_call | solution.py:61
  1.4 6.7 %collective-permute-start = (bf16[4,64,128]{2,1,0:T(8,128)(2,1)S(1)}, bf16[4,64,128]{2,1,0:T(8,128)(2,1)S(1)}, u32[]{:S(2)}, u32[]{:S(2)}) collective-permute-start(bf16[4,64,128]{2,1,0:T(8,128)(2,1)S(1)} %get-tuple-element.62), channel_id=1, source_target_pairs={{0,120},{4,124},{8,16},{12,20},{16,8},{20,12},{24,32},{28,36},{32,... | collective-permute-start | bytes 196616 | tf_op jit(solution)/shard_map/ppermute | solution.py:44
  8.1 2.1 %collective-permute-start.3 = (bf16[4,64,128]{2,1,0:T(8,128)(2,1)S(1)}, bf16[4,64,128]{2,1,0:T(8,128)(2,1)S(1)}, u32[]{:S(2)}, u32[]{:S(2)}) collective-permute-start(bf16[4,64,128]{2,1,0:T(8,128)(2,1)S(1)} %get-tuple-element.65), channel_id=1, source_target_pairs={{0,4},{4,0},{8,12},{12,8},{16,20},{20,16},{24,28},{28,24},{32,36},... | collective-permute-start | bytes 196616 | tf_op jit(solution)/shard_map/ppermute | solution.py:44
  10.2 3.9 %prepare.1 = (f32[32,64,128]{2,1,0:T(8,128)S(1)}, bf16[32,64,128]{2,1,0:T(8,128)(2,1)S(1)}, bf16[8,16,128,128]{3,2,1,0:T(8,128)(2,1)S(1)}, s32[136]{0:T(256)S(4)}, s32[16,32]{1,0:T(8,128)S(4)}) custom-call(s32[1,8]{1,0:T(1,128)S(4)} %get-tuple-element.55.exports, s32[4,4,32]{2,1,0:T(4,128)S(4)} %get-tuple-element.56.positions, s32[32]{0:T(128)} %live.1, ...), custom_call_target="tpu_custom_call" | custom-call | flops 1073741824 | bytes 8388608 | tf_op jit(solution)/shard_map/prepare/pallas_call | solution.py:61
  14.1 0.0 collective-permute-done.1.refs_1_
  14.1 0.9 %collective-permute-done.2.refs_2_ = bf16[4,64,128]{2,1,0:T(8,128)(2,1)S(1)} collective-permute-done((bf16[4,64,128]{2,1,0:T(8,128)(2,1)S(1)}, bf16[4,64,128]{2,1,0:T(8,128)(2,1)S(1)}, u32[]{:S(2)}, u32[]{:S(2)}) %collective-permute-start.2) | collective-permute-done | bytes 65568 | tf_op jit(solution)/shard_map/ppermute | solution.py:44
  15.1 1.0 %export_step.4 = (f32[8,64,128]{2,1,0:T(8,128)S(1)}, bf16[4,64,128]{2,1,0:T(8,128)(2,1)S(1)}, bf16[4,64,128]{2,1,0:T(8,128)(2,1)S(1)}, bf16[4,64,128]{2,1,0:T(8,128)(2,1)S(1)}, bf16[4,64,128]{2,1,0:T(8,128)(2,1)S(1)}) custom-call(s32[16,32]{1,0:T(8,128)S(4)} %get-tuple-element.58.cols, s32[136]{0:T(256)S(4)} %get-tuple-element.57.table, ...), custom_call_target="tpu_custom_call" | custom-call | flops 268435456 | bytes 1048576 | tf_op jit(solution)/shard_map/export_step/pallas_call | solution.py:61
  16.1 2.3 %collective-permute-start.4 = (bf16[4,64,128]{2,1,0:T(8,128)(2,1)S(1)}, bf16[4,64,128]{2,1,0:T(8,128)(2,1)S(1)}, u32[]{:S(2)}, u32[]{:S(2)}) collective-permute-start(bf16[4,64,128]{2,1,0:T(8,128)(2,1)S(1)} %get-tuple-element.70), channel_id=1, source_target_pairs={{0,120},{4,124},{8,16},{12,20},{16,8},{20,12},{24,32},{28,36},{32,... | collective-permute-start | bytes 196616 | tf_op jit(solution)/shard_map/ppermute | solution.py:44
  18.4 1.3 %collective-permute-start.6 = (bf16[4,64,128]{2,1,0:T(8,128)(2,1)S(1)}, bf16[4,64,128]{2,1,0:T(8,128)(2,1)S(1)}, u32[]{:S(2)}, u32[]{:S(2)}) collective-permute-start(bf16[4,64,128]{2,1,0:T(8,128)(2,1)S(1)} %get-tuple-element.72), channel_id=1, source_target_pairs={{0,124},{4,8},{8,4},{12,16},{16,12},{20,24},{24,20},{28,32},{32,28... | collective-permute-start | bytes 196616 | tf_op jit(solution)/shard_map/ppermute | solution.py:44
  19.8 0.8 collective-permute-start.7
  20.6 6.5 %rest_step.4 = (f32[32,64,128]{2,1,0:T(8,128)S(1)}, bf16[32,64,128]{2,1,0:T(8,128)(2,1)S(1)}, bf16[24,16,128,128]{3,2,1,0:T(8,128)(2,1)S(1)}) custom-call(s32[16,32]{1,0:T(8,128)S(4)} %get-tuple-element.58.cols, s32[136]{0:T(256)S(4)} %get-tuple-element.57.table, bf16[32,16,128,128]{3,2,1,0:T(8,128)(2,1)} %weights.1, ...), custom_call_target="tpu_custom_call" | custom-call | flops 1073741824 | bytes 1048576 | tf_op jit(solution)/shard_map/rest_step/pallas_call | solution.py:61
  27.1 0.0 collective-permute-done.4.refs_0_
  27.1 0.0 collective-permute-done.5.refs_1_
  27.1 1.0 %export_step.5 = (f32[8,64,128]{2,1,0:T(8,128)S(1)}, bf16[4,64,128]{2,1,0:T(8,128)(2,1)S(1)}, bf16[4,64,128]{2,1,0:T(8,128)(2,1)S(1)}, bf16[4,64,128]{2,1,0:T(8,128)(2,1)S(1)}, bf16[4,64,128]{2,1,0:T(8,128)(2,1)S(1)}) custom-call(s32[16,32]{1,0:T(8,128)S(4)} %get-tuple-element.58.cols, s32[136]{0:T(256)S(4)} %get-tuple-element.57.table, ...), custom_call_target="tpu_custom_call" | custom-call | flops 268435456 | bytes 1048576 | tf_op jit(solution)/shard_map/export_step/pallas_call | solution.py:61
  28.1 3.4 %collective-permute-start.8 = (bf16[4,64,128]{2,1,0:T(8,128)(2,1)S(1)}, bf16[4,64,128]{2,1,0:T(8,128)(2,1)S(1)}, u32[]{:S(2)}, u32[]{:S(2)}) collective-permute-start(bf16[4,64,128]{2,1,0:T(8,128)(2,1)S(1)} %get-tuple-element.77), channel_id=1, source_target_pairs={{0,120},{4,124},{8,16},{12,20},{16,8},{20,12},{24,32},{28,36},{32,... | collective-permute-start | bytes 196616 | tf_op jit(solution)/shard_map/ppermute | solution.py:44
  31.5 0.0 collective-permute-start.9
  31.6 1.4 %collective-permute-start.10 = (bf16[4,64,128]{2,1,0:T(8,128)(2,1)S(1)}, bf16[4,64,128]{2,1,0:T(8,128)(2,1)S(1)}, u32[]{:S(2)}, u32[]{:S(2)}) collective-permute-start(bf16[4,64,128]{2,1,0:T(8,128)(2,1)S(1)} %get-tuple-element.79), channel_id=1, source_target_pairs={{0,124},{4,8},{8,4},{12,16},{16,12},{20,24},{24,20},{28,32},{32,28... | collective-permute-start | bytes 196616 | tf_op jit(solution)/shard_map/ppermute | solution.py:44
  32.9 0.8 collective-permute-start.11
  33.7 3.0 %rest_step.5 = (f32[32,64,128]{2,1,0:T(8,128)S(1)}, bf16[32,64,128]{2,1,0:T(8,128)(2,1)S(1)}) custom-call(s32[16,32]{1,0:T(8,128)S(4)} %get-tuple-element.58.cols, s32[136]{0:T(256)S(4)} %get-tuple-element.57.table, bf16[24,16,128,128]{3,2,1,0:T(8,128)(2,1)S(1)} %get-tuple-element.67.weights.turned, bf16[32,64,128]{2,1,0:T(8,128)(2,1)S(1)} %get-tuple-element.68.low, ...), custom_call_target="tpu_custom_call" | custom-call | flops 1073741824 | bytes 1048576 | tf_op jit(solution)/shard_map/rest_step/pallas_call | solution.py:61
  36.7 0.0 copy-start
  36.7 0.0 copy-start.1
  36.7 0.0 copy-start.2
  36.7 0.0 collective-permute-done.9.refs_1_
  36.7 1.8 %collective-permute-done.10.refs_2_ = bf16[4,64,128]{2,1,0:T(8,128)(2,1)S(1)} collective-permute-done((bf16[4,64,128]{2,1,0:T(8,128)(2,1)S(1)}, bf16[4,64,128]{2,1,0:T(8,128)(2,1)S(1)}, u32[]{:S(2)}, u32[]{:S(2)}) %collective-permute-start.10) | collective-permute-done | bytes 65568 | tf_op jit(solution)/shard_map/ppermute | solution.py:44
  38.6 0.0 collective-permute-done.11.refs_3_
  38.6 4.0 %whole_step.2 = (f32[32,64,128]{2,1,0:T(8,128)S(1)}, f32[32,128]{1,0:T(8,128)S(1)}) custom-call(s32[16,32]{1,0:T(8,128)S(4)} %get-tuple-element.58.cols, s32[136]{0:T(256)S(4)} %get-tuple-element.57.table, bf16[8,16,128,128]{3,2,1,0:T(8,128)(2,1)S(1)} %get-tuple-element.59.early, bf16[24,16,128,128]{3,2,1,0:T(8,128)(2,1)S(1)} %get-tuple-element.67.weights.turned, ...), custom_call_target="tpu_custom_call" | custom-call | flops 1073741824 | bytes 1048576 | tf_op jit(solution)/shard_map/whole_step/pallas_call | solution.py:61
  42.6 2.8 %collective-permute-start.14 = (f32[32,128]{1,0:T(8,128)S(1)}, f32[32,128]{1,0:T(8,128)S(1)}, u32[]{:S(2)}, u32[]{:S(2)}) collective-permute-start(f32[32,128]{1,0:T(8,128)S(1)} %get-tuple-element.82.refs_0_), channel_id=1, source_target_pairs={{1,0},{2,1},{3,2},{0,3},{5,4},{6,5},{7,6},{4,7},{9,8},{10,9},{11,1... | collective-permute-start | bytes 49160 | tf_op jit(solution)/shard_map/ppermute | solution.py:27
  45.4 0.8 collective-permute-start.13
  46.3 0.9 collective-permute-start.12
  47.1 3.5 %collective-permute-done.13.refs_2_ = f32[32,128]{1,0:T(8,128)S(1)} collective-permute-done((f32[32,128]{1,0:T(8,128)S(1)}, f32[32,128]{1,0:T(8,128)S(1)}, u32[]{:S(2)}, u32[]{:S(2)}) %collective-permute-start.13) | collective-permute-done | bytes 16416 | tf_op jit(solution)/shard_map/ppermute | solution.py:27
  50.7 0.5 collective-permute-done.12.refs_1_
  51.2 0.4 export_mix.1
  51.6 1.6 %collective-permute-start.15 = (bf16[4,64,128]{2,1,0:T(8,128)(2,1)S(1)}, bf16[4,64,128]{2,1,0:T(8,128)(2,1)S(1)}, u32[]{:S(2)}, u32[]{:S(2)}) collective-permute-start(bf16[4,64,128]{2,1,0:T(8,128)(2,1)S(1)} %get-tuple-element.85), channel_id=1, source_target_pairs={{0,120},{4,124},{8,16},{12,20},{16,8},{20,12},{24,32},{28,36},{32,... | collective-permute-start | bytes 196616 | tf_op jit(solution)/shard_map/ppermute | solution.py:44
  53.2 2.1 %collective-permute-start.18 = (bf16[4,64,128]{2,1,0:T(8,128)(2,1)S(1)}, bf16[4,64,128]{2,1,0:T(8,128)(2,1)S(1)}, u32[]{:S(2)}, u32[]{:S(2)}) collective-permute-start(bf16[4,64,128]{2,1,0:T(8,128)(2,1)S(1)} %get-tuple-element.88), channel_id=1, source_target_pairs={{0,4},{4,0},{8,12},{12,8},{16,20},{20,16},{24,28},{28,24},{32,36},... | collective-permute-start | bytes 196616 | tf_op jit(solution)/shard_map/ppermute | solution.py:44
  55.3 0.9 rest_mix.1
  56.2 3.1 %collective-permute-done.15.refs_0_ = bf16[4,64,128]{2,1,0:T(8,128)(2,1)S(1)} collective-permute-done((bf16[4,64,128]{2,1,0:T(8,128)(2,1)S(1)}, bf16[4,64,128]{2,1,0:T(8,128)(2,1)S(1)}, u32[]{:S(2)}, u32[]{:S(2)}) %collective-permute-start.15) | collective-permute-done | bytes 65568 | tf_op jit(solution)/shard_map/ppermute | solution.py:44
  59.3 0.0 collective-permute-done.16.refs_1_
  59.3 0.9 collective-permute-done.17.refs_2_
  60.2 0.0 collective-permute-done.18.refs_3_
  60.2 1.0 %export_step.6 = (f32[8,64,128]{2,1,0:T(8,128)S(1)}, bf16[4,64,128]{2,1,0:T(8,128)(2,1)S(1)}, bf16[4,64,128]{2,1,0:T(8,128)(2,1)S(1)}, bf16[4,64,128]{2,1,0:T(8,128)(2,1)S(1)}, bf16[4,64,128]{2,1,0:T(8,128)(2,1)S(1)}) custom-call(s32[16,32]{1,0:T(8,128)S(4)} %get-tuple-element.58.cols, s32[136]{0:T(256)S(4)} %get-tuple-element.57.table, ...), custom_call_target="tpu_custom_call" | custom-call | flops 268435456 | bytes 1048576 | tf_op jit(solution)/shard_map/export_step/pallas_call | solution.py:61
  61.2 1.4 %collective-permute-start.19 = (bf16[4,64,128]{2,1,0:T(8,128)(2,1)S(1)}, bf16[4,64,128]{2,1,0:T(8,128)(2,1)S(1)}, u32[]{:S(2)}, u32[]{:S(2)}) collective-permute-start(bf16[4,64,128]{2,1,0:T(8,128)(2,1)S(1)} %get-tuple-element.92), channel_id=1, source_target_pairs={{0,120},{4,124},{8,16},{12,20},{16,8},{20,12},{24,32},{28,36},{32,... | collective-permute-start | bytes 196616 | tf_op jit(solution)/shard_map/ppermute | solution.py:44
  62.6 0.0 collective-permute-start.20
  62.6 1.5 %collective-permute-start.21 = (bf16[4,64,128]{2,1,0:T(8,128)(2,1)S(1)}, bf16[4,64,128]{2,1,0:T(8,128)(2,1)S(1)}, u32[]{:S(2)}, u32[]{:S(2)}) collective-permute-start(bf16[4,64,128]{2,1,0:T(8,128)(2,1)S(1)} %get-tuple-element.94), channel_id=1, source_target_pairs={{0,124},{4,8},{8,4},{12,16},{16,12},{20,24},{24,20},{28,32},{32,28... | collective-permute-start | bytes 196616 | tf_op jit(solution)/shard_map/ppermute | solution.py:44
  64.0 0.7 collective-permute-start.22
  64.7 3.0 %rest_step.6 = (f32[32,64,128]{2,1,0:T(8,128)S(1)}, bf16[32,64,128]{2,1,0:T(8,128)(2,1)S(1)}) custom-call(s32[16,32]{1,0:T(8,128)S(4)} %get-tuple-element.58.cols, s32[136]{0:T(256)S(4)} %get-tuple-element.57.table, bf16[24,16,128,128]{3,2,1,0:T(8,128)(2,1)S(1)} %get-tuple-element.67.weights.turned, bf16[32,64,128]{2,1,0:T(8,128)(2,1)S(1)} %get-tuple-element.83.low, ...), custom_call_target="tpu_custom_call" | custom-call | flops 1073741824 | bytes 1048576 | tf_op jit(solution)/shard_map/rest_step/pallas_call | solution.py:61
  67.7 1.2 %collective-permute-done.19.refs_0_ = bf16[4,64,128]{2,1,0:T(8,128)(2,1)S(1)} collective-permute-done((bf16[4,64,128]{2,1,0:T(8,128)(2,1)S(1)}, bf16[4,64,128]{2,1,0:T(8,128)(2,1)S(1)}, u32[]{:S(2)}, u32[]{:S(2)}) %collective-permute-start.19) | collective-permute-done | bytes 65568 | tf_op jit(solution)/shard_map/ppermute | solution.py:44
  68.9 0.7 collective-permute-done.21.refs_2_
  69.6 0.0 collective-permute-done.22.refs_3_
  69.6 1.0 %export_step.7 = (f32[8,64,128]{2,1,0:T(8,128)S(1)}, bf16[4,64,128]{2,1,0:T(8,128)(2,1)S(1)}, bf16[4,64,128]{2,1,0:T(8,128)(2,1)S(1)}, bf16[4,64,128]{2,1,0:T(8,128)(2,1)S(1)}, bf16[4,64,128]{2,1,0:T(8,128)(2,1)S(1)}) custom-call(s32[16,32]{1,0:T(8,128)S(4)} %get-tuple-element.58.cols, s32[136]{0:T(256)S(4)} %get-tuple-element.57.table, ...), custom_call_target="tpu_custom_call" | custom-call | flops 268435456 | bytes 1048576 | tf_op jit(solution)/shard_map/export_step/pallas_call | solution.py:61
  70.6 1.6 %collective-permute-start.23 = (bf16[4,64,128]{2,1,0:T(8,128)(2,1)S(1)}, bf16[4,64,128]{2,1,0:T(8,128)(2,1)S(1)}, u32[]{:S(2)}, u32[]{:S(2)}) collective-permute-start(bf16[4,64,128]{2,1,0:T(8,128)(2,1)S(1)} %get-tuple-element.99), channel_id=1, source_target_pairs={{0,120},{4,124},{8,16},{12,20},{16,8},{20,12},{24,32},{28,36},{32,... | collective-permute-start | bytes 196616 | tf_op jit(solution)/shard_map/ppermute | solution.py:44
  72.2 0.0 collective-permute-start.24
  72.2 1.8 %collective-permute-start.25 = (bf16[4,64,128]{2,1,0:T(8,128)(2,1)S(1)}, bf16[4,64,128]{2,1,0:T(8,128)(2,1)S(1)}, u32[]{:S(2)}, u32[]{:S(2)}) collective-permute-start(bf16[4,64,128]{2,1,0:T(8,128)(2,1)S(1)} %get-tuple-element.101), channel_id=1, source_target_pairs={{0,124},{4,8},{8,4},{12,16},{16,12},{20,24},{24,20},{28,32},{32,28... | collective-permute-start | bytes 196616 | tf_op jit(solution)/shard_map/ppermute | solution.py:44
  74.0 0.3 collective-permute-start.26
  74.3 3.0 %rest_step.7 = (f32[32,64,128]{2,1,0:T(8,128)S(1)}, bf16[32,64,128]{2,1,0:T(8,128)(2,1)S(1)}) custom-call(s32[16,32]{1,0:T(8,128)S(4)} %get-tuple-element.58.cols, s32[136]{0:T(256)S(4)} %get-tuple-element.57.table, bf16[24,16,128,128]{3,2,1,0:T(8,128)(2,1)S(1)} %get-tuple-element.67.weights.turned, bf16[32,64,128]{2,1,0:T(8,128)(2,1)S(1)} %get-tuple-element.90.low, ...), custom_call_target="tpu_custom_call" | custom-call | flops 1073741824 | bytes 1048576 | tf_op jit(solution)/shard_map/rest_step/pallas_call | solution.py:61
  77.3 1.0 %collective-permute-done.23.refs_0_ = bf16[4,64,128]{2,1,0:T(8,128)(2,1)S(1)} collective-permute-done((bf16[4,64,128]{2,1,0:T(8,128)(2,1)S(1)}, bf16[4,64,128]{2,1,0:T(8,128)(2,1)S(1)}, u32[]{:S(2)}, u32[]{:S(2)}) %collective-permute-start.23) | collective-permute-done | bytes 65568 | tf_op jit(solution)/shard_map/ppermute | solution.py:44
  78.3 0.9 collective-permute-done.25.refs_2_
  79.2 4.1 %whole_step.3 = (f32[32,64,128]{2,1,0:T(8,128)S(1)}, f32[32,128]{1,0:T(8,128)S(1)}) custom-call(s32[16,32]{1,0:T(8,128)S(4)} %get-tuple-element.58.cols, s32[136]{0:T(256)S(4)} %get-tuple-element.57.table, bf16[8,16,128,128]{3,2,1,0:T(8,128)(2,1)S(1)} %get-tuple-element.59.early, bf16[24,16,128,128]{3,2,1,0:T(8,128)(2,1)S(1)} %get-tuple-element.67.weights.turned, ...), custom_call_target="tpu_custom_call" | custom-call | flops 1073741824 | bytes 1048576 | tf_op jit(solution)/shard_map/whole_step/pallas_call | solution.py:61
  83.3 0.4 collective-permute-start.29
  83.7 1.4 %collective-permute-start.28 = (f32[32,128]{1,0:T(8,128)S(1)}, f32[32,128]{1,0:T(8,128)S(1)}, u32[]{:S(2)}, u32[]{:S(2)}) collective-permute-start(f32[32,128]{1,0:T(8,128)S(1)} %get-tuple-element.104.refs_0_), channel_id=1, source_target_pairs={{2,0},{3,1},{0,2},{1,3},{6,4},{7,5},{4,6},{5,7},{10,8},{11,9},{8,1... | collective-permute-start | bytes 49160 | tf_op jit(solution)/shard_map/ppermute | solution.py:27
  85.1 1.2 %collective-permute-start.27 = (f32[32,128]{1,0:T(8,128)S(1)}, f32[32,128]{1,0:T(8,128)S(1)}, u32[]{:S(2)}, u32[]{:S(2)}) collective-permute-start(f32[32,128]{1,0:T(8,128)S(1)} %get-tuple-element.104.refs_0_), channel_id=1, source_target_pairs={{3,0},{0,1},{1,2},{2,3},{7,4},{4,5},{5,6},{6,7},{11,8},{8,9},{9,10... | collective-permute-start | bytes 49160 | tf_op jit(solution)/shard_map/ppermute | solution.py:27
  86.3 0.8 collective-permute-done.29.refs_3_
  87.1 1.8 %collective-permute-done.28.refs_2_ = f32[32,128]{1,0:T(8,128)S(1)} collective-permute-done((f32[32,128]{1,0:T(8,128)S(1)}, f32[32,128]{1,0:T(8,128)S(1)}, u32[]{:S(2)}, u32[]{:S(2)}) %collective-permute-start.28) | collective-permute-done | bytes 16416 | tf_op jit(solution)/shard_map/ppermute | solution.py:27
  88.9 1.1 %collective-permute-done.27.refs_1_ = f32[32,128]{1,0:T(8,128)S(1)} collective-permute-done((f32[32,128]{1,0:T(8,128)S(1)}, f32[32,128]{1,0:T(8,128)S(1)}, u32[]{:S(2)}, u32[]{:S(2)}) %collective-permute-start.27) | collective-permute-done | bytes 16416 | tf_op jit(solution)/shard_map/ppermute | solution.py:27
  90.0 1.6 %last_mix.1 = f32[64,4096]{1,0:T(8,128)} custom-call(s32[136]{0:T(256)S(4)} %get-tuple-element.57.table, f32[32,64,128]{2,1,0:T(8,128)S(1)} %get-tuple-element.103.state, bf16[32,128,128]{2,1,0:T(8,128)(2,1)S(1)} %copy-done, f32[1,64]{1,0:T(1,128)S(1)} %bitcast.6, f32[1,64]{1,0:T(1,128)S(1)} %bitcast.9, f32[32,128]{1,0:T(8,128)S(1)} %get-tuple-element.104.refs_0_, ...), custom_call_target="tpu_custom_call" | custom-call | flops 67108864 | bytes 1048576 | tf_op jit(solution)/shard_map/last_mix/pallas_call | solution.py:61
  (17 shorter events, 0.0 us)
Async XLA Ops:
  1.4 12.7 %collective-permute-start = (bf16[4,64,128]{2,1,0:T(8,128)(2,1)S(1)}, bf16[4,64,128]{2,1,0:T(8,128)(2,1)S(1)}, u32[]{:S(2)}, u32[]{:S(2)}) collective-permute-start(bf16[4,64,128]{2,1,0:T(8,128)(2,1)S(1)} %get-tuple-element.62), channel_id=1, source_target_pairs={{0,120},{4,124},{8,16},{12,20},{16,8},{20,12},{24,32},{28,36},{32,... | collective-permute-start | bytes 196616 | tf_op jit(solution)/shard_map/ppermute | solution.py:44
  8.1 6.1 %collective-permute-start.1 = (bf16[4,64,128]{2,1,0:T(8,128)(2,1)S(1)}, bf16[4,64,128]{2,1,0:T(8,128)(2,1)S(1)}, u32[]{:S(2)}, u32[]{:S(2)}) collective-permute-start(bf16[4,64,128]{2,1,0:T(8,128)(2,1)S(1)} %get-tuple-element.63), channel_id=1, source_target_pairs={{0,8},{4,12},{8,0},{12,4},{16,24},{20,28},{24,16},{28,20},{32,40},... | collective-permute-start | bytes 196616 | tf_op jit(solution)/shard_map/ppermute | solution.py:44
  8.1 7.0 %collective-permute-start.2 = (bf16[4,64,128]{2,1,0:T(8,128)(2,1)S(1)}, bf16[4,64,128]{2,1,0:T(8,128)(2,1)S(1)}, u32[]{:S(2)}, u32[]{:S(2)}) collective-permute-start(bf16[4,64,128]{2,1,0:T(8,128)(2,1)S(1)} %get-tuple-element.64), channel_id=1, source_target_pairs={{0,124},{4,8},{8,4},{12,16},{16,12},{20,24},{24,20},{28,32},{32,28... | collective-permute-start | bytes 196616 | tf_op jit(solution)/shard_map/ppermute | solution.py:44
  8.1 7.0 %collective-permute-start.3 = (bf16[4,64,128]{2,1,0:T(8,128)(2,1)S(1)}, bf16[4,64,128]{2,1,0:T(8,128)(2,1)S(1)}, u32[]{:S(2)}, u32[]{:S(2)}) collective-permute-start(bf16[4,64,128]{2,1,0:T(8,128)(2,1)S(1)} %get-tuple-element.65), channel_id=1, source_target_pairs={{0,4},{4,0},{8,12},{12,8},{16,20},{20,16},{24,28},{28,24},{32,36},... | collective-permute-start | bytes 196616 | tf_op jit(solution)/shard_map/ppermute | solution.py:44
  16.1 11.0 %collective-permute-start.4 = (bf16[4,64,128]{2,1,0:T(8,128)(2,1)S(1)}, bf16[4,64,128]{2,1,0:T(8,128)(2,1)S(1)}, u32[]{:S(2)}, u32[]{:S(2)}) collective-permute-start(bf16[4,64,128]{2,1,0:T(8,128)(2,1)S(1)} %get-tuple-element.70), channel_id=1, source_target_pairs={{0,120},{4,124},{8,16},{12,20},{16,8},{20,12},{24,32},{28,36},{32,... | collective-permute-start | bytes 196616 | tf_op jit(solution)/shard_map/ppermute | solution.py:44
  18.4 8.7 %collective-permute-start.5 = (bf16[4,64,128]{2,1,0:T(8,128)(2,1)S(1)}, bf16[4,64,128]{2,1,0:T(8,128)(2,1)S(1)}, u32[]{:S(2)}, u32[]{:S(2)}) collective-permute-start(bf16[4,64,128]{2,1,0:T(8,128)(2,1)S(1)} %get-tuple-element.71), channel_id=1, source_target_pairs={{0,8},{4,12},{8,0},{12,4},{16,24},{20,28},{24,16},{28,20},{32,40},... | collective-permute-start | bytes 196616 | tf_op jit(solution)/shard_map/ppermute | solution.py:44
  18.4 8.7 %collective-permute-start.6 = (bf16[4,64,128]{2,1,0:T(8,128)(2,1)S(1)}, bf16[4,64,128]{2,1,0:T(8,128)(2,1)S(1)}, u32[]{:S(2)}, u32[]{:S(2)}) collective-permute-start(bf16[4,64,128]{2,1,0:T(8,128)(2,1)S(1)} %get-tuple-element.72), channel_id=1, source_target_pairs={{0,124},{4,8},{8,4},{12,16},{16,12},{20,24},{24,20},{28,32},{32,28... | collective-permute-start | bytes 196616 | tf_op jit(solution)/shard_map/ppermute | solution.py:44
  19.8 7.3 %collective-permute-start.7 = (bf16[4,64,128]{2,1,0:T(8,128)(2,1)S(1)}, bf16[4,64,128]{2,1,0:T(8,128)(2,1)S(1)}, u32[]{:S(2)}, u32[]{:S(2)}) collective-permute-start(bf16[4,64,128]{2,1,0:T(8,128)(2,1)S(1)} %get-tuple-element.73), channel_id=1, source_target_pairs={{0,4},{4,0},{8,12},{12,8},{16,20},{20,16},{24,28},{28,24},{32,36},... | collective-permute-start | bytes 196616 | tf_op jit(solution)/shard_map/ppermute | solution.py:44
  28.1 8.6 %collective-permute-start.8 = (bf16[4,64,128]{2,1,0:T(8,128)(2,1)S(1)}, bf16[4,64,128]{2,1,0:T(8,128)(2,1)S(1)}, u32[]{:S(2)}, u32[]{:S(2)}) collective-permute-start(bf16[4,64,128]{2,1,0:T(8,128)(2,1)S(1)} %get-tuple-element.77), channel_id=1, source_target_pairs={{0,120},{4,124},{8,16},{12,20},{16,8},{20,12},{24,32},{28,36},{32,... | collective-permute-start | bytes 196616 | tf_op jit(solution)/shard_map/ppermute | solution.py:44
  31.5 5.2 %collective-permute-start.9 = (bf16[4,64,128]{2,1,0:T(8,128)(2,1)S(1)}, bf16[4,64,128]{2,1,0:T(8,128)(2,1)S(1)}, u32[]{:S(2)}, u32[]{:S(2)}) collective-permute-start(bf16[4,64,128]{2,1,0:T(8,128)(2,1)S(1)} %get-tuple-element.78), channel_id=1, source_target_pairs={{0,8},{4,12},{8,0},{12,4},{16,24},{20,28},{24,16},{28,20},{32,40},... | collective-permute-start | bytes 196616 | tf_op jit(solution)/shard_map/ppermute | solution.py:44
  31.6 7.0 %collective-permute-start.10 = (bf16[4,64,128]{2,1,0:T(8,128)(2,1)S(1)}, bf16[4,64,128]{2,1,0:T(8,128)(2,1)S(1)}, u32[]{:S(2)}, u32[]{:S(2)}) collective-permute-start(bf16[4,64,128]{2,1,0:T(8,128)(2,1)S(1)} %get-tuple-element.79), channel_id=1, source_target_pairs={{0,124},{4,8},{8,4},{12,16},{16,12},{20,24},{24,20},{28,32},{32,28... | collective-permute-start | bytes 196616 | tf_op jit(solution)/shard_map/ppermute | solution.py:44
  32.9 5.7 %collective-permute-start.11 = (bf16[4,64,128]{2,1,0:T(8,128)(2,1)S(1)}, bf16[4,64,128]{2,1,0:T(8,128)(2,1)S(1)}, u32[]{:S(2)}, u32[]{:S(2)}) collective-permute-start(bf16[4,64,128]{2,1,0:T(8,128)(2,1)S(1)} %get-tuple-element.80), channel_id=1, source_target_pairs={{0,4},{4,0},{8,12},{12,8},{16,20},{20,16},{24,28},{28,24},{32,36},... | collective-permute-start | bytes 196616 | tf_op jit(solution)/shard_map/ppermute | solution.py:44
  36.7 14.6 %copy-start = (bf16[32,128,128]{2,1,0:T(8,128)(2,1)S(1)}, bf16[32,128,128]{2,1,0:T(8,128)(2,1)}, u32[]{:S(2)}) copy-start(bf16[32,128,128]{2,1,0:T(8,128)(2,1)} %inverse.5) | copy-start | bytes 3145732
  36.7 14.5 %copy-start.1 = (f32[64]{0:T(128)S(1)}, f32[64]{0:T(128)}, u32[]{:S(2)}) copy-start(f32[64]{0:T(128)} %param.16) | copy-start | bytes 772
  36.7 14.5 %copy-start.2 = (f32[64]{0:T(128)S(1)}, f32[64]{0:T(128)}, u32[]{:S(2)}) copy-start(f32[64]{0:T(128)} %param.17) | copy-start | bytes 772
  42.6 4.5 %collective-permute-start.14 = (f32[32,128]{1,0:T(8,128)S(1)}, f32[32,128]{1,0:T(8,128)S(1)}, u32[]{:S(2)}, u32[]{:S(2)}) collective-permute-start(f32[32,128]{1,0:T(8,128)S(1)} %get-tuple-element.82.refs_0_), channel_id=1, source_target_pairs={{1,0},{2,1},{3,2},{0,3},{5,4},{6,5},{7,6},{4,7},{9,8},{10,9},{11,1... | collective-permute-start | bytes 49160 | tf_op jit(solution)/shard_map/ppermute | solution.py:27
  45.4 5.2 %collective-permute-start.13 = (f32[32,128]{1,0:T(8,128)S(1)}, f32[32,128]{1,0:T(8,128)S(1)}, u32[]{:S(2)}, u32[]{:S(2)}) collective-permute-start(f32[32,128]{1,0:T(8,128)S(1)} %get-tuple-element.82.refs_0_), channel_id=1, source_target_pairs={{2,0},{3,1},{0,2},{1,3},{6,4},{7,5},{4,6},{5,7},{10,8},{11,9},{8,1... | collective-permute-start | bytes 49160 | tf_op jit(solution)/shard_map/ppermute | solution.py:27
  46.3 4.9 %collective-permute-start.12 = (f32[32,128]{1,0:T(8,128)S(1)}, f32[32,128]{1,0:T(8,128)S(1)}, u32[]{:S(2)}, u32[]{:S(2)}) collective-permute-start(f32[32,128]{1,0:T(8,128)S(1)} %get-tuple-element.82.refs_0_), channel_id=1, source_target_pairs={{3,0},{0,1},{1,2},{2,3},{7,4},{4,5},{5,6},{6,7},{11,8},{8,9},{9,10... | collective-permute-start | bytes 49160 | tf_op jit(solution)/shard_map/ppermute | solution.py:27
  51.6 7.7 %collective-permute-start.15 = (bf16[4,64,128]{2,1,0:T(8,128)(2,1)S(1)}, bf16[4,64,128]{2,1,0:T(8,128)(2,1)S(1)}, u32[]{:S(2)}, u32[]{:S(2)}) collective-permute-start(bf16[4,64,128]{2,1,0:T(8,128)(2,1)S(1)} %get-tuple-element.85), channel_id=1, source_target_pairs={{0,120},{4,124},{8,16},{12,20},{16,8},{20,12},{24,32},{28,36},{32,... | collective-permute-start | bytes 196616 | tf_op jit(solution)/shard_map/ppermute | solution.py:44
  53.2 6.1 %collective-permute-start.16 = (bf16[4,64,128]{2,1,0:T(8,128)(2,1)S(1)}, bf16[4,64,128]{2,1,0:T(8,128)(2,1)S(1)}, u32[]{:S(2)}, u32[]{:S(2)}) collective-permute-start(bf16[4,64,128]{2,1,0:T(8,128)(2,1)S(1)} %get-tuple-element.86), channel_id=1, source_target_pairs={{0,8},{4,12},{8,0},{12,4},{16,24},{20,28},{24,16},{28,20},{32,40},... | collective-permute-start | bytes 196616 | tf_op jit(solution)/shard_map/ppermute | solution.py:44
  53.2 7.0 %collective-permute-start.17 = (bf16[4,64,128]{2,1,0:T(8,128)(2,1)S(1)}, bf16[4,64,128]{2,1,0:T(8,128)(2,1)S(1)}, u32[]{:S(2)}, u32[]{:S(2)}) collective-permute-start(bf16[4,64,128]{2,1,0:T(8,128)(2,1)S(1)} %get-tuple-element.87), channel_id=1, source_target_pairs={{0,124},{4,8},{8,4},{12,16},{16,12},{20,24},{24,20},{28,32},{32,28... | collective-permute-start | bytes 196616 | tf_op jit(solution)/shard_map/ppermute | solution.py:44
  53.2 7.0 %collective-permute-start.18 = (bf16[4,64,128]{2,1,0:T(8,128)(2,1)S(1)}, bf16[4,64,128]{2,1,0:T(8,128)(2,1)S(1)}, u32[]{:S(2)}, u32[]{:S(2)}) collective-permute-start(bf16[4,64,128]{2,1,0:T(8,128)(2,1)S(1)} %get-tuple-element.88), channel_id=1, source_target_pairs={{0,4},{4,0},{8,12},{12,8},{16,20},{20,16},{24,28},{28,24},{32,36},... | collective-permute-start | bytes 196616 | tf_op jit(solution)/shard_map/ppermute | solution.py:44
  61.2 7.7 %collective-permute-start.19 = (bf16[4,64,128]{2,1,0:T(8,128)(2,1)S(1)}, bf16[4,64,128]{2,1,0:T(8,128)(2,1)S(1)}, u32[]{:S(2)}, u32[]{:S(2)}) collective-permute-start(bf16[4,64,128]{2,1,0:T(8,128)(2,1)S(1)} %get-tuple-element.92), channel_id=1, source_target_pairs={{0,120},{4,124},{8,16},{12,20},{16,8},{20,12},{24,32},{28,36},{32,... | collective-permute-start | bytes 196616 | tf_op jit(solution)/shard_map/ppermute | solution.py:44
  62.6 6.3 %collective-permute-start.20 = (bf16[4,64,128]{2,1,0:T(8,128)(2,1)S(1)}, bf16[4,64,128]{2,1,0:T(8,128)(2,1)S(1)}, u32[]{:S(2)}, u32[]{:S(2)}) collective-permute-start(bf16[4,64,128]{2,1,0:T(8,128)(2,1)S(1)} %get-tuple-element.93), channel_id=1, source_target_pairs={{0,8},{4,12},{8,0},{12,4},{16,24},{20,28},{24,16},{28,20},{32,40},... | collective-permute-start | bytes 196616 | tf_op jit(solution)/shard_map/ppermute | solution.py:44
  62.6 7.0 %collective-permute-start.21 = (bf16[4,64,128]{2,1,0:T(8,128)(2,1)S(1)}, bf16[4,64,128]{2,1,0:T(8,128)(2,1)S(1)}, u32[]{:S(2)}, u32[]{:S(2)}) collective-permute-start(bf16[4,64,128]{2,1,0:T(8,128)(2,1)S(1)} %get-tuple-element.94), channel_id=1, source_target_pairs={{0,124},{4,8},{8,4},{12,16},{16,12},{20,24},{24,20},{28,32},{32,28... | collective-permute-start | bytes 196616 | tf_op jit(solution)/shard_map/ppermute | solution.py:44
  64.0 5.6 %collective-permute-start.22 = (bf16[4,64,128]{2,1,0:T(8,128)(2,1)S(1)}, bf16[4,64,128]{2,1,0:T(8,128)(2,1)S(1)}, u32[]{:S(2)}, u32[]{:S(2)}) collective-permute-start(bf16[4,64,128]{2,1,0:T(8,128)(2,1)S(1)} %get-tuple-element.95), channel_id=1, source_target_pairs={{0,4},{4,0},{8,12},{12,8},{16,20},{20,16},{24,28},{28,24},{32,36},... | collective-permute-start | bytes 196616 | tf_op jit(solution)/shard_map/ppermute | solution.py:44
  70.6 7.7 %collective-permute-start.23 = (bf16[4,64,128]{2,1,0:T(8,128)(2,1)S(1)}, bf16[4,64,128]{2,1,0:T(8,128)(2,1)S(1)}, u32[]{:S(2)}, u32[]{:S(2)}) collective-permute-start(bf16[4,64,128]{2,1,0:T(8,128)(2,1)S(1)} %get-tuple-element.99), channel_id=1, source_target_pairs={{0,120},{4,124},{8,16},{12,20},{16,8},{20,12},{24,32},{28,36},{32,... | collective-permute-start | bytes 196616 | tf_op jit(solution)/shard_map/ppermute | solution.py:44
  72.2 6.1 %collective-permute-start.24 = (bf16[4,64,128]{2,1,0:T(8,128)(2,1)S(1)}, bf16[4,64,128]{2,1,0:T(8,128)(2,1)S(1)}, u32[]{:S(2)}, u32[]{:S(2)}) collective-permute-start(bf16[4,64,128]{2,1,0:T(8,128)(2,1)S(1)} %get-tuple-element.100), channel_id=1, source_target_pairs={{0,8},{4,12},{8,0},{12,4},{16,24},{20,28},{24,16},{28,20},{32,40},... | collective-permute-start | bytes 196616 | tf_op jit(solution)/shard_map/ppermute | solution.py:44
  72.2 7.0 %collective-permute-start.25 = (bf16[4,64,128]{2,1,0:T(8,128)(2,1)S(1)}, bf16[4,64,128]{2,1,0:T(8,128)(2,1)S(1)}, u32[]{:S(2)}, u32[]{:S(2)}) collective-permute-start(bf16[4,64,128]{2,1,0:T(8,128)(2,1)S(1)} %get-tuple-element.101), channel_id=1, source_target_pairs={{0,124},{4,8},{8,4},{12,16},{16,12},{20,24},{24,20},{28,32},{32,28... | collective-permute-start | bytes 196616 | tf_op jit(solution)/shard_map/ppermute | solution.py:44
  74.0 5.2 %collective-permute-start.26 = (bf16[4,64,128]{2,1,0:T(8,128)(2,1)S(1)}, bf16[4,64,128]{2,1,0:T(8,128)(2,1)S(1)}, u32[]{:S(2)}, u32[]{:S(2)}) collective-permute-start(bf16[4,64,128]{2,1,0:T(8,128)(2,1)S(1)} %get-tuple-element.102), channel_id=1, source_target_pairs={{0,4},{4,0},{8,12},{12,8},{16,20},{20,16},{24,28},{28,24},{32,36},... | collective-permute-start | bytes 196616 | tf_op jit(solution)/shard_map/ppermute | solution.py:44
  83.3 3.8 %collective-permute-start.29 = (f32[32,128]{1,0:T(8,128)S(1)}, f32[32,128]{1,0:T(8,128)S(1)}, u32[]{:S(2)}, u32[]{:S(2)}) collective-permute-start(f32[32,128]{1,0:T(8,128)S(1)} %get-tuple-element.104.refs_0_), channel_id=1, source_target_pairs={{1,0},{2,1},{3,2},{0,3},{5,4},{6,5},{7,6},{4,7},{9,8},{10,9},{11,1... | collective-permute-start | bytes 49160 | tf_op jit(solution)/shard_map/ppermute | solution.py:27
  83.7 5.2 %collective-permute-start.28 = (f32[32,128]{1,0:T(8,128)S(1)}, f32[32,128]{1,0:T(8,128)S(1)}, u32[]{:S(2)}, u32[]{:S(2)}) collective-permute-start(f32[32,128]{1,0:T(8,128)S(1)} %get-tuple-element.104.refs_0_), channel_id=1, source_target_pairs={{2,0},{3,1},{0,2},{1,3},{6,4},{7,5},{4,6},{5,7},{10,8},{11,9},{8,1... | collective-permute-start | bytes 49160 | tf_op jit(solution)/shard_map/ppermute | solution.py:27
  85.1 4.9 %collective-permute-start.27 = (f32[32,128]{1,0:T(8,128)S(1)}, f32[32,128]{1,0:T(8,128)S(1)}, u32[]{:S(2)}, u32[]{:S(2)}) collective-permute-start(f32[32,128]{1,0:T(8,128)S(1)} %get-tuple-element.104.refs_0_), channel_id=1, source_target_pairs={{3,0},{0,1},{1,2},{2,3},{7,4},{4,5},{5,6},{6,7},{11,8},{8,9},{9,10... | collective-permute-start | bytes 49160 | tf_op jit(solution)/shard_map/ppermute | solution.py:27

commit v3 on v2

--- a/solution.py
+++ b/solution.py
@@ -64,7 +64,7 @@
         out_specs=[spec(s) for _, s in outs],
         out_shape=[o for o, _ in outs],
         scratch_shapes=list(scratch),
-        compiler_params=pltpu.CompilerParams(vmem_limit_bytes=24 << 20),
+        compiler_params=pltpu.CompilerParams(vmem_limit_bytes=12 << 20),
         cost_estimate=pl.CostEstimate(flops=flops, bytes_accessed=moved, transcendentals=0),
         name=name,
     )(*[v for v, _ in args])
@@ -115,42 +115,32 @@
             sends[link][k] = landed[:, columns].astype(BF16)
 
 
-def write_table(table, exports, positions, lives, blocks):
-    offered = exports.shape[1]
+def write_table(table, exported, again, set_of_offered, positions, wet, blocks, first, places):
     near, reach = positions.shape[:2]
-    exported = [exports[0, e] for e in range(offered)]
+    offered = len(exported)
     free = jnp.int32(0)
-    places = SPARE - offered
     for e, row in enumerate(exported):
         table[EXPORTS + e] = row
-        seen = jnp.bool_(False)
-        place = jnp.int32(e)
-        for f in reversed(range(e)):
-            same = exported[f] == row
-            seen = jnp.logical_or(seen, same)
-            place = jnp.where(same, f, place)
-        table[SPARE + e] = place
-        table[places + free] = jnp.int32(e)
-        free = free + jnp.where(seen, 1, 0)
+        places[jnp.minimum(free, offered - 1)] = jnp.int32(EXPORTS + e)
+        free = free + again[e].astype(jnp.int32)
+    for e in reversed(range(offered)):
+        first[exported[e]] = jnp.int32(e)
+    mine = lax.axis_index("region")
     for link in range(near):
-        table[LINKS + link] = link_neighbour(link, lax.axis_index("region"))
+        table[LINKS + link] = link_neighbour(link, mine)
         for k in range(reach):
-            table[SENDS + link * reach + k] = table[SPARE + read_position(positions, link, k)]
-    wet = lives[lax.axis_index("region")]
+            place = read_position(positions, link, k)
+            table[SENDS + link * reach + k] = first[table[EXPORTS + place]]
     table[LIVE] = wet
     n = jnp.int32(0)
     count = jnp.int32(0)
     for b in range(blocks):
-        hit = exported[0] == b
-        for row in exported[1:]:
-            hit = jnp.logical_or(hit, row == b)
-        fills = EXPORTS + table[places + jnp.minimum(n, offered - 1)]
-        place = jnp.where(n < free, fills, REST + n - free)
-        table[jnp.where(hit, TABLE - 1, place)] = jnp.int32(b)
-        listed = jnp.logical_and(jnp.logical_not(hit), n >= free)
-        count = count + jnp.where(jnp.logical_and(listed, b < wet), 1, 0)
-        n = n + jnp.where(hit, 0, 1)
-    table[COUNT] = count
+        other = 1 - jnp.bitwise_and(lax.shift_right_logical(set_of_offered, jnp.int32(b)), 1)
+        place = jnp.where(n < free, places[jnp.minimum(n, offered - 1)], REST + n - free)
+        table[jnp.where(other == 1, place, TABLE - 1)] = jnp.int32(b)
+        count = count + jnp.where(b < wet, other, 0)
+        n = n + other
+    table[COUNT] = jnp.maximum(count - free, 0)
 
 
 def prepare_kernel(
@@ -166,49 +156,33 @@
     table,
     cols,
     lives,
-    landed,
-    landed_rows,
+    first,
+    places,
     sems,
-    block_sems,
 ):
     blocks, slots, block, _ = transport.shape
     offered = exports.shape[1]
-    small = fetch([(live, lives), (col_slot, cols), (tracers, landed)], sems)
+    small = fetch([(live, lives), (col_slot, cols)], sems)
     exported = [exports[0, e] for e in range(offered)]
     again = []
-    for e in range(offered):
-        seen = jnp.bool_(False)
-        for f in range(e):
-            seen = jnp.logical_or(seen, exported[f] == exported[e])
-        again.append(seen)
-
-    def rows_copy(e, b):
-        return pltpu.make_async_copy(transport.at[b], landed_rows.at[e], block_sems.at[e])
-
-    for e in range(offered):
-
-        @pl.when(jnp.logical_not(again[e]))
-        def _():
-            rows_copy(e, exported[e]).start()
+    set_of_offered = jnp.int32(0)
+    for row in exported:
+        bit = lax.shift_left(jnp.int32(1), row)
+        again.append(jnp.bitwise_and(set_of_offered, bit) != 0)
+        set_of_offered = jnp.bitwise_or(set_of_offered, bit)
 
     small[0].wait()
-    write_table(table, exports, positions, lives, blocks)
-    for e in range(offered):
-
-        @pl.when(again[e])
-        def _():
-            rows_copy(e, table[EXPORTS + e]).start()
-
-    for copy in small[1:]:
-        copy.wait()
+    wet = lives[lax.axis_index("region")]
+    write_table(table, exported, again, set_of_offered, positions, wet, blocks, first, places)
     for b in range(blocks):
-        value = landed[:, b * block : (b + 1) * block]
+        value = tracers[:, b * block : (b + 1) * block]
         state[b] = value
         low[b] = value.astype(BF16)
     for e in range(offered):
-        rows_copy(e, table[EXPORTS + e]).wait()
+        b = table[EXPORTS + e]
         for s in range(slots):
-            early[e, s] = landed_rows[e, s].T
+            early[e, s] = transport[b, s].T
+    small[1].wait()
 
 
 def fill(ext, low, halo, table):
@@ -282,18 +256,8 @@
     offered = exported.shape[0]
     rest = state.shape[0] - offered
     if first:
-        new_state, new_low, turned, ext, landed, sems, *fresh = refs
-
-        def chunk(i):
-            return pltpu.make_async_copy(weights.at[table[REST + i]], landed.at[i], sems.at[i])
-
+        new_state, new_low, turned, ext, *fresh = refs
         quads = jnp.maximum(lax.div(table[COUNT] + 3, 4), 1)
-
-        def begin(i, carry):
-            chunk(i).start()
-            return carry
-
-        lax.fori_loop(0, 4 * quads, begin, 0)
     else:
         new_state, new_low, ext = refs
     fill(ext, low, halo, table)
@@ -321,14 +285,11 @@
 
     def turn(start, there):
         for i in range(group):
-            for s in range(landed.shape[1]):
-                tile = landed[start + i, s].T
+            b = table[REST + start + i]
+            for s in range(weights.shape[1]):
+                tile = weights[b, s].T
                 turned[start + i, s] = tile
                 there[i, s] = tile
-
-    def wait(start):
-        for i in range(group):
-            chunk(start + i).wait()
 
     def compute(start, there):
         for i in range(group):
@@ -336,19 +297,15 @@
 
     def several(g, carry):
         start = 2 * g * group
-        wait(start + group)
-        wait(start + 2 * group)
         compute(start, fresh[0])
         turn(start + group, fresh[1])
         compute(start + group, fresh[1])
         turn(start + 2 * group, fresh[0])
         return carry
 
-    wait(0)
     turn(0, fresh[0])
     lax.fori_loop(0, quads - 1, several, 0)
     last = 2 * group * (quads - 1)
-    wait(last + group)
     compute(last, fresh[0])
     turn(last + group, fresh[1])
     compute(last + group, fresh[1])
@@ -455,27 +412,28 @@
     low_type = kept((blocks, width, block), BF16)
 
     def across(part):
-        return [part] + [from_behind(part, "tracer", d) for d in range(1, peers)]
-
-    tracers, transport = in_hbm(tracers), in_hbm(transport)
+        return [part] + [lax.ppermute(part, "tracer", [(i, i ^ d) for i in range(peers)]) for d in (1, 3, 2)]
+
     regions = send_pos.shape[0]
     *parts, exports, positions = call(
         functools.partial(first_kernel, block),
         "offer_first",
-        whole([in_hbm(export_rows), in_hbm(send_pos.transpose(1, 2, 0)), tracers], pl.ANY),
+        whole([in_hbm(export_rows), in_hbm(send_pos.transpose(1, 2, 0)), in_hbm(tracers)], pl.ANY),
         sends
         + [
             (SMEM((1, offered), jnp.int32), SMEM),
             (SMEM((near, reach, regions), jnp.int32), SMEM),
         ],
         scratch=[VMEM((width, rows), F32), pltpu.SemaphoreType.DMA((3,))],
+        flops=12 * row_flops * blocks,
     )
     halo = exchange(parts)
     state, low, early, table, cols = call(
         prepare_kernel,
         "prepare",
         whole([exports, positions], SMEM)
-        + whole([in_hbm(live_blocks), in_hbm(col_slot.T), tracers, transport], pl.ANY),
+        + whole([in_hbm(live_blocks), in_hbm(col_slot.T)], pl.ANY)
+        + whole([in_vmem(tracers), in_vmem(transport)]),
         [
             state_type,
             low_type,
@@ -485,20 +443,15 @@
         ],
         scratch=[
             SMEM((regions,), jnp.int32),
-            VMEM((width, rows), F32),
-            VMEM((offered, slots, block, block), BF16),
-            pltpu.SemaphoreType.DMA((3,)),
-            pltpu.SemaphoreType.DMA((offered,)),
+            SMEM((blocks,), jnp.int32),
+            SMEM((offered,), jnp.int32),
+            pltpu.SemaphoreType.DMA((2,)),
         ],
         flops=row_flops * blocks,
         moved=8 << 20,
     )
     turned = None
-    landing = [
-        VMEM((blocks - offered, slots, block, block), BF16),
-        pltpu.SemaphoreType.DMA((blocks - offered,)),
-        *[VMEM((2, slots, block, block), BF16)] * 2,
-    ]
+    staging = [VMEM((2, slots, block, block), BF16)] * 2
     scalars = whole([cols, table], SMEM)
     tracer_rows = [in_vmem(inverse), vmax.reshape(1, -1), half_sat.reshape(1, -1)]
     for cycle in range(CYCLES):
@@ -517,11 +470,11 @@
                 functools.partial(rest_kernel, first),
                 "rest_step",
                 scalars
-                + [(transport, pl.ANY) if first else (turned, VMEM)]
+                + [(in_vmem(transport) if first else turned, VMEM)]
                 + whole([low, state, *halo, exported]),
                 [state_type, low_type]
                 + ([kept((blocks - offered, *transport.shape[1:]), BF16)] if first else []),
-                scratch=[ext] + (landing if first else []),
+                scratch=[ext] + (staging if first else []),
                 flops=row_flops * blocks,
             )
             if first:

time: 92 us -> 86.4 us (0.939)
  Pallas kernels: 35.7 us -> 32.3 us
  starting transfers between devices: 37.2 us -> 34.1 us
  waiting for transfers between devices: 18.4 us -> 19.5 us
    pallas_call x15, Pallas kernels: 35.7 us -> 32.3 us  [call(): pl.pallas_call(kernel, in_specs=[spec(s) for _, s in args], out_specs=[sp...]
    ppermute x24, starting transfers between devices: 29.7 us -> 26.3 us  [exchange(): arrived.append(lax.ppermute(part, 'region', route))]
    ppermute x24, waiting for transfers between devices: 10.6 us -> 12.7 us  [exchange(): arrived.append(lax.ppermute(part, 'region', route))]
    ppermute x6, waiting for transfers between devices: 7.84 us -> 6.75 us  [across(): lax.ppermute(part, 'tracer', [(i, i ^ d) for i in range(peers)])]
  transfers between devices with their start and end apart: 30 -> 30, of which waited for: 13 -> 15; matrix products, arithmetic and copies ran while one was open for 0% -> 0% of each run, Pallas kernels for 22% -> 19%
where the time goes in v3:
time: 86.4 us; the launch traced here: 86.3 us
  starting transfers between devices  34.1 us (39%)
  Pallas kernels  32.3 us (37%)
  waiting for transfers between devices  19.5 us (23%)
    pallas_call x15, Pallas kernels, call(): pl.pallas_call(kernel, in_specs=[spec(s) for _, s in args], out_specs=[sp...  32.3 us
    ppermute x24, starting transfers between devices, exchange(): arrived.append(lax.ppermute(part, 'region', route))  26.3 us
    ppermute x24, waiting for transfers between devices, exchange(): arrived.append(lax.ppermute(part, 'region', route))  12.7 us
    ppermute x6, starting transfers between devices, across(): lax.ppermute(part, 'tracer', [(i, i ^ d) for i in range(peers)])  7.81 us
    ppermute x6, waiting for transfers between devices, across(): lax.ppermute(part, 'tracer', [(i, i ^ d) for i in range(peers)])  6.75 us
  transfers between devices with their start and end apart: 30, of which 15 were waited for; matrix products, arithmetic and copies ran while one was open for 0% of the time, Pallas kernels for 19%

profile of v3, /device:TPU:0, one launch (start us, length us, event | category | flops | bytes accessed | tf_op | source)
XLA Modules:
  0.0 86.3 jit_solution(10075003798482666741)
XLA Ops:
  0.0 1.6 %offer_first.1 = (bf16[4,64,128]{2,1,0:T(8,128)(2,1)S(1)}, bf16[4,64,128]{2,1,0:T(8,128)(2,1)S(1)}, bf16[4,64,128]{2,1,0:T(8,128)(2,1)S(1)}, bf16[4,64,128]{2,1,...) custom-call(s32[1,8]{1,0:T(1,128)} %export_rows.1, s32[4,4,32]{2,1,0:T(4,128)} %bitcast.11, ...), custom_call_target="tpu_custom_call" | custom-call | flops 12884901888 | bytes 1048576 | tf_op jit(solution)/shard_map/offer_first/pallas_call | solution.py:61
  1.6 6.7 %collective-permute-start = (bf16[4,64,128]{2,1,0:T(8,128)(2,1)S(1)}, bf16[4,64,128]{2,1,0:T(8,128)(2,1)S(1)}, u32[]{:S(2)}, u32[]{:S(2)}) collective-permute-start(bf16[4,64,128]{2,1,0:T(8,128)(2,1)S(1)} %get-tuple-element.62), channel_id=1, source_target_pairs={{0,120},{4,124},{8,16},{12,20},{16,8},{20,12},{24,32},{28,36},{32,... | collective-permute-start | bytes 196616 | tf_op jit(solution)/shard_map/ppermute | solution.py:44
  8.2 0.0 collective-permute-start.1
  8.2 0.0 collective-permute-start.2
  8.2 2.1 %collective-permute-start.3 = (bf16[4,64,128]{2,1,0:T(8,128)(2,1)S(1)}, bf16[4,64,128]{2,1,0:T(8,128)(2,1)S(1)}, u32[]{:S(2)}, u32[]{:S(2)}) collective-permute-start(bf16[4,64,128]{2,1,0:T(8,128)(2,1)S(1)} %get-tuple-element.65), channel_id=1, source_target_pairs={{0,4},{4,0},{8,12},{12,8},{16,20},{20,16},{24,28},{28,24},{32,36},... | collective-permute-start | bytes 196616 | tf_op jit(solution)/shard_map/ppermute | solution.py:44
  10.4 2.2 %prepare.1 = (f32[32,64,128]{2,1,0:T(8,128)S(1)}, bf16[32,64,128]{2,1,0:T(8,128)(2,1)S(1)}, bf16[8,16,128,128]{3,2,1,0:T(8,128)(2,1)S(1)}, s32[136]{0:T(256)S(4)}, s32[16,32]{1,0:T(8,128)S(4)}) custom-call(s32[1,8]{1,0:T(1,128)S(4)} %get-tuple-element.55.exports, s32[4,4,32]{2,1,0:T(4,128)S(4)} %get-tuple-element.56.positions, s32[32]{0:T(128)} %live.1, ...), custom_call_target="tpu_custom_call" | custom-call | flops 1073741824 | bytes 8388608 | tf_op jit(solution)/shard_map/prepare/pallas_call | solution.py:61
  12.5 0.0 collective-permute-done.refs_0_
  12.5 0.0 collective-permute-done.1.refs_1_
  12.6 2.7 %collective-permute-done.2.refs_2_ = bf16[4,64,128]{2,1,0:T(8,128)(2,1)S(1)} collective-permute-done((bf16[4,64,128]{2,1,0:T(8,128)(2,1)S(1)}, bf16[4,64,128]{2,1,0:T(8,128)(2,1)S(1)}, u32[]{:S(2)}, u32[]{:S(2)}) %collective-permute-start.2) | collective-permute-done | bytes 65568 | tf_op jit(solution)/shard_map/ppermute | solution.py:44
  15.2 0.0 collective-permute-done.3.refs_3_
  15.2 1.0 %export_step.4 = (f32[8,64,128]{2,1,0:T(8,128)S(1)}, bf16[4,64,128]{2,1,0:T(8,128)(2,1)S(1)}, bf16[4,64,128]{2,1,0:T(8,128)(2,1)S(1)}, bf16[4,64,128]{2,1,0:T(8,128)(2,1)S(1)}, bf16[4,64,128]{2,1,0:T(8,128)(2,1)S(1)}) custom-call(s32[16,32]{1,0:T(8,128)S(4)} %get-tuple-element.58.cols, s32[136]{0:T(256)S(4)} %get-tuple-element.57.table, ...), custom_call_target="tpu_custom_call" | custom-call | flops 268435456 | bytes 1048576 | tf_op jit(solution)/shard_map/export_step/pallas_call | solution.py:61
  16.2 0.8 collective-permute-start.4
  17.0 1.8 %collective-permute-start.6 = (bf16[4,64,128]{2,1,0:T(8,128)(2,1)S(1)}, bf16[4,64,128]{2,1,0:T(8,128)(2,1)S(1)}, u32[]{:S(2)}, u32[]{:S(2)}) collective-permute-start(bf16[4,64,128]{2,1,0:T(8,128)(2,1)S(1)} %get-tuple-element.72), channel_id=1, source_target_pairs={{0,124},{4,8},{8,4},{12,16},{16,12},{20,24},{24,20},{28,32},{32,28... | collective-permute-start | bytes 196616 | tf_op jit(solution)/shard_map/ppermute | solution.py:44
  18.8 0.4 collective-permute-start.7
  19.1 4.9 %rest_step.4 = (f32[32,64,128]{2,1,0:T(8,128)S(1)}, bf16[32,64,128]{2,1,0:T(8,128)(2,1)S(1)}, bf16[24,16,128,128]{3,2,1,0:T(8,128)(2,1)S(1)}) custom-call(s32[16,32]{1,0:T(8,128)S(4)} %get-tuple-element.58.cols, s32[136]{0:T(256)S(4)} %get-tuple-element.57.table, bf16[32,16,128,128]{3,2,1,0:T(8,128)(2,1)S(1)} %copy-done, ...), custom_call_target="tpu_custom_call" | custom-call | flops 1073741824 | bytes 1048576 | tf_op jit(solution)/shard_map/rest_step/pallas_call | solution.py:61
  24.0 0.5 collective-permute-done.4.refs_0_
  24.5 0.1 collective-permute-done.6.refs_2_
  24.6 0.0 collective-permute-done.7.refs_3_
  24.6 1.0 %export_step.5 = (f32[8,64,128]{2,1,0:T(8,128)S(1)}, bf16[4,64,128]{2,1,0:T(8,128)(2,1)S(1)}, bf16[4,64,128]{2,1,0:T(8,128)(2,1)S(1)}, bf16[4,64,128]{2,1,0:T(8,128)(2,1)S(1)}, bf16[4,64,128]{2,1,0:T(8,128)(2,1)S(1)}) custom-call(s32[16,32]{1,0:T(8,128)S(4)} %get-tuple-element.58.cols, s32[136]{0:T(256)S(4)} %get-tuple-element.57.table, ...), custom_call_target="tpu_custom_call" | custom-call | flops 268435456 | bytes 1048576 | tf_op jit(solution)/shard_map/export_step/pallas_call | solution.py:61
  25.6 1.6 %collective-permute-start.8 = (bf16[4,64,128]{2,1,0:T(8,128)(2,1)S(1)}, bf16[4,64,128]{2,1,0:T(8,128)(2,1)S(1)}, u32[]{:S(2)}, u32[]{:S(2)}) collective-permute-start(bf16[4,64,128]{2,1,0:T(8,128)(2,1)S(1)} %get-tuple-element.77), channel_id=1, source_target_pairs={{0,120},{4,124},{8,16},{12,20},{16,8},{20,12},{24,32},{28,36},{32,... | collective-permute-start | bytes 196616 | tf_op jit(solution)/shard_map/ppermute | solution.py:44
  27.2 2.8 %collective-permute-start.10 = (bf16[4,64,128]{2,1,0:T(8,128)(2,1)S(1)}, bf16[4,64,128]{2,1,0:T(8,128)(2,1)S(1)}, u32[]{:S(2)}, u32[]{:S(2)}) collective-permute-start(bf16[4,64,128]{2,1,0:T(8,128)(2,1)S(1)} %get-tuple-element.79), channel_id=1, source_target_pairs={{0,124},{4,8},{8,4},{12,16},{16,12},{20,24},{24,20},{28,32},{32,28... | collective-permute-start | bytes 196616 | tf_op jit(solution)/shard_map/ppermute | solution.py:44
  30.0 3.0 %rest_step.5 = (f32[32,64,128]{2,1,0:T(8,128)S(1)}, bf16[32,64,128]{2,1,0:T(8,128)(2,1)S(1)}) custom-call(s32[16,32]{1,0:T(8,128)S(4)} %get-tuple-element.58.cols, s32[136]{0:T(256)S(4)} %get-tuple-element.57.table, bf16[24,16,128,128]{3,2,1,0:T(8,128)(2,1)S(1)} %get-tuple-element.67.weights.turned, bf16[32,64,128]{2,1,0:T(8,128)(2,1)S(1)} %get-tuple-element.68.low, ...), custom_call_target="tpu_custom_call" | custom-call | flops 1073741824 | bytes 1048576 | tf_op jit(solution)/shard_map/rest_step/pallas_call | solution.py:61
  32.9 0.0 copy-start.1
  33.0 0.0 copy-start.3
  33.0 0.0 copy-start.4
  33.0 0.3 collective-permute-done.8.refs_0_
  33.3 0.0 collective-permute-done.9.refs_1_
  33.3 0.9 %collective-permute-done.10.refs_2_ = bf16[4,64,128]{2,1,0:T(8,128)(2,1)S(1)} collective-permute-done((bf16[4,64,128]{2,1,0:T(8,128)(2,1)S(1)}, bf16[4,64,128]{2,1,0:T(8,128)(2,1)S(1)}, u32[]{:S(2)}, u32[]{:S(2)}) %collective-permute-start.10) | collective-permute-done | bytes 65568 | tf_op jit(solution)/shard_map/ppermute | solution.py:44
  34.2 0.0 collective-permute-done.11.refs_3_
  34.2 4.1 %whole_step.2 = (f32[32,64,128]{2,1,0:T(8,128)S(1)}, f32[32,128]{1,0:T(8,128)S(1)}) custom-call(s32[16,32]{1,0:T(8,128)S(4)} %get-tuple-element.58.cols, s32[136]{0:T(256)S(4)} %get-tuple-element.57.table, bf16[8,16,128,128]{3,2,1,0:T(8,128)(2,1)S(1)} %get-tuple-element.59.early, bf16[24,16,128,128]{3,2,1,0:T(8,128)(2,1)S(1)} %get-tuple-element.67.weights.turned, ...), custom_call_target="tpu_custom_call" | custom-call | flops 1073741824 | bytes 1048576 | tf_op jit(solution)/shard_map/whole_step/pallas_call | solution.py:61
  38.3 3.1 %collective-permute-start.14 = (f32[32,128]{1,0:T(8,128)S(1)}, f32[32,128]{1,0:T(8,128)S(1)}, u32[]{:S(2)}, u32[]{:S(2)}) collective-permute-start(f32[32,128]{1,0:T(8,128)S(1)} %get-tuple-element.82.refs_0_), channel_id=1, source_target_pairs={{0,2},{1,3},{2,0},{3,1},{4,6},{5,7},{6,4},{7,5},{8,10},{9,11},{10,... | collective-permute-start | bytes 49160 | tf_op jit(solution)/shard_map/ppermute | solution.py:415
  41.4 1.1 %collective-permute-start.13 = (f32[32,128]{1,0:T(8,128)S(1)}, f32[32,128]{1,0:T(8,128)S(1)}, u32[]{:S(2)}, u32[]{:S(2)}) collective-permute-start(f32[32,128]{1,0:T(8,128)S(1)} %get-tuple-element.82.refs_0_), channel_id=1, source_target_pairs={{0,3},{1,2},{2,1},{3,0},{4,7},{5,6},{6,5},{7,4},{8,11},{9,10},{10,... | collective-permute-start | bytes 49160 | tf_op jit(solution)/shard_map/ppermute | solution.py:415
  42.5 1.1 %collective-permute-done.14.refs_3_ = f32[32,128]{1,0:T(8,128)S(1)} collective-permute-done((f32[32,128]{1,0:T(8,128)S(1)}, f32[32,128]{1,0:T(8,128)S(1)}, u32[]{:S(2)}, u32[]{:S(2)}) %collective-permute-start.14) | collective-permute-done | bytes 16416 | tf_op jit(solution)/shard_map/ppermute | solution.py:415
  43.6 2.7 %collective-permute-done.13.refs_2_ = f32[32,128]{1,0:T(8,128)S(1)} collective-permute-done((f32[32,128]{1,0:T(8,128)S(1)}, f32[32,128]{1,0:T(8,128)S(1)}, u32[]{:S(2)}, u32[]{:S(2)}) %collective-permute-start.13) | collective-permute-done | bytes 16416 | tf_op jit(solution)/shard_map/ppermute | solution.py:415
  46.3 0.0 collective-permute-done.12.refs_1_
  46.4 0.4 export_mix.1
  46.7 1.0 %collective-permute-start.15 = (bf16[4,64,128]{2,1,0:T(8,128)(2,1)S(1)}, bf16[4,64,128]{2,1,0:T(8,128)(2,1)S(1)}, u32[]{:S(2)}, u32[]{:S(2)}) collective-permute-start(bf16[4,64,128]{2,1,0:T(8,128)(2,1)S(1)} %get-tuple-element.85), channel_id=1, source_target_pairs={{0,120},{4,124},{8,16},{12,20},{16,8},{20,12},{24,32},{28,36},{32,... | collective-permute-start | bytes 196616 | tf_op jit(solution)/shard_map/ppermute | solution.py:44
  47.7 0.0 collective-permute-start.16
  47.7 1.6 %collective-permute-start.17 = (bf16[4,64,128]{2,1,0:T(8,128)(2,1)S(1)}, bf16[4,64,128]{2,1,0:T(8,128)(2,1)S(1)}, u32[]{:S(2)}, u32[]{:S(2)}) collective-permute-start(bf16[4,64,128]{2,1,0:T(8,128)(2,1)S(1)} %get-tuple-element.87), channel_id=1, source_target_pairs={{0,124},{4,8},{8,4},{12,16},{16,12},{20,24},{24,20},{28,32},{32,28... | collective-permute-start | bytes 196616 | tf_op jit(solution)/shard_map/ppermute | solution.py:44
  49.4 0.5 collective-permute-start.18
  49.9 0.9 %rest_mix.1 = (f32[32,64,128]{2,1,0:T(8,128)S(1)}, bf16[32,64,128]{2,1,0:T(8,128)(2,1)S(1)}) custom-call(s32[136]{0:T(256)S(4)} %get-tuple-element.57.table, f32[32,64,128]{2,1,0:T(8,128)S(1)} %get-tuple-element.81.state, bf16[32,128,128]{2,1,0:T(8,128)(2,1)S(1)} %copy-done.1, f32[1,64]{1,0:T(1,128)S(1)} %bitcast.5, f32[1,64]{1,0:T(1,128)S(1)} %bitcast.8, ...), custom_call_target="tpu_custom_call" | custom-call | flops 67108864 | bytes 1048576 | tf_op jit(solution)/shard_map/rest_mix/pallas_call | solution.py:61
  50.7 4.0 %collective-permute-done.15.refs_0_ = bf16[4,64,128]{2,1,0:T(8,128)(2,1)S(1)} collective-permute-done((bf16[4,64,128]{2,1,0:T(8,128)(2,1)S(1)}, bf16[4,64,128]{2,1,0:T(8,128)(2,1)S(1)}, u32[]{:S(2)}, u32[]{:S(2)}) %collective-permute-start.15) | collective-permute-done | bytes 65568 | tf_op jit(solution)/shard_map/ppermute | solution.py:44
  54.8 0.3 collective-permute-done.17.refs_2_
  55.1 1.0 %export_step.6 = (f32[8,64,128]{2,1,0:T(8,128)S(1)}, bf16[4,64,128]{2,1,0:T(8,128)(2,1)S(1)}, bf16[4,64,128]{2,1,0:T(8,128)(2,1)S(1)}, bf16[4,64,128]{2,1,0:T(8,128)(2,1)S(1)}, bf16[4,64,128]{2,1,0:T(8,128)(2,1)S(1)}) custom-call(s32[16,32]{1,0:T(8,128)S(4)} %get-tuple-element.58.cols, s32[136]{0:T(256)S(4)} %get-tuple-element.57.table, ...), custom_call_target="tpu_custom_call" | custom-call | flops 268435456 | bytes 1048576 | tf_op jit(solution)/shard_map/export_step/pallas_call | solution.py:61
  56.1 1.6 %collective-permute-start.19 = (bf16[4,64,128]{2,1,0:T(8,128)(2,1)S(1)}, bf16[4,64,128]{2,1,0:T(8,128)(2,1)S(1)}, u32[]{:S(2)}, u32[]{:S(2)}) collective-permute-start(bf16[4,64,128]{2,1,0:T(8,128)(2,1)S(1)} %get-tuple-element.92), channel_id=1, source_target_pairs={{0,120},{4,124},{8,16},{12,20},{16,8},{20,12},{24,32},{28,36},{32,... | collective-permute-start | bytes 196616 | tf_op jit(solution)/shard_map/ppermute | solution.py:44
  57.7 0.7 collective-permute-start.21
  58.4 1.4 %collective-permute-start.22 = (bf16[4,64,128]{2,1,0:T(8,128)(2,1)S(1)}, bf16[4,64,128]{2,1,0:T(8,128)(2,1)S(1)}, u32[]{:S(2)}, u32[]{:S(2)}) collective-permute-start(bf16[4,64,128]{2,1,0:T(8,128)(2,1)S(1)} %get-tuple-element.95), channel_id=1, source_target_pairs={{0,4},{4,0},{8,12},{12,8},{16,20},{20,16},{24,28},{28,24},{32,36},... | collective-permute-start | bytes 196616 | tf_op jit(solution)/shard_map/ppermute | solution.py:44
  59.8 3.0 %rest_step.6 = (f32[32,64,128]{2,1,0:T(8,128)S(1)}, bf16[32,64,128]{2,1,0:T(8,128)(2,1)S(1)}) custom-call(s32[16,32]{1,0:T(8,128)S(4)} %get-tuple-element.58.cols, s32[136]{0:T(256)S(4)} %get-tuple-element.57.table, bf16[24,16,128,128]{3,2,1,0:T(8,128)(2,1)S(1)} %get-tuple-element.67.weights.turned, bf16[32,64,128]{2,1,0:T(8,128)(2,1)S(1)} %get-tuple-element.83.low, ...), custom_call_target="tpu_custom_call" | custom-call | flops 1073741824 | bytes 1048576 | tf_op jit(solution)/shard_map/rest_step/pallas_call | solution.py:61
  62.8 1.0 %collective-permute-done.19.refs_0_ = bf16[4,64,128]{2,1,0:T(8,128)(2,1)S(1)} collective-permute-done((bf16[4,64,128]{2,1,0:T(8,128)(2,1)S(1)}, bf16[4,64,128]{2,1,0:T(8,128)(2,1)S(1)}, u32[]{:S(2)}, u32[]{:S(2)}) %collective-permute-start.19) | collective-permute-done | bytes 65568 | tf_op jit(solution)/shard_map/ppermute | solution.py:44
  63.8 0.9 %collective-permute-done.21.refs_2_ = bf16[4,64,128]{2,1,0:T(8,128)(2,1)S(1)} collective-permute-done((bf16[4,64,128]{2,1,0:T(8,128)(2,1)S(1)}, bf16[4,64,128]{2,1,0:T(8,128)(2,1)S(1)}, u32[]{:S(2)}, u32[]{:S(2)}) %collective-permute-start.21) | collective-permute-done | bytes 65568 | tf_op jit(solution)/shard_map/ppermute | solution.py:44
  64.7 1.0 %export_step.7 = (f32[8,64,128]{2,1,0:T(8,128)S(1)}, bf16[4,64,128]{2,1,0:T(8,128)(2,1)S(1)}, bf16[4,64,128]{2,1,0:T(8,128)(2,1)S(1)}, bf16[4,64,128]{2,1,0:T(8,128)(2,1)S(1)}, bf16[4,64,128]{2,1,0:T(8,128)(2,1)S(1)}) custom-call(s32[16,32]{1,0:T(8,128)S(4)} %get-tuple-element.58.cols, s32[136]{0:T(256)S(4)} %get-tuple-element.57.table, ...), custom_call_target="tpu_custom_call" | custom-call | flops 268435456 | bytes 1048576 | tf_op jit(solution)/shard_map/export_step/pallas_call | solution.py:61
  65.7 1.3 %collective-permute-start.23 = (bf16[4,64,128]{2,1,0:T(8,128)(2,1)S(1)}, bf16[4,64,128]{2,1,0:T(8,128)(2,1)S(1)}, u32[]{:S(2)}, u32[]{:S(2)}) collective-permute-start(bf16[4,64,128]{2,1,0:T(8,128)(2,1)S(1)} %get-tuple-element.99), channel_id=1, source_target_pairs={{0,120},{4,124},{8,16},{12,20},{16,8},{20,12},{24,32},{28,36},{32,... | collective-permute-start | bytes 196616 | tf_op jit(solution)/shard_map/ppermute | solution.py:44
  67.1 1.5 %collective-permute-start.25 = (bf16[4,64,128]{2,1,0:T(8,128)(2,1)S(1)}, bf16[4,64,128]{2,1,0:T(8,128)(2,1)S(1)}, u32[]{:S(2)}, u32[]{:S(2)}) collective-permute-start(bf16[4,64,128]{2,1,0:T(8,128)(2,1)S(1)} %get-tuple-element.101), channel_id=1, source_target_pairs={{0,124},{4,8},{8,4},{12,16},{16,12},{20,24},{24,20},{28,32},{32,28... | collective-permute-start | bytes 196616 | tf_op jit(solution)/shard_map/ppermute | solution.py:44
  68.6 0.6 collective-permute-start.26
  69.2 3.0 %rest_step.7 = (f32[32,64,128]{2,1,0:T(8,128)S(1)}, bf16[32,64,128]{2,1,0:T(8,128)(2,1)S(1)}) custom-call(s32[16,32]{1,0:T(8,128)S(4)} %get-tuple-element.58.cols, s32[136]{0:T(256)S(4)} %get-tuple-element.57.table, bf16[24,16,128,128]{3,2,1,0:T(8,128)(2,1)S(1)} %get-tuple-element.67.weights.turned, bf16[32,64,128]{2,1,0:T(8,128)(2,1)S(1)} %get-tuple-element.90.low, ...), custom_call_target="tpu_custom_call" | custom-call | flops 1073741824 | bytes 1048576 | tf_op jit(solution)/shard_map/rest_step/pallas_call | solution.py:61
  72.2 1.3 %collective-permute-done.23.refs_0_ = bf16[4,64,128]{2,1,0:T(8,128)(2,1)S(1)} collective-permute-done((bf16[4,64,128]{2,1,0:T(8,128)(2,1)S(1)}, bf16[4,64,128]{2,1,0:T(8,128)(2,1)S(1)}, u32[]{:S(2)}, u32[]{:S(2)}) %collective-permute-start.23) | collective-permute-done | bytes 65568 | tf_op jit(solution)/shard_map/ppermute | solution.py:44
  73.5 0.6 collective-permute-done.25.refs_2_
  74.1 3.9 %whole_step.3 = (f32[32,64,128]{2,1,0:T(8,128)S(1)}, f32[32,128]{1,0:T(8,128)S(1)}) custom-call(s32[16,32]{1,0:T(8,128)S(4)} %get-tuple-element.58.cols, s32[136]{0:T(256)S(4)} %get-tuple-element.57.table, bf16[8,16,128,128]{3,2,1,0:T(8,128)(2,1)S(1)} %get-tuple-element.59.early, bf16[24,16,128,128]{3,2,1,0:T(8,128)(2,1)S(1)} %get-tuple-element.67.weights.turned, ...), custom_call_target="tpu_custom_call" | custom-call | flops 1073741824 | bytes 1048576 | tf_op jit(solution)/shard_map/whole_step/pallas_call | solution.py:61
  78.0 1.6 %collective-permute-start.29 = (f32[32,128]{1,0:T(8,128)S(1)}, f32[32,128]{1,0:T(8,128)S(1)}, u32[]{:S(2)}, u32[]{:S(2)}) collective-permute-start(f32[32,128]{1,0:T(8,128)S(1)} %get-tuple-element.104.refs_0_), channel_id=1, source_target_pairs={{0,2},{1,3},{2,0},{3,1},{4,6},{5,7},{6,4},{7,5},{8,10},{9,11},{10,... | collective-permute-start | bytes 49160 | tf_op jit(solution)/shard_map/ppermute | solution.py:415
  79.5 1.1 %collective-permute-start.28 = (f32[32,128]{1,0:T(8,128)S(1)}, f32[32,128]{1,0:T(8,128)S(1)}, u32[]{:S(2)}, u32[]{:S(2)}) collective-permute-start(f32[32,128]{1,0:T(8,128)S(1)} %get-tuple-element.104.refs_0_), channel_id=1, source_target_pairs={{0,3},{1,2},{2,1},{3,0},{4,7},{5,6},{6,5},{7,4},{8,11},{9,10},{10,... | collective-permute-start | bytes 49160 | tf_op jit(solution)/shard_map/ppermute | solution.py:415
  80.7 0.9 %collective-permute-start.27 = (f32[32,128]{1,0:T(8,128)S(1)}, f32[32,128]{1,0:T(8,128)S(1)}, u32[]{:S(2)}, u32[]{:S(2)}) collective-permute-start(f32[32,128]{1,0:T(8,128)S(1)} %get-tuple-element.104.refs_0_), channel_id=1, source_target_pairs={{0,1},{1,0},{2,3},{3,2},{4,5},{5,4},{6,7},{7,6},{8,9},{9,8},{10,11... | collective-permute-start | bytes 49160 | tf_op jit(solution)/shard_map/ppermute | solution.py:415
  81.6 1.8 %collective-permute-done.29.refs_3_ = f32[32,128]{1,0:T(8,128)S(1)} collective-permute-done((f32[32,128]{1,0:T(8,128)S(1)}, f32[32,128]{1,0:T(8,128)S(1)}, u32[]{:S(2)}, u32[]{:S(2)}) %collective-permute-start.29) | collective-permute-done | bytes 16416 | tf_op jit(solution)/shard_map/ppermute | solution.py:415
  83.3 1.2 %collective-permute-done.28.refs_2_ = f32[32,128]{1,0:T(8,128)S(1)} collective-permute-done((f32[32,128]{1,0:T(8,128)S(1)}, f32[32,128]{1,0:T(8,128)S(1)}, u32[]{:S(2)}, u32[]{:S(2)}) %collective-permute-start.28) | collective-permute-done | bytes 16416 | tf_op jit(solution)/shard_map/ppermute | solution.py:415
  84.5 1.6 %last_mix.1 = f32[64,4096]{1,0:T(8,128)} custom-call(s32[136]{0:T(256)S(4)} %get-tuple-element.57.table, f32[32,64,128]{2,1,0:T(8,128)S(1)} %get-tuple-element.103.state, bf16[32,128,128]{2,1,0:T(8,128)(2,1)S(1)} %copy-done.1, f32[1,64]{1,0:T(1,128)S(1)} %bitcast.6, f32[1,64]{1,0:T(1,128)S(1)} %bitcast.9, f32[32,128]{1,0:T(8,128)S(1)} %get-tuple-element.104.refs_0_, ...), custom_call_target="tpu_custom_call" | custom-call | flops 67108864 | bytes 1048576 | tf_op jit(solution)/shard_map/last_mix/pallas_call | solution.py:61
  (21 shorter events, 0.1 us)
Async XLA Ops:
  0.0 10.4 %copy-start = (bf16[32,16,128,128]{3,2,1,0:T(8,128)(2,1)S(1)}, bf16[32,16,128,128]{3,2,1,0:T(8,128)(2,1)}, u32[]{:S(2)}) copy-start(bf16[32,16,128,128]{3,2,1,0:T(8,128)(2,1)} %weights.1) | copy-start | bytes 50331652
  0.0 10.4 %copy-start.2 = (f32[64,4096]{1,0:T(8,128)S(1)}, f32[64,4096]{1,0:T(8,128)}, u32[]{:S(2)}) copy-start(f32[64,4096]{1,0:T(8,128)} %tracers.3) | copy-start | bytes 3145732
  1.6 11.0 %collective-permute-start = (bf16[4,64,128]{2,1,0:T(8,128)(2,1)S(1)}, bf16[4,64,128]{2,1,0:T(8,128)(2,1)S(1)}, u32[]{:S(2)}, u32[]{:S(2)}) collective-permute-start(bf16[4,64,128]{2,1,0:T(8,128)(2,1)S(1)} %get-tuple-element.62), channel_id=1, source_target_pairs={{0,120},{4,124},{8,16},{12,20},{16,8},{20,12},{24,32},{28,36},{32,... | collective-permute-start | bytes 196616 | tf_op jit(solution)/shard_map/ppermute | solution.py:44
  8.2 4.3 %collective-permute-start.1 = (bf16[4,64,128]{2,1,0:T(8,128)(2,1)S(1)}, bf16[4,64,128]{2,1,0:T(8,128)(2,1)S(1)}, u32[]{:S(2)}, u32[]{:S(2)}) collective-permute-start(bf16[4,64,128]{2,1,0:T(8,128)(2,1)S(1)} %get-tuple-element.63), channel_id=1, source_target_pairs={{0,8},{4,12},{8,0},{12,4},{16,24},{20,28},{24,16},{28,20},{32,40},... | collective-permute-start | bytes 196616 | tf_op jit(solution)/shard_map/ppermute | solution.py:44
  8.2 7.0 %collective-permute-start.2 = (bf16[4,64,128]{2,1,0:T(8,128)(2,1)S(1)}, bf16[4,64,128]{2,1,0:T(8,128)(2,1)S(1)}, u32[]{:S(2)}, u32[]{:S(2)}) collective-permute-start(bf16[4,64,128]{2,1,0:T(8,128)(2,1)S(1)} %get-tuple-element.64), channel_id=1, source_target_pairs={{0,124},{4,8},{8,4},{12,16},{16,12},{20,24},{24,20},{28,32},{32,28... | collective-permute-start | bytes 196616 | tf_op jit(solution)/shard_map/ppermute | solution.py:44
  8.2 7.0 %collective-permute-start.3 = (bf16[4,64,128]{2,1,0:T(8,128)(2,1)S(1)}, bf16[4,64,128]{2,1,0:T(8,128)(2,1)S(1)}, u32[]{:S(2)}, u32[]{:S(2)}) collective-permute-start(bf16[4,64,128]{2,1,0:T(8,128)(2,1)S(1)} %get-tuple-element.65), channel_id=1, source_target_pairs={{0,4},{4,0},{8,12},{12,8},{16,20},{20,16},{24,28},{28,24},{32,36},... | collective-permute-start | bytes 196616 | tf_op jit(solution)/shard_map/ppermute | solution.py:44
  16.2 8.3 %collective-permute-start.4 = (bf16[4,64,128]{2,1,0:T(8,128)(2,1)S(1)}, bf16[4,64,128]{2,1,0:T(8,128)(2,1)S(1)}, u32[]{:S(2)}, u32[]{:S(2)}) collective-permute-start(bf16[4,64,128]{2,1,0:T(8,128)(2,1)S(1)} %get-tuple-element.70), channel_id=1, source_target_pairs={{0,120},{4,124},{8,16},{12,20},{16,8},{20,12},{24,32},{28,36},{32,... | collective-permute-start | bytes 196616 | tf_op jit(solution)/shard_map/ppermute | solution.py:44
  17.0 7.5 %collective-permute-start.5 = (bf16[4,64,128]{2,1,0:T(8,128)(2,1)S(1)}, bf16[4,64,128]{2,1,0:T(8,128)(2,1)S(1)}, u32[]{:S(2)}, u32[]{:S(2)}) collective-permute-start(bf16[4,64,128]{2,1,0:T(8,128)(2,1)S(1)} %get-tuple-element.71), channel_id=1, source_target_pairs={{0,8},{4,12},{8,0},{12,4},{16,24},{20,28},{24,16},{28,20},{32,40},... | collective-permute-start | bytes 196616 | tf_op jit(solution)/shard_map/ppermute | solution.py:44
  17.0 7.6 %collective-permute-start.6 = (bf16[4,64,128]{2,1,0:T(8,128)(2,1)S(1)}, bf16[4,64,128]{2,1,0:T(8,128)(2,1)S(1)}, u32[]{:S(2)}, u32[]{:S(2)}) collective-permute-start(bf16[4,64,128]{2,1,0:T(8,128)(2,1)S(1)} %get-tuple-element.72), channel_id=1, source_target_pairs={{0,124},{4,8},{8,4},{12,16},{16,12},{20,24},{24,20},{28,32},{32,28... | collective-permute-start | bytes 196616 | tf_op jit(solution)/shard_map/ppermute | solution.py:44
  18.8 5.8 %collective-permute-start.7 = (bf16[4,64,128]{2,1,0:T(8,128)(2,1)S(1)}, bf16[4,64,128]{2,1,0:T(8,128)(2,1)S(1)}, u32[]{:S(2)}, u32[]{:S(2)}) collective-permute-start(bf16[4,64,128]{2,1,0:T(8,128)(2,1)S(1)} %get-tuple-element.73), channel_id=1, source_target_pairs={{0,4},{4,0},{8,12},{12,8},{16,20},{20,16},{24,28},{28,24},{32,36},... | collective-permute-start | bytes 196616 | tf_op jit(solution)/shard_map/ppermute | solution.py:44
  25.6 7.7 %collective-permute-start.8 = (bf16[4,64,128]{2,1,0:T(8,128)(2,1)S(1)}, bf16[4,64,128]{2,1,0:T(8,128)(2,1)S(1)}, u32[]{:S(2)}, u32[]{:S(2)}) collective-permute-start(bf16[4,64,128]{2,1,0:T(8,128)(2,1)S(1)} %get-tuple-element.77), channel_id=1, source_target_pairs={{0,120},{4,124},{8,16},{12,20},{16,8},{20,12},{24,32},{28,36},{32,... | collective-permute-start | bytes 196616 | tf_op jit(solution)/shard_map/ppermute | solution.py:44
  27.2 6.1 %collective-permute-start.9 = (bf16[4,64,128]{2,1,0:T(8,128)(2,1)S(1)}, bf16[4,64,128]{2,1,0:T(8,128)(2,1)S(1)}, u32[]{:S(2)}, u32[]{:S(2)}) collective-permute-start(bf16[4,64,128]{2,1,0:T(8,128)(2,1)S(1)} %get-tuple-element.78), channel_id=1, source_target_pairs={{0,8},{4,12},{8,0},{12,4},{16,24},{20,28},{24,16},{28,20},{32,40},... | collective-permute-start | bytes 196616 | tf_op jit(solution)/shard_map/ppermute | solution.py:44
  27.2 7.0 %collective-permute-start.10 = (bf16[4,64,128]{2,1,0:T(8,128)(2,1)S(1)}, bf16[4,64,128]{2,1,0:T(8,128)(2,1)S(1)}, u32[]{:S(2)}, u32[]{:S(2)}) collective-permute-start(bf16[4,64,128]{2,1,0:T(8,128)(2,1)S(1)} %get-tuple-element.79), channel_id=1, source_target_pairs={{0,124},{4,8},{8,4},{12,16},{16,12},{20,24},{24,20},{28,32},{32,28... | collective-permute-start | bytes 196616 | tf_op jit(solution)/shard_map/ppermute | solution.py:44
  30.0 4.3 %collective-permute-start.11 = (bf16[4,64,128]{2,1,0:T(8,128)(2,1)S(1)}, bf16[4,64,128]{2,1,0:T(8,128)(2,1)S(1)}, u32[]{:S(2)}, u32[]{:S(2)}) collective-permute-start(bf16[4,64,128]{2,1,0:T(8,128)(2,1)S(1)} %get-tuple-element.80), channel_id=1, source_target_pairs={{0,4},{4,0},{8,12},{12,8},{16,20},{20,16},{24,28},{28,24},{32,36},... | collective-permute-start | bytes 196616 | tf_op jit(solution)/shard_map/ppermute | solution.py:44
  32.9 13.4 %copy-start.1 = (bf16[32,128,128]{2,1,0:T(8,128)(2,1)S(1)}, bf16[32,128,128]{2,1,0:T(8,128)(2,1)}, u32[]{:S(2)}) copy-start(bf16[32,128,128]{2,1,0:T(8,128)(2,1)} %inverse.5) | copy-start | bytes 3145732
  33.0 13.4 %copy-start.3 = (f32[64]{0:T(128)S(1)}, f32[64]{0:T(128)}, u32[]{:S(2)}) copy-start(f32[64]{0:T(128)} %param.16) | copy-start | bytes 772
  33.0 13.4 %copy-start.4 = (f32[64]{0:T(128)S(1)}, f32[64]{0:T(128)}, u32[]{:S(2)}) copy-start(f32[64]{0:T(128)} %param.17) | copy-start | bytes 772
  38.3 5.3 %collective-permute-start.14 = (f32[32,128]{1,0:T(8,128)S(1)}, f32[32,128]{1,0:T(8,128)S(1)}, u32[]{:S(2)}, u32[]{:S(2)}) collective-permute-start(f32[32,128]{1,0:T(8,128)S(1)} %get-tuple-element.82.refs_0_), channel_id=1, source_target_pairs={{0,2},{1,3},{2,0},{3,1},{4,6},{5,7},{6,4},{7,5},{8,10},{9,11},{10,... | collective-permute-start | bytes 49160 | tf_op jit(solution)/shard_map/ppermute | solution.py:415
  41.4 4.9 %collective-permute-start.13 = (f32[32,128]{1,0:T(8,128)S(1)}, f32[32,128]{1,0:T(8,128)S(1)}, u32[]{:S(2)}, u32[]{:S(2)}) collective-permute-start(f32[32,128]{1,0:T(8,128)S(1)} %get-tuple-element.82.refs_0_), channel_id=1, source_target_pairs={{0,3},{1,2},{2,1},{3,0},{4,7},{5,6},{6,5},{7,4},{8,11},{9,10},{10,... | collective-permute-start | bytes 49160 | tf_op jit(solution)/shard_map/ppermute | solution.py:415
  42.5 3.8 %collective-permute-start.12 = (f32[32,128]{1,0:T(8,128)S(1)}, f32[32,128]{1,0:T(8,128)S(1)}, u32[]{:S(2)}, u32[]{:S(2)}) collective-permute-start(f32[32,128]{1,0:T(8,128)S(1)} %get-tuple-element.82.refs_0_), channel_id=1, source_target_pairs={{0,1},{1,0},{2,3},{3,2},{4,5},{5,4},{6,7},{7,6},{8,9},{9,8},{10,11... | collective-permute-start | bytes 49160 | tf_op jit(solution)/shard_map/ppermute | solution.py:415
  46.7 8.0 %collective-permute-start.15 = (bf16[4,64,128]{2,1,0:T(8,128)(2,1)S(1)}, bf16[4,64,128]{2,1,0:T(8,128)(2,1)S(1)}, u32[]{:S(2)}, u32[]{:S(2)}) collective-permute-start(bf16[4,64,128]{2,1,0:T(8,128)(2,1)S(1)} %get-tuple-element.85), channel_id=1, source_target_pairs={{0,120},{4,124},{8,16},{12,20},{16,8},{20,12},{24,32},{28,36},{32,... | collective-permute-start | bytes 196616 | tf_op jit(solution)/shard_map/ppermute | solution.py:44
  47.7 7.1 %collective-permute-start.16 = (bf16[4,64,128]{2,1,0:T(8,128)(2,1)S(1)}, bf16[4,64,128]{2,1,0:T(8,128)(2,1)S(1)}, u32[]{:S(2)}, u32[]{:S(2)}) collective-permute-start(bf16[4,64,128]{2,1,0:T(8,128)(2,1)S(1)} %get-tuple-element.86), channel_id=1, source_target_pairs={{0,8},{4,12},{8,0},{12,4},{16,24},{20,28},{24,16},{28,20},{32,40},... | collective-permute-start | bytes 196616 | tf_op jit(solution)/shard_map/ppermute | solution.py:44
  47.7 7.4 %collective-permute-start.17 = (bf16[4,64,128]{2,1,0:T(8,128)(2,1)S(1)}, bf16[4,64,128]{2,1,0:T(8,128)(2,1)S(1)}, u32[]{:S(2)}, u32[]{:S(2)}) collective-permute-start(bf16[4,64,128]{2,1,0:T(8,128)(2,1)S(1)} %get-tuple-element.87), channel_id=1, source_target_pairs={{0,124},{4,8},{8,4},{12,16},{16,12},{20,24},{24,20},{28,32},{32,28... | collective-permute-start | bytes 196616 | tf_op jit(solution)/shard_map/ppermute | solution.py:44
  49.4 5.7 %collective-permute-start.18 = (bf16[4,64,128]{2,1,0:T(8,128)(2,1)S(1)}, bf16[4,64,128]{2,1,0:T(8,128)(2,1)S(1)}, u32[]{:S(2)}, u32[]{:S(2)}) collective-permute-start(bf16[4,64,128]{2,1,0:T(8,128)(2,1)S(1)} %get-tuple-element.88), channel_id=1, source_target_pairs={{0,4},{4,0},{8,12},{12,8},{16,20},{20,16},{24,28},{28,24},{32,36},... | collective-permute-start | bytes 196616 | tf_op jit(solution)/shard_map/ppermute | solution.py:44
  56.1 7.7 %collective-permute-start.19 = (bf16[4,64,128]{2,1,0:T(8,128)(2,1)S(1)}, bf16[4,64,128]{2,1,0:T(8,128)(2,1)S(1)}, u32[]{:S(2)}, u32[]{:S(2)}) collective-permute-start(bf16[4,64,128]{2,1,0:T(8,128)(2,1)S(1)} %get-tuple-element.92), channel_id=1, source_target_pairs={{0,120},{4,124},{8,16},{12,20},{16,8},{20,12},{24,32},{28,36},{32,... | collective-permute-start | bytes 196616 | tf_op jit(solution)/shard_map/ppermute | solution.py:44
  57.7 6.1 %collective-permute-start.20 = (bf16[4,64,128]{2,1,0:T(8,128)(2,1)S(1)}, bf16[4,64,128]{2,1,0:T(8,128)(2,1)S(1)}, u32[]{:S(2)}, u32[]{:S(2)}) collective-permute-start(bf16[4,64,128]{2,1,0:T(8,128)(2,1)S(1)} %get-tuple-element.93), channel_id=1, source_target_pairs={{0,8},{4,12},{8,0},{12,4},{16,24},{20,28},{24,16},{28,20},{32,40},... | collective-permute-start | bytes 196616 | tf_op jit(solution)/shard_map/ppermute | solution.py:44
  57.7 7.0 %collective-permute-start.21 = (bf16[4,64,128]{2,1,0:T(8,128)(2,1)S(1)}, bf16[4,64,128]{2,1,0:T(8,128)(2,1)S(1)}, u32[]{:S(2)}, u32[]{:S(2)}) collective-permute-start(bf16[4,64,128]{2,1,0:T(8,128)(2,1)S(1)} %get-tuple-element.94), channel_id=1, source_target_pairs={{0,124},{4,8},{8,4},{12,16},{16,12},{20,24},{24,20},{28,32},{32,28... | collective-permute-start | bytes 196616 | tf_op jit(solution)/shard_map/ppermute | solution.py:44
  58.4 6.3 %collective-permute-start.22 = (bf16[4,64,128]{2,1,0:T(8,128)(2,1)S(1)}, bf16[4,64,128]{2,1,0:T(8,128)(2,1)S(1)}, u32[]{:S(2)}, u32[]{:S(2)}) collective-permute-start(bf16[4,64,128]{2,1,0:T(8,128)(2,1)S(1)} %get-tuple-element.95), channel_id=1, source_target_pairs={{0,4},{4,0},{8,12},{12,8},{16,20},{20,16},{24,28},{28,24},{32,36},... | collective-permute-start | bytes 196616 | tf_op jit(solution)/shard_map/ppermute | solution.py:44
  65.7 7.7 %collective-permute-start.23 = (bf16[4,64,128]{2,1,0:T(8,128)(2,1)S(1)}, bf16[4,64,128]{2,1,0:T(8,128)(2,1)S(1)}, u32[]{:S(2)}, u32[]{:S(2)}) collective-permute-start(bf16[4,64,128]{2,1,0:T(8,128)(2,1)S(1)} %get-tuple-element.99), channel_id=1, source_target_pairs={{0,120},{4,124},{8,16},{12,20},{16,8},{20,12},{24,32},{28,36},{32,... | collective-permute-start | bytes 196616 | tf_op jit(solution)/shard_map/ppermute | solution.py:44
  67.1 6.4 %collective-permute-start.24 = (bf16[4,64,128]{2,1,0:T(8,128)(2,1)S(1)}, bf16[4,64,128]{2,1,0:T(8,128)(2,1)S(1)}, u32[]{:S(2)}, u32[]{:S(2)}) collective-permute-start(bf16[4,64,128]{2,1,0:T(8,128)(2,1)S(1)} %get-tuple-element.100), channel_id=1, source_target_pairs={{0,8},{4,12},{8,0},{12,4},{16,24},{20,28},{24,16},{28,20},{32,40},... | collective-permute-start | bytes 196616 | tf_op jit(solution)/shard_map/ppermute | solution.py:44
  67.1 7.0 %collective-permute-start.25 = (bf16[4,64,128]{2,1,0:T(8,128)(2,1)S(1)}, bf16[4,64,128]{2,1,0:T(8,128)(2,1)S(1)}, u32[]{:S(2)}, u32[]{:S(2)}) collective-permute-start(bf16[4,64,128]{2,1,0:T(8,128)(2,1)S(1)} %get-tuple-element.101), channel_id=1, source_target_pairs={{0,124},{4,8},{8,4},{12,16},{16,12},{20,24},{24,20},{28,32},{32,28... | collective-permute-start | bytes 196616 | tf_op jit(solution)/shard_map/ppermute | solution.py:44
  68.6 5.5 %collective-permute-start.26 = (bf16[4,64,128]{2,1,0:T(8,128)(2,1)S(1)}, bf16[4,64,128]{2,1,0:T(8,128)(2,1)S(1)}, u32[]{:S(2)}, u32[]{:S(2)}) collective-permute-start(bf16[4,64,128]{2,1,0:T(8,128)(2,1)S(1)} %get-tuple-element.102), channel_id=1, source_target_pairs={{0,4},{4,0},{8,12},{12,8},{16,20},{20,16},{24,28},{28,24},{32,36},... | collective-permute-start | bytes 196616 | tf_op jit(solution)/shard_map/ppermute | solution.py:44
  78.0 5.3 %collective-permute-start.29 = (f32[32,128]{1,0:T(8,128)S(1)}, f32[32,128]{1,0:T(8,128)S(1)}, u32[]{:S(2)}, u32[]{:S(2)}) collective-permute-start(f32[32,128]{1,0:T(8,128)S(1)} %get-tuple-element.104.refs_0_), channel_id=1, source_target_pairs={{0,2},{1,3},{2,0},{3,1},{4,6},{5,7},{6,4},{7,5},{8,10},{9,11},{10,... | collective-permute-start | bytes 49160 | tf_op jit(solution)/shard_map/ppermute | solution.py:415
  79.5 4.9 %collective-permute-start.28 = (f32[32,128]{1,0:T(8,128)S(1)}, f32[32,128]{1,0:T(8,128)S(1)}, u32[]{:S(2)}, u32[]{:S(2)}) collective-permute-start(f32[32,128]{1,0:T(8,128)S(1)} %get-tuple-element.104.refs_0_), channel_id=1, source_target_pairs={{0,3},{1,2},{2,1},{3,0},{4,7},{5,6},{6,5},{7,4},{8,11},{9,10},{10,... | collective-permute-start | bytes 49160 | tf_op jit(solution)/shard_map/ppermute | solution.py:415
  80.7 3.8 %collective-permute-start.27 = (f32[32,128]{1,0:T(8,128)S(1)}, f32[32,128]{1,0:T(8,128)S(1)}, u32[]{:S(2)}, u32[]{:S(2)}) collective-permute-start(f32[32,128]{1,0:T(8,128)S(1)} %get-tuple-element.104.refs_0_), channel_id=1, source_target_pairs={{0,1},{1,0},{2,3},{3,2},{4,5},{5,4},{6,7},{7,6},{8,9},{9,8},{10,11... | collective-permute-start | bytes 49160 | tf_op jit(solution)/shard_map/ppermute | solution.py:415

commit v4 on v3

--- a/solution.py
+++ b/solution.py
@@ -346,28 +346,43 @@
     return jnp.sum(jnp.where(there, row, 0.0), axis=1, keepdims=True)
 
 
-def mixed_block(value, shade, vmax, half_sat, inverse):
+def uptake_kernel(state, vmax_row, half_row, uptakes):
+    vmax = column_of(vmax_row[...])
+    half_sat = column_of(half_row[...])
+    for b in range(state.shape[0]):
+        uptakes[b] = uptake_of(state[b], vmax, half_sat)
+
+
+def uptake_of(value, vmax, half_sat):
+    return vmax * value / (half_sat + jnp.abs(value))
+
+
+def mixed_block(value, shade, uptake, inverse):
     level = lax.rem(lax.broadcasted_iota(jnp.int32, shade.shape, 1), LEVPAD)
     light = jnp.exp(-level.astype(F32) / LEVELS)
-    uptake = vmax * (light / (1.0 + shade)) * value / (half_sat + jnp.abs(value))
-    pre = (value - uptake).astype(BF16)
+    pre = (value - light / (1.0 + shade) * uptake).astype(BF16)
     return lax.dot_general(pre, inverse, (((1,), (1,)), ((), ())), preferred_element_type=F32)
 
 
-def implicit_kernel(kind, peers, table, state, inverse, vmax_row, half_row, *refs):
+def implicit_kernel(kind, peers, table, state, inverse, *refs):
+    if kind == "last":
+        uptakes, *refs = refs
+    else:
+        vmax, half_sat = column_of(refs[0][...]), column_of(refs[1][...])
+        refs = refs[2:]
     parts, outs = refs[:peers], refs[peers:]
     total = parts[0][...]
     for p in parts[1:]:
         total = total + p[...]
     total = total / (16.0 * NTR)
-    vmax = column_of(vmax_row[...])
-    half_sat = column_of(half_row[...])
     if kind == "export":
         *sends, mixes, shade = outs
         shade[...] = total
         for e in range(mixes.shape[0]):
             b = table[EXPORTS + e]
-            mixed = mixed_block(state[b], shade[pl.ds(b, 1), :], vmax, half_sat, inverse[b])
+            mixed = mixed_block(
+                state[b], shade[pl.ds(b, 1), :], uptake_of(state[b], vmax, half_sat), inverse[b]
+            )
             mixes[e] = (row_mask(b, table[LIVE], mixed.shape) * mixed).astype(BF16)
         reach = sends[0].shape[0]
         for link, part in enumerate(sends):
@@ -377,7 +392,8 @@
     blocks, _, block = state.shape
     copies = []
     for b in range(blocks):
-        mixed = mixed_block(state[b], total[b : b + 1], vmax, half_sat, inverse[b])
+        uptake = uptakes[b] if kind == "last" else uptake_of(state[b], vmax, half_sat)
+        mixed = mixed_block(state[b], total[b : b + 1], uptake, inverse[b])
         mixed = row_mask(b, table[LIVE], mixed.shape) * mixed
         if kind == "rest":
             outs[0][b] = mixed
@@ -453,7 +469,7 @@
     turned = None
     staging = [VMEM((2, slots, block, block), BF16)] * 2
     scalars = whole([cols, table], SMEM)
-    tracer_rows = [in_vmem(inverse), vmax.reshape(1, -1), half_sat.reshape(1, -1)]
+    tracer_rows = [vmax.reshape(1, -1), half_sat.reshape(1, -1)]
     for cycle in range(CYCLES):
         for step in range(2):
             exported, *parts = call(
@@ -488,7 +504,13 @@
             scratch=[ext],
             flops=row_flops * blocks,
         )
-        operands = [(table, SMEM)] + whole([state, *tracer_rows, *across(part)])
+        shades = across(part)
+        uptakes = tracer_rows
+        if cycle == CYCLES - 1:
+            uptakes = call(
+                uptake_kernel, "uptake", whole([state, *tracer_rows]), [state_type], moved=2 << 20
+            )
+        operands = [(table, SMEM)] + whole([state, in_vmem(inverse), *uptakes, *shades])
         if cycle == CYCLES - 1:
             (out,) = call(
                 functools.partial(implicit_kernel, "last", peers),

time: 86.4 us -> 86.7 us (level)
  Pallas kernels: 32.3 us -> 23.9 us
  waiting for transfers between devices: 19.5 us -> 25.8 us
  starting transfers between devices: 34.1 us -> 36.3 us
    pallas_call x15 -> x16, Pallas kernels: 32.3 us -> 23.9 us  [call(): pl.pallas_call(kernel, in_specs=[spec(s) for _, s in args], out_specs=[sp...]
    ppermute x24, waiting for transfers between devices: 12.7 us -> 19.3 us  [exchange(): arrived.append(lax.ppermute(part, 'region', route))]
    ppermute x24, starting transfers between devices: 26.3 us -> 28.5 us  [exchange(): arrived.append(lax.ppermute(part, 'region', route))]
  transfers between devices with their start and end apart: 30 -> 30, of which waited for: 15 -> 14; matrix products, arithmetic and copies ran while one was open for 0% -> 0% of each run, Pallas kernels for 19% -> 13%
where the time goes in v4:
time: 86.7 us; the launch traced here: 86.4 us
  starting transfers between devices  36.3 us (42%)
  waiting for transfers between devices  25.8 us (30%)
  Pallas kernels  23.9 us (28%)
    ppermute x24, starting transfers between devices, exchange(): arrived.append(lax.ppermute(part, 'region', route))  28.5 us
    pallas_call x16, Pallas kernels, call(): pl.pallas_call(kernel, in_specs=[spec(s) for _, s in args], out_specs=[sp...  23.9 us
    ppermute x24, waiting for transfers between devices, exchange(): arrived.append(lax.ppermute(part, 'region', route))  19.3 us
    ppermute x6, starting transfers between devices, across(): lax.ppermute(part, 'tracer', [(i, i ^ d) for i in range(peers)])  7.82 us
    ppermute x6, waiting for transfers between devices, across(): lax.ppermute(part, 'tracer', [(i, i ^ d) for i in range(peers)])  6.41 us
  transfers between devices with their start and end apart: 30, of which 14 were waited for; matrix products, arithmetic and copies ran while one was open for 0% of the time, Pallas kernels for 13%

profile of v4, /device:TPU:0, one launch (start us, length us, event | category | flops | bytes accessed | tf_op | source)
XLA Modules:
  0.0 86.4 jit_solution(16191397514480557174)
XLA Ops:
  0.0 1.6 %offer_first.1 = (bf16[4,64,128]{2,1,0:T(8,128)(2,1)S(1)}, bf16[4,64,128]{2,1,0:T(8,128)(2,1)S(1)}, bf16[4,64,128]{2,1,0:T(8,128)(2,1)S(1)}, bf16[4,64,128]{2,1,...) custom-call(s32[1,8]{1,0:T(1,128)} %export_rows.1, s32[4,4,32]{2,1,0:T(4,128)} %bitcast.11, ...), custom_call_target="tpu_custom_call" | custom-call | flops 12884901888 | bytes 1048576 | tf_op jit(solution)/shard_map/offer_first/pallas_call | solution.py:61
  1.6 6.7 %collective-permute-start = (bf16[4,64,128]{2,1,0:T(8,128)(2,1)S(1)}, bf16[4,64,128]{2,1,0:T(8,128)(2,1)S(1)}, u32[]{:S(2)}, u32[]{:S(2)}) collective-permute-start(bf16[4,64,128]{2,1,0:T(8,128)(2,1)S(1)} %get-tuple-element.62), channel_id=1, source_target_pairs={{0,120},{4,124},{8,16},{12,20},{16,8},{20,12},{24,32},{28,36},{32,... | collective-permute-start | bytes 196616 | tf_op jit(solution)/shard_map/ppermute | solution.py:44
  8.2 0.0 collective-permute-start.1
  8.2 0.0 collective-permute-start.2
  8.2 2.1 %collective-permute-start.3 = (bf16[4,64,128]{2,1,0:T(8,128)(2,1)S(1)}, bf16[4,64,128]{2,1,0:T(8,128)(2,1)S(1)}, u32[]{:S(2)}, u32[]{:S(2)}) collective-permute-start(bf16[4,64,128]{2,1,0:T(8,128)(2,1)S(1)} %get-tuple-element.65), channel_id=1, source_target_pairs={{0,4},{4,0},{8,12},{12,8},{16,20},{20,16},{24,28},{28,24},{32,36},... | collective-permute-start | bytes 196616 | tf_op jit(solution)/shard_map/ppermute | solution.py:44
  10.4 2.2 %prepare.1 = (f32[32,64,128]{2,1,0:T(8,128)S(1)}, bf16[32,64,128]{2,1,0:T(8,128)(2,1)S(1)}, bf16[8,16,128,128]{3,2,1,0:T(8,128)(2,1)S(1)}, s32[136]{0:T(256)S(4)}, s32[16,32]{1,0:T(8,128)S(4)}) custom-call(s32[1,8]{1,0:T(1,128)S(4)} %get-tuple-element.55.exports, s32[4,4,32]{2,1,0:T(4,128)S(4)} %get-tuple-element.56.positions, s32[32]{0:T(128)} %live.1, ...), custom_call_target="tpu_custom_call" | custom-call | flops 1073741824 | bytes 8388608 | tf_op jit(solution)/shard_map/prepare/pallas_call | solution.py:61
  12.5 0.0 collective-permute-done.refs_0_
  12.5 0.0 collective-permute-done.1.refs_1_
  12.6 2.7 %collective-permute-done.2.refs_2_ = bf16[4,64,128]{2,1,0:T(8,128)(2,1)S(1)} collective-permute-done((bf16[4,64,128]{2,1,0:T(8,128)(2,1)S(1)}, bf16[4,64,128]{2,1,0:T(8,128)(2,1)S(1)}, u32[]{:S(2)}, u32[]{:S(2)}) %collective-permute-start.2) | collective-permute-done | bytes 65568 | tf_op jit(solution)/shard_map/ppermute | solution.py:44
  15.2 1.0 %export_step.4 = (f32[8,64,128]{2,1,0:T(8,128)S(1)}, bf16[4,64,128]{2,1,0:T(8,128)(2,1)S(1)}, bf16[4,64,128]{2,1,0:T(8,128)(2,1)S(1)}, bf16[4,64,128]{2,1,0:T(8,128)(2,1)S(1)}, bf16[4,64,128]{2,1,0:T(8,128)(2,1)S(1)}) custom-call(s32[16,32]{1,0:T(8,128)S(4)} %get-tuple-element.58.cols, s32[136]{0:T(256)S(4)} %get-tuple-element.57.table, ...), custom_call_target="tpu_custom_call" | custom-call | flops 268435456 | bytes 1048576 | tf_op jit(solution)/shard_map/export_step/pallas_call | solution.py:61
  16.3 0.7 collective-permute-start.4
  17.0 0.0 collective-permute-start.5
  17.0 1.8 %collective-permute-start.6 = (bf16[4,64,128]{2,1,0:T(8,128)(2,1)S(1)}, bf16[4,64,128]{2,1,0:T(8,128)(2,1)S(1)}, u32[]{:S(2)}, u32[]{:S(2)}) collective-permute-start(bf16[4,64,128]{2,1,0:T(8,128)(2,1)S(1)} %get-tuple-element.72), channel_id=1, source_target_pairs={{0,124},{4,8},{8,4},{12,16},{16,12},{20,24},{24,20},{28,32},{32,28... | collective-permute-start | bytes 196616 | tf_op jit(solution)/shard_map/ppermute | solution.py:44
  18.8 0.4 collective-permute-start.7
  19.1 2.7 %rest_step.4 = (f32[32,64,128]{2,1,0:T(8,128)S(1)}, bf16[32,64,128]{2,1,0:T(8,128)(2,1)S(1)}, bf16[24,16,128,128]{3,2,1,0:T(8,128)(2,1)S(1)}) custom-call(s32[16,32]{1,0:T(8,128)S(4)} %get-tuple-element.58.cols, s32[136]{0:T(256)S(4)} %get-tuple-element.57.table, bf16[32,16,128,128]{3,2,1,0:T(8,128)(2,1)S(1)} %copy-done, ...), custom_call_target="tpu_custom_call" | custom-call | flops 1073741824 | bytes 1048576 | tf_op jit(solution)/shard_map/rest_step/pallas_call | solution.py:61
  21.8 2.7 %collective-permute-done.4.refs_0_ = bf16[4,64,128]{2,1,0:T(8,128)(2,1)S(1)} collective-permute-done((bf16[4,64,128]{2,1,0:T(8,128)(2,1)S(1)}, bf16[4,64,128]{2,1,0:T(8,128)(2,1)S(1)}, u32[]{:S(2)}, u32[]{:S(2)}) %collective-permute-start.4) | collective-permute-done | bytes 65568 | tf_op jit(solution)/shard_map/ppermute | solution.py:44
  24.5 0.0 collective-permute-done.5.refs_1_
  24.5 0.1 collective-permute-done.6.refs_2_
  24.6 0.0 collective-permute-done.7.refs_3_
  24.6 1.0 %export_step.5 = (f32[8,64,128]{2,1,0:T(8,128)S(1)}, bf16[4,64,128]{2,1,0:T(8,128)(2,1)S(1)}, bf16[4,64,128]{2,1,0:T(8,128)(2,1)S(1)}, bf16[4,64,128]{2,1,0:T(8,128)(2,1)S(1)}, bf16[4,64,128]{2,1,0:T(8,128)(2,1)S(1)}) custom-call(s32[16,32]{1,0:T(8,128)S(4)} %get-tuple-element.58.cols, s32[136]{0:T(256)S(4)} %get-tuple-element.57.table, ...), custom_call_target="tpu_custom_call" | custom-call | flops 268435456 | bytes 1048576 | tf_op jit(solution)/shard_map/export_step/pallas_call | solution.py:61
  25.6 2.8 %collective-permute-start.8 = (bf16[4,64,128]{2,1,0:T(8,128)(2,1)S(1)}, bf16[4,64,128]{2,1,0:T(8,128)(2,1)S(1)}, u32[]{:S(2)}, u32[]{:S(2)}) collective-permute-start(bf16[4,64,128]{2,1,0:T(8,128)(2,1)S(1)} %get-tuple-element.77), channel_id=1, source_target_pairs={{0,120},{4,124},{8,16},{12,20},{16,8},{20,12},{24,32},{28,36},{32,... | collective-permute-start | bytes 196616 | tf_op jit(solution)/shard_map/ppermute | solution.py:44
  28.5 2.5 %collective-permute-start.10 = (bf16[4,64,128]{2,1,0:T(8,128)(2,1)S(1)}, bf16[4,64,128]{2,1,0:T(8,128)(2,1)S(1)}, u32[]{:S(2)}, u32[]{:S(2)}) collective-permute-start(bf16[4,64,128]{2,1,0:T(8,128)(2,1)S(1)} %get-tuple-element.79), channel_id=1, source_target_pairs={{0,124},{4,8},{8,4},{12,16},{16,12},{20,24},{24,20},{28,32},{32,28... | collective-permute-start | bytes 196616 | tf_op jit(solution)/shard_map/ppermute | solution.py:44
  30.9 0.0 collective-permute-start.11
  30.9 1.7 %rest_step.5 = (f32[32,64,128]{2,1,0:T(8,128)S(1)}, bf16[32,64,128]{2,1,0:T(8,128)(2,1)S(1)}) custom-call(s32[16,32]{1,0:T(8,128)S(4)} %get-tuple-element.58.cols, s32[136]{0:T(256)S(4)} %get-tuple-element.57.table, bf16[24,16,128,128]{3,2,1,0:T(8,128)(2,1)S(1)} %get-tuple-element.67.weights.turned, bf16[32,64,128]{2,1,0:T(8,128)(2,1)S(1)} %get-tuple-element.68.low, ...), custom_call_target="tpu_custom_call" | custom-call | flops 1073741824 | bytes 1048576 | tf_op jit(solution)/shard_map/rest_step/pallas_call | solution.py:61
  32.6 0.0 copy-start.1
  32.6 0.0 copy-start.3
  32.6 0.0 copy-start.4
  32.7 0.7 collective-permute-done.8.refs_0_
  33.3 2.2 %collective-permute-done.10.refs_2_ = bf16[4,64,128]{2,1,0:T(8,128)(2,1)S(1)} collective-permute-done((bf16[4,64,128]{2,1,0:T(8,128)(2,1)S(1)}, bf16[4,64,128]{2,1,0:T(8,128)(2,1)S(1)}, u32[]{:S(2)}, u32[]{:S(2)}) %collective-permute-start.10) | collective-permute-done | bytes 65568 | tf_op jit(solution)/shard_map/ppermute | solution.py:44
  35.5 2.7 %whole_step.2 = (f32[32,64,128]{2,1,0:T(8,128)S(1)}, f32[32,128]{1,0:T(8,128)S(1)}) custom-call(s32[16,32]{1,0:T(8,128)S(4)} %get-tuple-element.58.cols, s32[136]{0:T(256)S(4)} %get-tuple-element.57.table, bf16[8,16,128,128]{3,2,1,0:T(8,128)(2,1)S(1)} %get-tuple-element.59.early, bf16[24,16,128,128]{3,2,1,0:T(8,128)(2,1)S(1)} %get-tuple-element.67.weights.turned, ...), custom_call_target="tpu_custom_call" | custom-call | flops 1073741824 | bytes 1048576 | tf_op jit(solution)/shard_map/whole_step/pallas_call | solution.py:61
  38.2 3.1 %collective-permute-start.14 = (f32[32,128]{1,0:T(8,128)S(1)}, f32[32,128]{1,0:T(8,128)S(1)}, u32[]{:S(2)}, u32[]{:S(2)}) collective-permute-start(f32[32,128]{1,0:T(8,128)S(1)} %get-tuple-element.82.refs_2_), channel_id=1, source_target_pairs={{0,2},{1,3},{2,0},{3,1},{4,6},{5,7},{6,4},{7,5},{8,10},{9,11},{10,... | collective-permute-start | bytes 49160 | tf_op jit(solution)/shard_map/ppermute | solution.py:431
  41.4 1.1 %collective-permute-start.13 = (f32[32,128]{1,0:T(8,128)S(1)}, f32[32,128]{1,0:T(8,128)S(1)}, u32[]{:S(2)}, u32[]{:S(2)}) collective-permute-start(f32[32,128]{1,0:T(8,128)S(1)} %get-tuple-element.82.refs_2_), channel_id=1, source_target_pairs={{0,3},{1,2},{2,1},{3,0},{4,7},{5,6},{6,5},{7,4},{8,11},{9,10},{10,... | collective-permute-start | bytes 49160 | tf_op jit(solution)/shard_map/ppermute | solution.py:431
  42.5 1.2 %collective-permute-done.14.refs_5_ = f32[32,128]{1,0:T(8,128)S(1)} collective-permute-done((f32[32,128]{1,0:T(8,128)S(1)}, f32[32,128]{1,0:T(8,128)S(1)}, u32[]{:S(2)}, u32[]{:S(2)}) %collective-permute-start.14) | collective-permute-done | bytes 16416 | tf_op jit(solution)/shard_map/ppermute | solution.py:431
  43.7 2.6 %collective-permute-done.13.refs_4_ = f32[32,128]{1,0:T(8,128)S(1)} collective-permute-done((f32[32,128]{1,0:T(8,128)S(1)}, f32[32,128]{1,0:T(8,128)S(1)}, u32[]{:S(2)}, u32[]{:S(2)}) %collective-permute-start.13) | collective-permute-done | bytes 16416 | tf_op jit(solution)/shard_map/ppermute | solution.py:431
  46.3 0.0 collective-permute-done.12.refs_3_
  46.3 0.4 export_mix.1
  46.7 2.9 %collective-permute-start.15 = (bf16[4,64,128]{2,1,0:T(8,128)(2,1)S(1)}, bf16[4,64,128]{2,1,0:T(8,128)(2,1)S(1)}, u32[]{:S(2)}, u32[]{:S(2)}) collective-permute-start(bf16[4,64,128]{2,1,0:T(8,128)(2,1)S(1)} %get-tuple-element.85), channel_id=1, source_target_pairs={{0,120},{4,124},{8,16},{12,20},{16,8},{20,12},{24,32},{28,36},{32,... | collective-permute-start | bytes 196616 | tf_op jit(solution)/shard_map/ppermute | solution.py:44
  49.6 0.0 collective-permute-start.16
  49.6 2.1 %collective-permute-start.18 = (bf16[4,64,128]{2,1,0:T(8,128)(2,1)S(1)}, bf16[4,64,128]{2,1,0:T(8,128)(2,1)S(1)}, u32[]{:S(2)}, u32[]{:S(2)}) collective-permute-start(bf16[4,64,128]{2,1,0:T(8,128)(2,1)S(1)} %get-tuple-element.88), channel_id=1, source_target_pairs={{0,4},{4,0},{8,12},{12,8},{16,20},{20,16},{24,28},{28,24},{32,36},... | collective-permute-start | bytes 196616 | tf_op jit(solution)/shard_map/ppermute | solution.py:44
  51.7 0.9 %rest_mix.1 = (f32[32,64,128]{2,1,0:T(8,128)S(1)}, bf16[32,64,128]{2,1,0:T(8,128)(2,1)S(1)}) custom-call(s32[136]{0:T(256)S(4)} %get-tuple-element.57.table, f32[32,64,128]{2,1,0:T(8,128)S(1)} %get-tuple-element.81.state, bf16[32,128,128]{2,1,0:T(8,128)(2,1)S(1)} %copy-done.1, f32[1,64]{1,0:T(1,128)S(1)} %bitcast.5, f32[1,64]{1,0:T(1,128)S(1)} %bitcast.8, ...), custom_call_target="tpu_custom_call" | custom-call | flops 67108864 | bytes 1048576 | tf_op jit(solution)/shard_map/rest_mix/pallas_call | solution.py:61
  52.6 1.7 %collective-permute-done.15.refs_0_ = bf16[4,64,128]{2,1,0:T(8,128)(2,1)S(1)} collective-permute-done((bf16[4,64,128]{2,1,0:T(8,128)(2,1)S(1)}, bf16[4,64,128]{2,1,0:T(8,128)(2,1)S(1)}, u32[]{:S(2)}, u32[]{:S(2)}) %collective-permute-start.15) | collective-permute-done | bytes 65568 | tf_op jit(solution)/shard_map/ppermute | solution.py:44
  54.4 2.2 %collective-permute-done.17.refs_2_ = bf16[4,64,128]{2,1,0:T(8,128)(2,1)S(1)} collective-permute-done((bf16[4,64,128]{2,1,0:T(8,128)(2,1)S(1)}, bf16[4,64,128]{2,1,0:T(8,128)(2,1)S(1)}, u32[]{:S(2)}, u32[]{:S(2)}) %collective-permute-start.17) | collective-permute-done | bytes 65568 | tf_op jit(solution)/shard_map/ppermute | solution.py:44
  56.6 1.0 %export_step.6 = (f32[8,64,128]{2,1,0:T(8,128)S(1)}, bf16[4,64,128]{2,1,0:T(8,128)(2,1)S(1)}, bf16[4,64,128]{2,1,0:T(8,128)(2,1)S(1)}, bf16[4,64,128]{2,1,0:T(8,128)(2,1)S(1)}, bf16[4,64,128]{2,1,0:T(8,128)(2,1)S(1)}) custom-call(s32[16,32]{1,0:T(8,128)S(4)} %get-tuple-element.58.cols, s32[136]{0:T(256)S(4)} %get-tuple-element.57.table, ...), custom_call_target="tpu_custom_call" | custom-call | flops 268435456 | bytes 1048576 | tf_op jit(solution)/shard_map/export_step/pallas_call | solution.py:61
  57.6 0.7 collective-permute-start.19
  58.3 2.0 %collective-permute-start.21 = (bf16[4,64,128]{2,1,0:T(8,128)(2,1)S(1)}, bf16[4,64,128]{2,1,0:T(8,128)(2,1)S(1)}, u32[]{:S(2)}, u32[]{:S(2)}) collective-permute-start(bf16[4,64,128]{2,1,0:T(8,128)(2,1)S(1)} %get-tuple-element.94), channel_id=1, source_target_pairs={{0,124},{4,8},{8,4},{12,16},{16,12},{20,24},{24,20},{28,32},{32,28... | collective-permute-start | bytes 196616 | tf_op jit(solution)/shard_map/ppermute | solution.py:44
  60.2 0.2 collective-permute-start.22
  60.4 1.7 %rest_step.6 = (f32[32,64,128]{2,1,0:T(8,128)S(1)}, bf16[32,64,128]{2,1,0:T(8,128)(2,1)S(1)}) custom-call(s32[16,32]{1,0:T(8,128)S(4)} %get-tuple-element.58.cols, s32[136]{0:T(256)S(4)} %get-tuple-element.57.table, bf16[24,16,128,128]{3,2,1,0:T(8,128)(2,1)S(1)} %get-tuple-element.67.weights.turned, bf16[32,64,128]{2,1,0:T(8,128)(2,1)S(1)} %get-tuple-element.83.low, ...), custom_call_target="tpu_custom_call" | custom-call | flops 1073741824 | bytes 1048576 | tf_op jit(solution)/shard_map/rest_step/pallas_call | solution.py:61
  62.1 3.8 %collective-permute-done.19.refs_0_ = bf16[4,64,128]{2,1,0:T(8,128)(2,1)S(1)} collective-permute-done((bf16[4,64,128]{2,1,0:T(8,128)(2,1)S(1)}, bf16[4,64,128]{2,1,0:T(8,128)(2,1)S(1)}, u32[]{:S(2)}, u32[]{:S(2)}) %collective-permute-start.19) | collective-permute-done | bytes 65568 | tf_op jit(solution)/shard_map/ppermute | solution.py:44
  66.0 0.0 collective-permute-done.21.refs_2_
  66.0 1.0 %export_step.7 = (f32[8,64,128]{2,1,0:T(8,128)S(1)}, bf16[4,64,128]{2,1,0:T(8,128)(2,1)S(1)}, bf16[4,64,128]{2,1,0:T(8,128)(2,1)S(1)}, bf16[4,64,128]{2,1,0:T(8,128)(2,1)S(1)}, bf16[4,64,128]{2,1,0:T(8,128)(2,1)S(1)}) custom-call(s32[16,32]{1,0:T(8,128)S(4)} %get-tuple-element.58.cols, s32[136]{0:T(256)S(4)} %get-tuple-element.57.table, ...), custom_call_target="tpu_custom_call" | custom-call | flops 268435456 | bytes 1048576 | tf_op jit(solution)/shard_map/export_step/pallas_call | solution.py:61
  67.0 1.6 %collective-permute-start.23 = (bf16[4,64,128]{2,1,0:T(8,128)(2,1)S(1)}, bf16[4,64,128]{2,1,0:T(8,128)(2,1)S(1)}, u32[]{:S(2)}, u32[]{:S(2)}) collective-permute-start(bf16[4,64,128]{2,1,0:T(8,128)(2,1)S(1)} %get-tuple-element.99), channel_id=1, source_target_pairs={{0,120},{4,124},{8,16},{12,20},{16,8},{20,12},{24,32},{28,36},{32,... | collective-permute-start | bytes 196616 | tf_op jit(solution)/shard_map/ppermute | solution.py:44
  68.6 1.8 %collective-permute-start.25 = (bf16[4,64,128]{2,1,0:T(8,128)(2,1)S(1)}, bf16[4,64,128]{2,1,0:T(8,128)(2,1)S(1)}, u32[]{:S(2)}, u32[]{:S(2)}) collective-permute-start(bf16[4,64,128]{2,1,0:T(8,128)(2,1)S(1)} %get-tuple-element.101), channel_id=1, source_target_pairs={{0,124},{4,8},{8,4},{12,16},{16,12},{20,24},{24,20},{28,32},{32,28... | collective-permute-start | bytes 196616 | tf_op jit(solution)/shard_map/ppermute | solution.py:44
  70.4 0.3 collective-permute-start.26
  70.7 1.7 %rest_step.7 = (f32[32,64,128]{2,1,0:T(8,128)S(1)}, bf16[32,64,128]{2,1,0:T(8,128)(2,1)S(1)}) custom-call(s32[16,32]{1,0:T(8,128)S(4)} %get-tuple-element.58.cols, s32[136]{0:T(256)S(4)} %get-tuple-element.57.table, bf16[24,16,128,128]{3,2,1,0:T(8,128)(2,1)S(1)} %get-tuple-element.67.weights.turned, bf16[32,64,128]{2,1,0:T(8,128)(2,1)S(1)} %get-tuple-element.90.low, ...), custom_call_target="tpu_custom_call" | custom-call | flops 1073741824 | bytes 1048576 | tf_op jit(solution)/shard_map/rest_step/pallas_call | solution.py:61
  72.4 2.3 %collective-permute-done.23.refs_0_ = bf16[4,64,128]{2,1,0:T(8,128)(2,1)S(1)} collective-permute-done((bf16[4,64,128]{2,1,0:T(8,128)(2,1)S(1)}, bf16[4,64,128]{2,1,0:T(8,128)(2,1)S(1)}, u32[]{:S(2)}, u32[]{:S(2)}) %collective-permute-start.23) | collective-permute-done | bytes 65568 | tf_op jit(solution)/shard_map/ppermute | solution.py:44
  74.7 0.9 %collective-permute-done.25.refs_2_ = bf16[4,64,128]{2,1,0:T(8,128)(2,1)S(1)} collective-permute-done((bf16[4,64,128]{2,1,0:T(8,128)(2,1)S(1)}, bf16[4,64,128]{2,1,0:T(8,128)(2,1)S(1)}, u32[]{:S(2)}, u32[]{:S(2)}) %collective-permute-start.25) | collective-permute-done | bytes 65568 | tf_op jit(solution)/shard_map/ppermute | solution.py:44
  75.6 2.6 %whole_step.3 = (f32[32,64,128]{2,1,0:T(8,128)S(1)}, f32[32,128]{1,0:T(8,128)S(1)}) custom-call(s32[16,32]{1,0:T(8,128)S(4)} %get-tuple-element.58.cols, s32[136]{0:T(256)S(4)} %get-tuple-element.57.table, bf16[8,16,128,128]{3,2,1,0:T(8,128)(2,1)S(1)} %get-tuple-element.59.early, bf16[24,16,128,128]{3,2,1,0:T(8,128)(2,1)S(1)} %get-tuple-element.67.weights.turned, ...), custom_call_target="tpu_custom_call" | custom-call | flops 1073741824 | bytes 1048576 | tf_op jit(solution)/shard_map/whole_step/pallas_call | solution.py:61
  78.2 1.5 %collective-permute-start.29 = (f32[32,128]{1,0:T(8,128)S(1)}, f32[32,128]{1,0:T(8,128)S(1)}, u32[]{:S(2)}, u32[]{:S(2)}) collective-permute-start(f32[32,128]{1,0:T(8,128)S(1)} %get-tuple-element.104.refs_1_), channel_id=1, source_target_pairs={{0,2},{1,3},{2,0},{3,1},{4,6},{5,7},{6,4},{7,5},{8,10},{9,11},{10,... | collective-permute-start | bytes 49160 | tf_op jit(solution)/shard_map/ppermute | solution.py:431
  79.7 1.1 %collective-permute-start.28 = (f32[32,128]{1,0:T(8,128)S(1)}, f32[32,128]{1,0:T(8,128)S(1)}, u32[]{:S(2)}, u32[]{:S(2)}) collective-permute-start(f32[32,128]{1,0:T(8,128)S(1)} %get-tuple-element.104.refs_1_), channel_id=1, source_target_pairs={{0,3},{1,2},{2,1},{3,0},{4,7},{5,6},{6,5},{7,4},{8,11},{9,10},{10,... | collective-permute-start | bytes 49160 | tf_op jit(solution)/shard_map/ppermute | solution.py:431
  80.8 0.9 %collective-permute-start.27 = (f32[32,128]{1,0:T(8,128)S(1)}, f32[32,128]{1,0:T(8,128)S(1)}, u32[]{:S(2)}, u32[]{:S(2)}) collective-permute-start(f32[32,128]{1,0:T(8,128)S(1)} %get-tuple-element.104.refs_1_), channel_id=1, source_target_pairs={{0,1},{1,0},{2,3},{3,2},{4,5},{5,4},{6,7},{7,6},{8,9},{9,8},{10,11... | collective-permute-start | bytes 49160 | tf_op jit(solution)/shard_map/ppermute | solution.py:431
  81.7 0.3 uptake.1.refs_0_
  82.0 1.4 %collective-permute-done.29.refs_4_ = f32[32,128]{1,0:T(8,128)S(1)} collective-permute-done((f32[32,128]{1,0:T(8,128)S(1)}, f32[32,128]{1,0:T(8,128)S(1)}, u32[]{:S(2)}, u32[]{:S(2)}) %collective-permute-start.29) | collective-permute-done | bytes 16416 | tf_op jit(solution)/shard_map/ppermute | solution.py:431
  83.5 1.2 %collective-permute-done.28.refs_3_ = f32[32,128]{1,0:T(8,128)S(1)} collective-permute-done((f32[32,128]{1,0:T(8,128)S(1)}, f32[32,128]{1,0:T(8,128)S(1)}, u32[]{:S(2)}, u32[]{:S(2)}) %collective-permute-start.28) | collective-permute-done | bytes 16416 | tf_op jit(solution)/shard_map/ppermute | solution.py:431
  84.6 1.6 %last_mix.1 = f32[64,4096]{1,0:T(8,128)} custom-call(s32[136]{0:T(256)S(4)} %get-tuple-element.57.table, f32[32,64,128]{2,1,0:T(8,128)S(1)} %get-tuple-element.103.state, bf16[32,128,128]{2,1,0:T(8,128)(2,1)S(1)} %copy-done.1, f32[32,64,128]{2,1,0:T(8,128)S(1)} %uptake.1.refs_0_, f32[32,128]{1,0:T(8,128)S(1)} %get-tuple-element.104.refs_1_, ...), custom_call_target="tpu_custom_call" | custom-call | flops 67108864 | bytes 1048576 | tf_op jit(solution)/shard_map/last_mix/pallas_call | solution.py:61
  (22 shorter events, 0.1 us)
Async XLA Ops:
  0.0 10.4 %copy-start = (bf16[32,16,128,128]{3,2,1,0:T(8,128)(2,1)S(1)}, bf16[32,16,128,128]{3,2,1,0:T(8,128)(2,1)}, u32[]{:S(2)}) copy-start(bf16[32,16,128,128]{3,2,1,0:T(8,128)(2,1)} %weights.1) | copy-start | bytes 50331652
  0.0 10.4 %copy-start.2 = (f32[64,4096]{1,0:T(8,128)S(1)}, f32[64,4096]{1,0:T(8,128)}, u32[]{:S(2)}) copy-start(f32[64,4096]{1,0:T(8,128)} %tracers.3) | copy-start | bytes 3145732
  1.6 11.0 %collective-permute-start = (bf16[4,64,128]{2,1,0:T(8,128)(2,1)S(1)}, bf16[4,64,128]{2,1,0:T(8,128)(2,1)S(1)}, u32[]{:S(2)}, u32[]{:S(2)}) collective-permute-start(bf16[4,64,128]{2,1,0:T(8,128)(2,1)S(1)} %get-tuple-element.62), channel_id=1, source_target_pairs={{0,120},{4,124},{8,16},{12,20},{16,8},{20,12},{24,32},{28,36},{32,... | collective-permute-start | bytes 196616 | tf_op jit(solution)/shard_map/ppermute | solution.py:44
  8.2 4.3 %collective-permute-start.1 = (bf16[4,64,128]{2,1,0:T(8,128)(2,1)S(1)}, bf16[4,64,128]{2,1,0:T(8,128)(2,1)S(1)}, u32[]{:S(2)}, u32[]{:S(2)}) collective-permute-start(bf16[4,64,128]{2,1,0:T(8,128)(2,1)S(1)} %get-tuple-element.63), channel_id=1, source_target_pairs={{0,8},{4,12},{8,0},{12,4},{16,24},{20,28},{24,16},{28,20},{32,40},... | collective-permute-start | bytes 196616 | tf_op jit(solution)/shard_map/ppermute | solution.py:44
  8.2 7.0 %collective-permute-start.2 = (bf16[4,64,128]{2,1,0:T(8,128)(2,1)S(1)}, bf16[4,64,128]{2,1,0:T(8,128)(2,1)S(1)}, u32[]{:S(2)}, u32[]{:S(2)}) collective-permute-start(bf16[4,64,128]{2,1,0:T(8,128)(2,1)S(1)} %get-tuple-element.64), channel_id=1, source_target_pairs={{0,124},{4,8},{8,4},{12,16},{16,12},{20,24},{24,20},{28,32},{32,28... | collective-permute-start | bytes 196616 | tf_op jit(solution)/shard_map/ppermute | solution.py:44
  8.2 7.0 %collective-permute-start.3 = (bf16[4,64,128]{2,1,0:T(8,128)(2,1)S(1)}, bf16[4,64,128]{2,1,0:T(8,128)(2,1)S(1)}, u32[]{:S(2)}, u32[]{:S(2)}) collective-permute-start(bf16[4,64,128]{2,1,0:T(8,128)(2,1)S(1)} %get-tuple-element.65), channel_id=1, source_target_pairs={{0,4},{4,0},{8,12},{12,8},{16,20},{20,16},{24,28},{28,24},{32,36},... | collective-permute-start | bytes 196616 | tf_op jit(solution)/shard_map/ppermute | solution.py:44
  16.3 8.3 %collective-permute-start.4 = (bf16[4,64,128]{2,1,0:T(8,128)(2,1)S(1)}, bf16[4,64,128]{2,1,0:T(8,128)(2,1)S(1)}, u32[]{:S(2)}, u32[]{:S(2)}) collective-permute-start(bf16[4,64,128]{2,1,0:T(8,128)(2,1)S(1)} %get-tuple-element.70), channel_id=1, source_target_pairs={{0,120},{4,124},{8,16},{12,20},{16,8},{20,12},{24,32},{28,36},{32,... | collective-permute-start | bytes 196616 | tf_op jit(solution)/shard_map/ppermute | solution.py:44
  17.0 7.5 %collective-permute-start.5 = (bf16[4,64,128]{2,1,0:T(8,128)(2,1)S(1)}, bf16[4,64,128]{2,1,0:T(8,128)(2,1)S(1)}, u32[]{:S(2)}, u32[]{:S(2)}) collective-permute-start(bf16[4,64,128]{2,1,0:T(8,128)(2,1)S(1)} %get-tuple-element.71), channel_id=1, source_target_pairs={{0,8},{4,12},{8,0},{12,4},{16,24},{20,28},{24,16},{28,20},{32,40},... | collective-permute-start | bytes 196616 | tf_op jit(solution)/shard_map/ppermute | solution.py:44
  17.0 7.6 %collective-permute-start.6 = (bf16[4,64,128]{2,1,0:T(8,128)(2,1)S(1)}, bf16[4,64,128]{2,1,0:T(8,128)(2,1)S(1)}, u32[]{:S(2)}, u32[]{:S(2)}) collective-permute-start(bf16[4,64,128]{2,1,0:T(8,128)(2,1)S(1)} %get-tuple-element.72), channel_id=1, source_target_pairs={{0,124},{4,8},{8,4},{12,16},{16,12},{20,24},{24,20},{28,32},{32,28... | collective-permute-start | bytes 196616 | tf_op jit(solution)/shard_map/ppermute | solution.py:44
  18.8 5.8 %collective-permute-start.7 = (bf16[4,64,128]{2,1,0:T(8,128)(2,1)S(1)}, bf16[4,64,128]{2,1,0:T(8,128)(2,1)S(1)}, u32[]{:S(2)}, u32[]{:S(2)}) collective-permute-start(bf16[4,64,128]{2,1,0:T(8,128)(2,1)S(1)} %get-tuple-element.73), channel_id=1, source_target_pairs={{0,4},{4,0},{8,12},{12,8},{16,20},{20,16},{24,28},{28,24},{32,36},... | collective-permute-start | bytes 196616 | tf_op jit(solution)/shard_map/ppermute | solution.py:44
  25.6 7.7 %collective-permute-start.8 = (bf16[4,64,128]{2,1,0:T(8,128)(2,1)S(1)}, bf16[4,64,128]{2,1,0:T(8,128)(2,1)S(1)}, u32[]{:S(2)}, u32[]{:S(2)}) collective-permute-start(bf16[4,64,128]{2,1,0:T(8,128)(2,1)S(1)} %get-tuple-element.77), channel_id=1, source_target_pairs={{0,120},{4,124},{8,16},{12,20},{16,8},{20,12},{24,32},{28,36},{32,... | collective-permute-start | bytes 196616 | tf_op jit(solution)/shard_map/ppermute | solution.py:44
  28.5 4.8 %collective-permute-start.9 = (bf16[4,64,128]{2,1,0:T(8,128)(2,1)S(1)}, bf16[4,64,128]{2,1,0:T(8,128)(2,1)S(1)}, u32[]{:S(2)}, u32[]{:S(2)}) collective-permute-start(bf16[4,64,128]{2,1,0:T(8,128)(2,1)S(1)} %get-tuple-element.78), channel_id=1, source_target_pairs={{0,8},{4,12},{8,0},{12,4},{16,24},{20,28},{24,16},{28,20},{32,40},... | collective-permute-start | bytes 196616 | tf_op jit(solution)/shard_map/ppermute | solution.py:44
  28.5 7.0 %collective-permute-start.10 = (bf16[4,64,128]{2,1,0:T(8,128)(2,1)S(1)}, bf16[4,64,128]{2,1,0:T(8,128)(2,1)S(1)}, u32[]{:S(2)}, u32[]{:S(2)}) collective-permute-start(bf16[4,64,128]{2,1,0:T(8,128)(2,1)S(1)} %get-tuple-element.79), channel_id=1, source_target_pairs={{0,124},{4,8},{8,4},{12,16},{16,12},{20,24},{24,20},{28,32},{32,28... | collective-permute-start | bytes 196616 | tf_op jit(solution)/shard_map/ppermute | solution.py:44
  30.9 4.6 %collective-permute-start.11 = (bf16[4,64,128]{2,1,0:T(8,128)(2,1)S(1)}, bf16[4,64,128]{2,1,0:T(8,128)(2,1)S(1)}, u32[]{:S(2)}, u32[]{:S(2)}) collective-permute-start(bf16[4,64,128]{2,1,0:T(8,128)(2,1)S(1)} %get-tuple-element.80), channel_id=1, source_target_pairs={{0,4},{4,0},{8,12},{12,8},{16,20},{20,16},{24,28},{28,24},{32,36},... | collective-permute-start | bytes 196616 | tf_op jit(solution)/shard_map/ppermute | solution.py:44
  32.6 13.7 %copy-start.1 = (bf16[32,128,128]{2,1,0:T(8,128)(2,1)S(1)}, bf16[32,128,128]{2,1,0:T(8,128)(2,1)}, u32[]{:S(2)}) copy-start(bf16[32,128,128]{2,1,0:T(8,128)(2,1)} %inverse.5) | copy-start | bytes 3145732
  32.6 13.7 %copy-start.3 = (f32[64]{0:T(128)S(1)}, f32[64]{0:T(128)}, u32[]{:S(2)}) copy-start(f32[64]{0:T(128)} %param.16) | copy-start | bytes 772
  32.6 13.7 %copy-start.4 = (f32[64]{0:T(128)S(1)}, f32[64]{0:T(128)}, u32[]{:S(2)}) copy-start(f32[64]{0:T(128)} %param.17) | copy-start | bytes 772
  38.2 5.4 %collective-permute-start.14 = (f32[32,128]{1,0:T(8,128)S(1)}, f32[32,128]{1,0:T(8,128)S(1)}, u32[]{:S(2)}, u32[]{:S(2)}) collective-permute-start(f32[32,128]{1,0:T(8,128)S(1)} %get-tuple-element.82.refs_2_), channel_id=1, source_target_pairs={{0,2},{1,3},{2,0},{3,1},{4,6},{5,7},{6,4},{7,5},{8,10},{9,11},{10,... | collective-permute-start | bytes 49160 | tf_op jit(solution)/shard_map/ppermute | solution.py:431
  41.4 4.9 %collective-permute-start.13 = (f32[32,128]{1,0:T(8,128)S(1)}, f32[32,128]{1,0:T(8,128)S(1)}, u32[]{:S(2)}, u32[]{:S(2)}) collective-permute-start(f32[32,128]{1,0:T(8,128)S(1)} %get-tuple-element.82.refs_2_), channel_id=1, source_target_pairs={{0,3},{1,2},{2,1},{3,0},{4,7},{5,6},{6,5},{7,4},{8,11},{9,10},{10,... | collective-permute-start | bytes 49160 | tf_op jit(solution)/shard_map/ppermute | solution.py:431
  42.5 3.8 %collective-permute-start.12 = (f32[32,128]{1,0:T(8,128)S(1)}, f32[32,128]{1,0:T(8,128)S(1)}, u32[]{:S(2)}, u32[]{:S(2)}) collective-permute-start(f32[32,128]{1,0:T(8,128)S(1)} %get-tuple-element.82.refs_2_), channel_id=1, source_target_pairs={{0,1},{1,0},{2,3},{3,2},{4,5},{5,4},{6,7},{7,6},{8,9},{9,8},{10,11... | collective-permute-start | bytes 49160 | tf_op jit(solution)/shard_map/ppermute | solution.py:431
  46.7 7.7 %collective-permute-start.15 = (bf16[4,64,128]{2,1,0:T(8,128)(2,1)S(1)}, bf16[4,64,128]{2,1,0:T(8,128)(2,1)S(1)}, u32[]{:S(2)}, u32[]{:S(2)}) collective-permute-start(bf16[4,64,128]{2,1,0:T(8,128)(2,1)S(1)} %get-tuple-element.85), channel_id=1, source_target_pairs={{0,120},{4,124},{8,16},{12,20},{16,8},{20,12},{24,32},{28,36},{32,... | collective-permute-start | bytes 196616 | tf_op jit(solution)/shard_map/ppermute | solution.py:44
  49.6 4.8 %collective-permute-start.16 = (bf16[4,64,128]{2,1,0:T(8,128)(2,1)S(1)}, bf16[4,64,128]{2,1,0:T(8,128)(2,1)S(1)}, u32[]{:S(2)}, u32[]{:S(2)}) collective-permute-start(bf16[4,64,128]{2,1,0:T(8,128)(2,1)S(1)} %get-tuple-element.86), channel_id=1, source_target_pairs={{0,8},{4,12},{8,0},{12,4},{16,24},{20,28},{24,16},{28,20},{32,40},... | collective-permute-start | bytes 196616 | tf_op jit(solution)/shard_map/ppermute | solution.py:44
  49.6 7.0 %collective-permute-start.17 = (bf16[4,64,128]{2,1,0:T(8,128)(2,1)S(1)}, bf16[4,64,128]{2,1,0:T(8,128)(2,1)S(1)}, u32[]{:S(2)}, u32[]{:S(2)}) collective-permute-start(bf16[4,64,128]{2,1,0:T(8,128)(2,1)S(1)} %get-tuple-element.87), channel_id=1, source_target_pairs={{0,124},{4,8},{8,4},{12,16},{16,12},{20,24},{24,20},{28,32},{32,28... | collective-permute-start | bytes 196616 | tf_op jit(solution)/shard_map/ppermute | solution.py:44
  49.6 7.0 %collective-permute-start.18 = (bf16[4,64,128]{2,1,0:T(8,128)(2,1)S(1)}, bf16[4,64,128]{2,1,0:T(8,128)(2,1)S(1)}, u32[]{:S(2)}, u32[]{:S(2)}) collective-permute-start(bf16[4,64,128]{2,1,0:T(8,128)(2,1)S(1)} %get-tuple-element.88), channel_id=1, source_target_pairs={{0,4},{4,0},{8,12},{12,8},{16,20},{20,16},{24,28},{28,24},{32,36},... | collective-permute-start | bytes 196616 | tf_op jit(solution)/shard_map/ppermute | solution.py:44
  57.6 8.3 %collective-permute-start.19 = (bf16[4,64,128]{2,1,0:T(8,128)(2,1)S(1)}, bf16[4,64,128]{2,1,0:T(8,128)(2,1)S(1)}, u32[]{:S(2)}, u32[]{:S(2)}) collective-permute-start(bf16[4,64,128]{2,1,0:T(8,128)(2,1)S(1)} %get-tuple-element.92), channel_id=1, source_target_pairs={{0,120},{4,124},{8,16},{12,20},{16,8},{20,12},{24,32},{28,36},{32,... | collective-permute-start | bytes 196616 | tf_op jit(solution)/shard_map/ppermute | solution.py:44
  58.3 7.7 %collective-permute-start.20 = (bf16[4,64,128]{2,1,0:T(8,128)(2,1)S(1)}, bf16[4,64,128]{2,1,0:T(8,128)(2,1)S(1)}, u32[]{:S(2)}, u32[]{:S(2)}) collective-permute-start(bf16[4,64,128]{2,1,0:T(8,128)(2,1)S(1)} %get-tuple-element.93), channel_id=1, source_target_pairs={{0,8},{4,12},{8,0},{12,4},{16,24},{20,28},{24,16},{28,20},{32,40},... | collective-permute-start | bytes 196616 | tf_op jit(solution)/shard_map/ppermute | solution.py:44
  58.3 7.7 %collective-permute-start.21 = (bf16[4,64,128]{2,1,0:T(8,128)(2,1)S(1)}, bf16[4,64,128]{2,1,0:T(8,128)(2,1)S(1)}, u32[]{:S(2)}, u32[]{:S(2)}) collective-permute-start(bf16[4,64,128]{2,1,0:T(8,128)(2,1)S(1)} %get-tuple-element.94), channel_id=1, source_target_pairs={{0,124},{4,8},{8,4},{12,16},{16,12},{20,24},{24,20},{28,32},{32,28... | collective-permute-start | bytes 196616 | tf_op jit(solution)/shard_map/ppermute | solution.py:44
  60.2 5.7 %collective-permute-start.22 = (bf16[4,64,128]{2,1,0:T(8,128)(2,1)S(1)}, bf16[4,64,128]{2,1,0:T(8,128)(2,1)S(1)}, u32[]{:S(2)}, u32[]{:S(2)}) collective-permute-start(bf16[4,64,128]{2,1,0:T(8,128)(2,1)S(1)} %get-tuple-element.95), channel_id=1, source_target_pairs={{0,4},{4,0},{8,12},{12,8},{16,20},{20,16},{24,28},{28,24},{32,36},... | collective-permute-start | bytes 196616 | tf_op jit(solution)/shard_map/ppermute | solution.py:44
  67.0 7.7 %collective-permute-start.23 = (bf16[4,64,128]{2,1,0:T(8,128)(2,1)S(1)}, bf16[4,64,128]{2,1,0:T(8,128)(2,1)S(1)}, u32[]{:S(2)}, u32[]{:S(2)}) collective-permute-start(bf16[4,64,128]{2,1,0:T(8,128)(2,1)S(1)} %get-tuple-element.99), channel_id=1, source_target_pairs={{0,120},{4,124},{8,16},{12,20},{16,8},{20,12},{24,32},{28,36},{32,... | collective-permute-start | bytes 196616 | tf_op jit(solution)/shard_map/ppermute | solution.py:44
  68.6 6.1 %collective-permute-start.24 = (bf16[4,64,128]{2,1,0:T(8,128)(2,1)S(1)}, bf16[4,64,128]{2,1,0:T(8,128)(2,1)S(1)}, u32[]{:S(2)}, u32[]{:S(2)}) collective-permute-start(bf16[4,64,128]{2,1,0:T(8,128)(2,1)S(1)} %get-tuple-element.100), channel_id=1, source_target_pairs={{0,8},{4,12},{8,0},{12,4},{16,24},{20,28},{24,16},{28,20},{32,40},... | collective-permute-start | bytes 196616 | tf_op jit(solution)/shard_map/ppermute | solution.py:44
  68.6 7.0 %collective-permute-start.25 = (bf16[4,64,128]{2,1,0:T(8,128)(2,1)S(1)}, bf16[4,64,128]{2,1,0:T(8,128)(2,1)S(1)}, u32[]{:S(2)}, u32[]{:S(2)}) collective-permute-start(bf16[4,64,128]{2,1,0:T(8,128)(2,1)S(1)} %get-tuple-element.101), channel_id=1, source_target_pairs={{0,124},{4,8},{8,4},{12,16},{16,12},{20,24},{24,20},{28,32},{32,28... | collective-permute-start | bytes 196616 | tf_op jit(solution)/shard_map/ppermute | solution.py:44
  70.4 5.2 %collective-permute-start.26 = (bf16[4,64,128]{2,1,0:T(8,128)(2,1)S(1)}, bf16[4,64,128]{2,1,0:T(8,128)(2,1)S(1)}, u32[]{:S(2)}, u32[]{:S(2)}) collective-permute-start(bf16[4,64,128]{2,1,0:T(8,128)(2,1)S(1)} %get-tuple-element.102), channel_id=1, source_target_pairs={{0,4},{4,0},{8,12},{12,8},{16,20},{20,16},{24,28},{28,24},{32,36},... | collective-permute-start | bytes 196616 | tf_op jit(solution)/shard_map/ppermute | solution.py:44
  78.2 5.3 %collective-permute-start.29 = (f32[32,128]{1,0:T(8,128)S(1)}, f32[32,128]{1,0:T(8,128)S(1)}, u32[]{:S(2)}, u32[]{:S(2)}) collective-permute-start(f32[32,128]{1,0:T(8,128)S(1)} %get-tuple-element.104.refs_1_), channel_id=1, source_target_pairs={{0,2},{1,3},{2,0},{3,1},{4,6},{5,7},{6,4},{7,5},{8,10},{9,11},{10,... | collective-permute-start | bytes 49160 | tf_op jit(solution)/shard_map/ppermute | solution.py:431
  79.7 4.9 %collective-permute-start.28 = (f32[32,128]{1,0:T(8,128)S(1)}, f32[32,128]{1,0:T(8,128)S(1)}, u32[]{:S(2)}, u32[]{:S(2)}) collective-permute-start(f32[32,128]{1,0:T(8,128)S(1)} %get-tuple-element.104.refs_1_), channel_id=1, source_target_pairs={{0,3},{1,2},{2,1},{3,0},{4,7},{5,6},{6,5},{7,4},{8,11},{9,10},{10,... | collective-permute-start | bytes 49160 | tf_op jit(solution)/shard_map/ppermute | solution.py:431
  80.8 3.8 %collective-permute-start.27 = (f32[32,128]{1,0:T(8,128)S(1)}, f32[32,128]{1,0:T(8,128)S(1)}, u32[]{:S(2)}, u32[]{:S(2)}) collective-permute-start(f32[32,128]{1,0:T(8,128)S(1)} %get-tuple-element.104.refs_1_), channel_id=1, source_target_pairs={{0,1},{1,0},{2,3},{3,2},{4,5},{5,4},{6,7},{7,6},{8,9},{9,8},{10,11... | collective-permute-start | bytes 49160 | tf_op jit(solution)/shard_map/ppermute | solution.py:431
